TPU v7x, 32 devices: a whole 2x2x4 slice. The times are simulated.
32 devices in a mesh: pool: 2 (over y), train: 16 (over z, x, core), cand: 1.
Axes of the slice: x: 2, y: 2, z: 4, core: 2. Of those that a mesh axis runs over, the one named last changes fastest.
Arguments:
- cand_desc: bfloat16 [4096, 768], P(('pool', 'cand', 'train')), parts along dimension 0, as said below
- struct_id: int32 [4096], P(('pool', 'cand', 'train')), parts along dimension 0, may hold values from 0 to 127, as said below
- train_desc: bfloat16 [24576, 768], P(('pool', 'train')), parts along dimension 0, as said below
- lanczos: bfloat16 [24576, 128], P(('pool', 'train')), parts along dimension 0, may hold values from -0.011962891 to 0.011962891
- mean_weight: bfloat16 [24576], P(('pool', 'train')), parts along dimension 0, may hold values from -0.29882812 to 0.29882812
Outputs:
- pred_mean: float32 [256], P(('pool', 'cand', 'train')), parts along dimension 0
- covariance: float32 [2, 128, 128], P(('pool', 'cand'), 'train'), parts along dimension 0
There are 2 independent parts, one for each index of `pool`. A program takes and returns all parts, laid end to end along the dimension named above; each array names one. Nothing has to cross between parts.
Inputs may be any that keep to these rules, and one draw needn't show every extreme that they name: `struct_id`: rows come in aligned blocks of 128; block b holds structures b * 8 to b * 8 + 7 in increasing order, each with at least one row. `cand_desc`: all entries are positive. `train_desc`: all entries are positive.
All inputs are finite; a program needn't handle non-finite values.
Results may differ from a plain program's by a relative error of at most 0.0015.
The roundings to bfloat16 on the way count: a program that leaves them out, or rounds other values in their place, can miss the bound.
Values may be sent and summed in bfloat16 or wider, within the bound.
No kernel may reach another device: no remote copies, remote signals or barrier semaphores. Data moves between devices by JAX's collectives and lax.ppermute only.
A program may use at most 64 MiB of HBM per device.

v0:
```python
import jax
import jax.numpy as jnp
from jax import lax
from jax.sharding import PartitionSpec as P

BLK = 128
SPB = 8


EPSILON = 1e-06


def unit_rows(values):
    wide = values.astype(jnp.float32)
    scale = lax.rsqrt(jnp.mean(wide * wide, axis=1, keepdims=True) + EPSILON)
    return (wide * scale).astype(jnp.bfloat16)


def kernel_block(left, right):
    products = lax.dot_general(
        left, right, (((1,), (1,)), ((), ())), preferred_element_type=jnp.float32
    )
    cosine = products / left.shape[1]
    square = cosine * cosine
    return square * square


def structure_weight(struct_ids, count):
    within = struct_ids - struct_ids[0]
    member = (jnp.arange(count, dtype=jnp.int32)[:, None] == within[None, :]).astype(jnp.float32)
    return member / jnp.sum(member, axis=1, keepdims=True)


def block_weight(struct_ids):
    grouped = struct_ids.reshape(struct_ids.shape[0] // BLK, BLK)
    within = grouped - grouped[:, 0:1]
    member = (jnp.arange(SPB, dtype=jnp.int32)[None, :, None] == within[:, None, :]).astype(
        jnp.float32
    )
    return member / jnp.sum(member, axis=2, keepdims=True)


def body(cand_desc, struct_id, train_desc, lanczos, mean_weight):
    high = lax.Precision.HIGHEST
    cand_unit = unit_rows(cand_desc)
    train_unit = unit_rows(train_desc)
    gathered, gathered_ids = (
        lax.all_gather(cand_unit, "train", axis=0, tiled=True),
        lax.all_gather(struct_id, "train", axis=0, tiled=True),
    )
    total_rows = gathered.shape[0]
    block_size = 512
    blocks = gathered.reshape(total_rows // block_size, block_size, gathered.shape[1])

    def project(members):
        kernel_rows = kernel_block(members, train_unit).astype(jnp.bfloat16)
        return (
            jnp.dot(kernel_rows, lanczos, preferred_element_type=jnp.float32),
            jnp.dot(kernel_rows, mean_weight, preferred_element_type=jnp.float32),
        )

    projection, mean_terms = lax.map(project, blocks)
    rank_width = lanczos.shape[1]
    projection = projection.reshape(total_rows, rank_width)
    mean_terms = mean_terms.reshape(total_rows)
    own_count = cand_desc.shape[0] // BLK * SPB
    group_count = total_rows // BLK
    batch_count = group_count * SPB
    own_weight = structure_weight(struct_id, own_count)
    grouped_weight = block_weight(gathered_ids)
    own_projection, own_terms = (
        lax.psum_scatter(projection, "train", scatter_dimension=0, tiled=True),
        lax.psum_scatter(mean_terms, "train", scatter_dimension=0, tiled=True),
    )
    own_q = jnp.dot(own_weight, own_projection, precision=high)
    own_mean = jnp.dot(own_weight, own_terms, precision=high)
    all_q = lax.all_gather(own_q, "train", axis=0, tiled=True)
    pairs = kernel_block(cand_unit, gathered)
    left_side = jnp.dot(own_weight, pairs, precision=high)
    prior = jnp.einsum(
        "anr,nsr->ans",
        left_side.reshape(own_count, group_count, BLK),
        grouped_weight,
        precision=high,
    ).reshape(own_count, batch_count)
    covariance = prior - jnp.dot(own_q, all_q.T, precision=high)
    return (own_mean, covariance[None])


def solution(mesh):
    placed = (
        P(("pool", "cand", "train"), None),
        P(("pool", "cand", "train")),
        P(("pool", "train"), None),
        P(("pool", "train"), None),
        P(("pool", "train")),
    )
    return jax.shard_map(
        body,
        mesh=mesh,
        in_specs=placed,
        out_specs=(P(("pool", "cand", "train")), P(("pool", "cand"), "train", None)),
        check_vma=False,
    )
```

profile of v0, /device:TPU:0, one launch (start us, length us, event | category | flops | bytes accessed | tf_op | source)
XLA Modules:
  0.0 156.9 jit_solution(10694136909668421953)
XLA Ops:
  7.2 1.1 fusion.9
  8.4 1.7 %fusion.10 = bf16[128,768]{1,0:T(8,128)(2,1)} fusion(bf16[128,768]{1,0:T(8,128)(2,1)} %param.7, f32[128]{0:T(128)S(1)} %add_rsqrt_fusion.1), kind=kLoop, calls=%fused_computation.21 | loop fusion | flops 294912 | bytes 393728 | tf_op jit(solution)/shard_map/convert_element_type | solution.py:16
  10.2 1.6 %fusion.6 = f32[768]{0:T(1024)S(1)} fusion(bf16[768,768]{1,0:T(8,128)(2,1)} %param.9), kind=kLoop, calls=%fused_computation.11 | loop fusion | flops 1768704 | bytes 1182720 | tf_op jit(solution)/shard_map/reduce_sum | solution.py:15
  12.1 46.1 %all-gather.3.cloned.1.call-done = bf16[2048,768]{1,0:T(8,128)(2,1)} async-done(((bf16[128,768]{1,0:T(8,128)(2,1)}), bf16[2048,768]{1,0:T(8,128)(2,1)}) %all-gather.3.cloned.1.call-update) | async-done | bytes 3145744 | tf_op jit(solution)/shard_map/all_gather | solution.py:48
  58.2 13.7 %while.12 = (s32[]{:T(128)}, f32[4,512,128]{2,1,0:T(8,128)}, f32[4,512]{1,0:T(4,128)S(1)}, bf16[4,512,768]{2,1,0:T(8,128)(2,1)}, bf16[768,768]{1,0:T(8,128)(2,1)...) while((s32[]{:T(128)}, f32[4,512,128]{2,1,0:T(8,128)}, ...), condition=%wide.region_4.5_spmd, body=%wide.region_3.4_spmd.sunk | while | flops 707002368 | bytes 4796001 | solution.py:62
  58.2 2.0 %multiply_convert_fusion.2 = bf16[512,768]{1,0:T(8,128)(2,1)S(1)} fusion(bf16[768,768]{1,0:T(8,128)(2,1)S(1)} %get-tuple-element.121, bf16[4,512,768]{2,1,0:T(8,128)(2,1)} %get-tuple-element.120, s32[]{:T(128)} %get-tuple-element.108), kind=kOutput, calls=%fused_computation.clone.1 | convolution fusion | flops 605552640 | bytes 2753024 | tf_op jit(solution)/shard_map/while/body/eval_jaxpr/dot_general | solution.py:20
  60.3 1.1 fusion.47
  61.8 1.9 %multiply_convert_fusion.2 = bf16[512,768]{1,0:T(8,128)(2,1)S(1)} fusion(bf16[768,768]{1,0:T(8,128)(2,1)S(1)} %get-tuple-element.121, bf16[4,512,768]{2,1,0:T(8,128)(2,1)} %get-tuple-element.120, s32[]{:T(128)} %get-tuple-element.108), kind=kOutput, calls=%fused_computation.clone.1 | convolution fusion | flops 605552640 | bytes 2753024 | tf_op jit(solution)/shard_map/while/body/eval_jaxpr/dot_general | solution.py:20
  63.7 1.1 fusion.47
  65.2 1.9 %multiply_convert_fusion.2 = bf16[512,768]{1,0:T(8,128)(2,1)S(1)} fusion(bf16[768,768]{1,0:T(8,128)(2,1)S(1)} %get-tuple-element.121, bf16[4,512,768]{2,1,0:T(8,128)(2,1)} %get-tuple-element.120, s32[]{:T(128)} %get-tuple-element.108), kind=kOutput, calls=%fused_computation.clone.1 | convolution fusion | flops 605552640 | bytes 2753024 | tf_op jit(solution)/shard_map/while/body/eval_jaxpr/dot_general | solution.py:20
  67.1 1.1 fusion.47
  68.6 1.9 %multiply_convert_fusion.2 = bf16[512,768]{1,0:T(8,128)(2,1)S(1)} fusion(bf16[768,768]{1,0:T(8,128)(2,1)S(1)} %get-tuple-element.121, bf16[4,512,768]{2,1,0:T(8,128)(2,1)} %get-tuple-element.120, s32[]{:T(128)} %get-tuple-element.108), kind=kOutput, calls=%fused_computation.clone.1 | convolution fusion | flops 605552640 | bytes 2753024 | tf_op jit(solution)/shard_map/while/body/eval_jaxpr/dot_general | solution.py:20
  70.5 1.1 fusion.47
  72.0 0.6 dynamic-slice
  73.3 19.1 %all-gather = s32[16,1,128]{2,1,0:T(1,128)S(1)} all-gather(s32[1,1,128]{2,1,0:T(1,128)S(1)} %bitcast.63), channel_id=1, replica_groups=mesh['pool'=2,'train'=16,'cand'=1] {'train'}, dimensions={0}, use_global_device_ids=true | all-gather | bytes 8704 | tf_op jit(solution)/shard_map/all_gather | solution.py:49
  92.8 3.0 %fusion.5 = f32[128,2048]{1,0:T(8,128)S(1)} fusion(bf16[128,768]{1,0:T(8,128)(2,1)S(1)} %copy-done.2, bf16[2048,768]{1,0:T(8,128)(2,1)} %bitcast.57), kind=kOutput, calls=%fused_computation.10 | convolution fusion | flops 403439616 | bytes 4390912 | tf_op jit(solution)/shard_map/dot_general | solution.py:20
  95.9 0.6 convolution_bitcast_fusion.2
  96.5 0.3 convolution_bitcast_fusion.1
  96.9 30.6 %all-reduce = f32[2048]{0:T(1024)S(1)} all-reduce(f32[2048]{0:T(1024)S(1)} %bitcast.61), channel_id=2, replica_groups=mesh['pool'=2,'train'=16,'cand'=1] {'train'}, use_global_device_ids=true, to_apply=%region_5.6.clone | all-reduce | flops 2048 | bytes 16384
  127.5 0.7 convolution_bitcast_fusion.3
  128.2 0.4 reduce-scatter.2.cloned.1.call-done
  128.6 1.0 fusion.13
  129.6 19.6 %all_gather.11 = f32[128,128]{1,0:T(8,128)S(1)} all-gather(f32[8,128]{1,0:T(8,128)S(1)} %fusion.13), channel_id=1, replica_groups=mesh['pool'=2,'train'=16,'cand'=1] {'train'}, dimensions={0}, use_global_device_ids=true | all-gather | bytes 69632 | tf_op jit(solution)/shard_map/all_gather | solution.py:77
  149.3 0.8 fusion.8
  (40 shorter events, 2.3 us)
Async XLA Ops:
  7.2 4.6 %copy-start.1 = (bf16[768,768]{1,0:T(8,128)(2,1)S(1)}, bf16[768,768]{1,0:T(8,128)(2,1)}, u32[]{:S(2)}) copy-start(bf16[768,768]{1,0:T(8,128)(2,1)} %param.9) | copy-start | bytes 3538948
  7.2 51.0 %all-gather.3.cloned.1.call-start = ((), (), s32[]{:S(2)}) async-start(), calls=%async_computation.1 | async-start | bytes 3342336 | tf_op jit(solution)/shard_map/all_gather | solution.py:48
  10.1 118.5 %reduce-scatter.2.cloned.1.call-start = ((), (), s32[]{:S(2)}) async-start(), calls=%async_computation.2 | async-start | bytes 1114112 | tf_op jit(solution)/shard_map/reduce_scatter | solution.py:72
  10.2 48.1 %copy-start = (bf16[768,128]{1,0:T(8,128)(2,1)S(1)}, bf16[768,128]{1,0:T(8,128)(2,1)}, u32[]{:S(2)}) copy-start(bf16[768,128]{1,0:T(8,128)(2,1)} %param.10) | copy-start | bytes 589828
  10.2 48.0 %copy-start.3 = (bf16[768]{0:T(1024)(128)(2,1)S(1)}, bf16[768]{0:T(1024)(128)(2,1)}, u32[]{:S(2)}) copy-start(bf16[768]{0:T(1024)(128)(2,1)} %param.11) | copy-start | bytes 4612
  58.2 13.8 %copy-start.5 = (u32[32]{0:T(128)S(1)}, u32[32]{0:T(128)}, u32[]{:S(2)}) copy-start(u32[32]{0:T(128)} %constant.32) | copy-start | bytes 388
  58.2 15.0 %copy-start.4 = (s32[128]{0:T(128)S(1)}, s32[128]{0:T(128)}, u32[]{:S(2)}) copy-start(s32[128]{0:T(128)} %param.8) | copy-start | bytes 1540
  58.2 34.6 %copy-start.2 = (bf16[128,768]{1,0:T(8,128)(2,1)S(1)}, bf16[128,768]{1,0:T(8,128)(2,1)}, u32[]{:S(2)}) copy-start(bf16[128,768]{1,0:T(8,128)(2,1)} %fusion.10) | copy-start | bytes 589828
Sparse Core Ops, SparseCore 0:
  10.3 47.8 all-gather.2
  72.1 56.4 reduce-scatter.1
where the time goes:
time: 157 us
  blocking collectives  69.3 us (44%)
  waiting for transfers between devices  46.6 us (30%)
  matrix products  20 us (13%)
  between operations  14.8 us (9%)
  other arithmetic  5.04 us (3%)
    all_gather x1, waiting for transfers between devices, body(): lax.all_gather(cand_unit, 'train', axis=0, tiled=True)  46.1 us
    unnamed x1, blocking collectives  30.6 us
    all_gather x1, blocking collectives, body(): all_q = lax.all_gather(own_q, 'train', axis=0, tiled=True)  19.6 us
    all_gather x1, blocking collectives, body(): lax.all_gather(struct_id, 'train', axis=0, tiled=True)  19.1 us
    dot_general x5, matrix products, kernel_block(): lax.dot_general(left, right, (((1,), (1,)), ((), ())), preferred_element_...  10.9 us
    dot_general x4, matrix products, project(): jnp.dot(kernel_rows, lanczos, preferred_element_type=jnp.float32)  4.36 us
  transfers between devices with their start and end apart: 2, of which 2 were waited for; matrix products, arithmetic and copies ran while one was open for 5% of the time, Pallas kernels for 0%

commit v1 on v0

v1 whole, which is shorter than its diff:
```python
import functools

import jax
import jax.numpy as jnp
from jax import lax
from jax.experimental import pallas as pl
from jax.experimental.pallas import tpu as pltpu
from jax.sharding import PartitionSpec as P

SPB = 8
EPSILON = 1e-06
HIGH = lax.Precision.HIGHEST
LANES = 128
VMEM = pl.BlockSpec(memory_space=pltpu.VMEM)


def unit_rows(values):
    wide = values.astype(jnp.float32)
    scale = lax.rsqrt(jnp.mean(wide * wide, axis=1, keepdims=True) + EPSILON)
    return (wide * scale).astype(jnp.bfloat16)


def contract_lanes(left, right, precision=None):
    return lax.dot_general(
        left,
        right,
        (((1,), (1,)), ((), ())),
        preferred_element_type=jnp.float32,
        precision=precision,
    )


def pack_cand(cand_ref, ids_ref, out_ref):
    rows, width = cand_ref.shape
    unit = unit_rows(cand_ref[...])
    for chunk in range(width // LANES):
        out_ref[chunk * rows : (chunk + 1) * rows, :] = unit[
            :, chunk * LANES : (chunk + 1) * LANES
        ]
    within = (ids_ref[...] - ids_ref[0, 0]).astype(jnp.float32)
    out_ref[width // LANES * rows :, :] = jnp.broadcast_to(within, (16, rows)).astype(
        jnp.bfloat16
    )


def pack_train(train_ref, lanczos_ref, weight_ref, out_ref):
    rows, width = train_ref.shape
    rank = lanczos_ref.shape[1]
    step = 128

    def one(start):
        part = pl.ds(pl.multiple_of(start * step, step), step)
        out_ref[part, :] = unit_rows(train_ref[part, :])

    pl.loop(0, rows // step)(one)
    out_ref[rows : rows + rank, :] = (
        lanczos_ref[...].astype(jnp.float32).T.astype(jnp.bfloat16)
    )
    out_ref[rows + rank :, :] = jnp.broadcast_to(
        weight_ref[...].astype(jnp.float32), (16, width)
    ).astype(jnp.bfloat16)


def unpack(ref, rows, chunks):
    return jnp.concatenate(
        [ref[c * rows : (c + 1) * rows, :] for c in range(chunks)], axis=1
    )


def quartic(products, width):
    cosine = products * (1.0 / width)
    square = cosine * cosine
    return square * square


def member_of(ids, base, count):
    row = lax.broadcasted_iota(jnp.int32, (count, ids.shape[1]), 0)
    return (row == ids.astype(jnp.int32) + base).astype(jnp.float32)


def group_kernel(
    masks, chips, rows, width, rank, first, own_ref, sib_ref, one_ref, two_ref,
    town_ref, tsib_ref, *rest
):
    if first:
        q_out, prior_out = rest
    else:
        q_in, prior_in, q_out, prior_out = rest
    chunks = width // LANES
    me = lax.axis_index("train")
    chip, core = me // 2, me % 2
    blocks = jnp.concatenate(
        [unpack(one_ref, rows, chunks), unpack(two_ref, rows, chunks)], axis=0
    )
    id_rows = [
        ref[chunks * rows : chunks * rows + 1, :].astype(jnp.float32)
        for ref in (one_ref, two_ref)
    ]
    owners = [lax.bitwise_xor(chip, mask) for mask in masks]
    structs = chips * SPB
    member = jnp.concatenate(
        [member_of(i, o * SPB, structs) for i, o in zip(id_rows, owners)], axis=1
    )
    scale = 1.0 / jnp.maximum(jnp.sum(member, axis=1, keepdims=True), 1.0)
    proj = None
    for ref in (town_ref, tsib_ref):
        train_rows = ref.shape[0] - rank - 16
        kernel_rows = quartic(
            contract_lanes(ref[:train_rows, :], blocks), width
        ).astype(jnp.bfloat16)
        term = jnp.dot(
            ref[train_rows:, :], kernel_rows, preferred_element_type=jnp.float32
        )
        proj = term if proj is None else proj + term
    q = contract_lanes(member, proj[:rank], HIGH) * scale
    means = contract_lanes(proj[rank : rank + 8], member * scale, HIGH)
    if structs < LANES:
        means = jnp.concatenate(
            [means, jnp.zeros((8, LANES - structs), jnp.float32)], axis=1
        )
    q_all = jnp.concatenate([q, means], axis=0)

    chip_rows = jnp.concatenate(
        [unpack(own_ref, rows, chunks), unpack(sib_ref, rows, chunks)], axis=0
    )
    pairs = quartic(contract_lanes(chip_rows, blocks), width)
    none = jnp.zeros((SPB, rows), jnp.float32)
    own_id, sib_id = [
        ref[chunks * rows : chunks * rows + 1, :].astype(jnp.float32)
        for ref in (own_ref, sib_ref)
    ]
    left = jnp.concatenate(
        [
            jnp.concatenate([member_of(own_id, 0, SPB), none], axis=1),
            jnp.concatenate([none, member_of(sib_id, 0, SPB)], axis=1),
        ],
        axis=0,
    )
    left = left / jnp.sum(left, axis=1, keepdims=True)
    wide = jnp.concatenate(
        [
            member_of(i, (o * 2 + core) * SPB, 2 * structs)
            for i, o in zip(id_rows, owners)
        ],
        axis=1,
    )
    wide = wide / jnp.maximum(jnp.sum(wide, axis=1, keepdims=True), 1.0)
    half = jnp.dot(left, pairs, preferred_element_type=jnp.float32, precision=HIGH)
    prior = contract_lanes(half, wide, HIGH)
    if first:
        q_out[...] = q_all
        prior_out[...] = prior
    else:
        q_out[...] = q_in[...] + q_all
        prior_out[...] = prior_in[...] + prior


def finish(q_ref, other_ref, mine_ref, theirs_ref, mean_ref, cov_ref, all_ref):
    structs = q_ref.shape[0] - 8
    me = lax.axis_index("train")
    chip, core = me // 2, me % 2
    for p in range(structs // SPB):
        rows = slice(p * SPB, (p + 1) * SPB)
        here = pl.multiple_of((2 * p + core) * SPB, SPB)
        there = pl.multiple_of((2 * p + 1 - core) * SPB, SPB)
        all_ref[pl.ds(here, SPB), :] = q_ref[rows, :]
        all_ref[pl.ds(there, SPB), :] = other_ref[rows, :]
    own = q_ref[pl.ds(pl.multiple_of(chip * SPB, SPB), SPB), :]
    cov_ref[...] = mine_ref[...] + theirs_ref[...] - contract_lanes(own, all_ref[...], HIGH)
    lane = lax.broadcasted_iota(jnp.int32, (SPB, LANES), 1)
    row = lax.broadcasted_iota(jnp.int32, (SPB, LANES), 0)
    means = jnp.broadcast_to(q_ref[structs : structs + 1, :], (SPB, LANES))
    column = jnp.sum(jnp.where(lane == chip * SPB + row, means, 0.0), axis=1, keepdims=True)
    mean_ref[...] = jnp.sum(jnp.where(lane == row, column, 0.0), axis=0, keepdims=True)


def call(kernel, shapes, count, flops=0, transfers=0, scratch=()):
    many = isinstance(shapes, (tuple, list))
    return pl.pallas_call(
        kernel,
        out_shape=shapes,
        in_specs=[VMEM] * count,
        out_specs=[VMEM] * len(shapes) if many else VMEM,
        scratch_shapes=scratch,
        cost_estimate=pl.CostEstimate(
            flops=flops, bytes_accessed=transfers, transcendentals=0
        ),
        compiler_params=pltpu.CompilerParams(vmem_limit_bytes=24 * 2**20),
    )


def body(size, cand_desc, struct_id, train_desc, lanczos, mean_weight):
    rows, width = cand_desc.shape
    train_rows, rank = lanczos.shape
    chips = size // 2
    structs = chips * SPB

    def swap(value, mask):
        return lax.ppermute(value, "train", [(i, i ^ mask) for i in range(size)])

    own = call(
        pack_cand,
        jax.ShapeDtypeStruct((rows * width // LANES + 16, LANES), jnp.bfloat16),
        2,
    )(cand_desc, struct_id.reshape(1, rows))
    blocks = {0: own}
    if size == 16:
        for mask in (6, 4, 2, 1):
            blocks[mask] = swap(own, 2 * mask)
        for mask in (2, 4, 6):
            blocks[mask + 1] = swap(blocks[mask], 2)
        groups = [(0, 1), (2, 3), (4, 5), (6, 7)]
    else:
        for mask in range(1, chips):
            blocks[mask] = swap(own, 2 * mask)
        groups = [(m, m + 1) for m in range(0, chips, 2)]
    sib = swap(own, 1)
    train_own = call(
        pack_train,
        jax.ShapeDtypeStruct((train_rows + rank + 16, width), jnp.bfloat16),
        3,
    )(train_desc, lanczos, mean_weight.reshape(1, train_rows))
    train_sib = swap(train_own, 1)

    q_shape = jax.ShapeDtypeStruct((structs + 8, LANES), jnp.float32)
    prior_shape = jax.ShapeDtypeStruct((2 * SPB, 2 * structs), jnp.float32)
    state = ()
    for masks in groups:
        kernel = functools.partial(
            group_kernel, masks, chips, rows, width, rank, not state
        )
        state = call(
            kernel,
            (q_shape, prior_shape),
            6 + len(state),
            flops=2 * 2 * rows * 2 * train_rows * (width + 2 * rank),
        )(own, sib, blocks[masks[0]], blocks[masks[1]], train_own, train_sib, *state)
    q, prior = state
    theirs = swap(prior[SPB:], 1)
    mask = 2
    while mask < size:
        q = q + swap(q, mask)
        mask *= 2
    other = swap(q, 1)
    mean, covariance = call(
        finish,
        (
            jax.ShapeDtypeStruct((1, LANES), jnp.float32),
            jax.ShapeDtypeStruct((SPB, 2 * structs), jnp.float32),
        ),
        4,
        scratch=[pltpu.VMEM((2 * structs, LANES), jnp.float32)],
    )(q, other, prior[:SPB], theirs)
    return mean[0, :SPB], covariance[None]


def solution(mesh):
    placed = (
        P(("pool", "cand", "train"), None),
        P(("pool", "cand", "train")),
        P(("pool", "train"), None),
        P(("pool", "train"), None),
        P(("pool", "train")),
    )
    return jax.shard_map(
        functools.partial(body, mesh.shape["train"]),
        mesh=mesh,
        in_specs=placed,
        out_specs=(P(("pool", "cand", "train")), P(("pool", "cand"), "train", None)),
        check_vma=False,
    )
```

time: 157 us -> 52.4 us (0.33)
  blocking collectives: 69.3 us -> 0 us
  waiting for transfers between devices: 46.6 us -> 18.6 us
  matrix products: 20 us -> 0 us
  starting transfers between devices: 0.08 us -> 19.9 us
  between operations: 14.8 us -> 0.7 us
  Pallas kernels: 0 us -> 9.58 us
  other arithmetic: 5.04 us -> 0.02 us
  local copies, waits for them, and re-layouts: 0.99 us -> 3.41 us
    all_gather x1 -> x0, waiting for transfers between devices: 46.1 us -> none  [body(): lax.all_gather(cand_unit, 'train', axis=0, tiled=True)]
    all_gather x2 -> x0, blocking collectives: 38.7 us -> none  [the longest x1 19.6 us: body(): all_q = lax.all_gather(own_q, 'train', axis=0, tiled=True)]
    unnamed x1 -> x0, blocking collectives: 30.6 us -> none
    dot_general x18 -> x0, matrix products: 20 us -> none  [the longest x5 10.9 us: kernel_block(): lax.dot_general(left, right, (((1,), (1,)), ((), ())), preferred_element_...]
    ppermute x0 -> x14, starting transfers between devices: none -> 19.9 us  [swap(): return lax.ppermute(value, 'train', [(i, i ^ mask) for i in range(size)])]
    ppermute x0 -> x14, waiting for transfers between devices: none -> 18.6 us  [swap(): return lax.ppermute(value, 'train', [(i, i ^ mask) for i in range(size)])]
    pallas_call x0 -> x7, Pallas kernels: none -> 9.58 us  [the longest x4 7.73 us: body(): call(kernel, (q_shape, prior_shape), 6 + len(state), flops=2 * 2 * rows *...]
    reduce_sum x4 -> x0, other arithmetic: 2.95 us -> none  [the longest x2 2.74 us: unit_rows(): scale = lax.rsqrt(jnp.mean(wide * wide, axis=1, keepdims=True) + EPSILON)]
  transfers between devices with their start and end apart: 2 -> 14, of which waited for: 2 -> 6; matrix products, arithmetic and copies ran while one was open for 5% -> 0% of each run, Pallas kernels for 0% -> 11%
where the time goes in v1:
time: 52.4 us; the launch traced here: 52.2 us
  starting transfers between devices  19.9 us (38%)
  waiting for transfers between devices  18.6 us (35%)
  Pallas kernels  9.58 us (18%)
  local copies, waits for them, and re-layouts  3.41 us (7%)
  between operations  0.7 us (1%)
    ppermute x14, starting transfers between devices, swap(): return lax.ppermute(value, 'train', [(i, i ^ mask) for i in range(size)])  19.9 us
    ppermute x14, waiting for transfers between devices, swap(): return lax.ppermute(value, 'train', [(i, i ^ mask) for i in range(size)])  18.6 us
    pallas_call x4, Pallas kernels, body(): call(kernel, (q_shape, prior_shape), 6 + len(state), flops=2 * 2 * rows *...  7.73 us
    unnamed x8, local copies, waits for them, and re-layouts  2.2 us
  transfers between devices with their start and end apart: 14, of which 6 were waited for; matrix products, arithmetic and copies ran while one was open for 0% of the time, Pallas kernels for 11%

profile of v1, /device:TPU:0, one launch (start us, length us, event | category | flops | bytes accessed | tf_op | source)
XLA Modules:
  0.0 52.2 jit_solution(14130421675059855612)
XLA Ops:
  0.6 0.7 %reshape.11.weight_ref = bf16[1,768]{1,0:T(2,128)(2,1)S(1)} reshape(bf16[768]{0:T(1024)(128)(2,1)} %param.9) | data formatting | bytes 3072 | tf_op jit(solution)/shard_map/reshape | solution.py:222
  1.3 1.3 %copy-done = bf16[768,768]{1,0:T(8,128)(2,1)S(1)} copy-done((bf16[768,768]{1,0:T(8,128)(2,1)S(1)}, bf16[768,768]{1,0:T(8,128)(2,1)}, u32[]{:S(2)}) %copy-start) | copy-done | bytes 1179672
  2.6 0.9 %copy-done.1 = bf16[768,128]{1,0:T(8,128)(2,1)S(1)} copy-done((bf16[768,128]{1,0:T(8,128)(2,1)S(1)}, bf16[768,128]{1,0:T(8,128)(2,1)}, u32[]{:S(2)}) %copy-start.1) | copy-done | bytes 196632
  3.5 0.9 %shard_map.69.town_ref = bf16[912,768]{1,0:T(8,128)(2,1)S(1)} custom-call(bf16[768,768]{1,0:T(8,128)(2,1)S(1)} %copy-done, bf16[768,128]{1,0:T(8,128)(2,1)S(1)} %copy-done.1, bf16[1,768]{1,0:T(2,128)(2,1)S(1)} %reshape.11.weight_ref), custom_call_target="tpu_custom_call" | custom-call | tf_op jit(solution)/shard_map/pallas_call | solution.py:218
  5.2 3.0 %collective-permute-start.6 = (bf16[784,128]{1,0:T(8,128)(2,1)S(1)}, bf16[784,128]{1,0:T(8,128)(2,1)S(1)}, u32[]{:S(2)}, u32[]{:S(2)}) collective-permute-start(bf16[784,128]{1,0:T(8,128)(2,1)S(1)} %shard_map.68.own_ref.one_ref), channel_id=1, source_target_pairs={{0,4},{1,5},{2,6},{3,7},{4,0},{5,1},{6,2},{7,3},{8,12},{9,13},{10,... | collective-permute-start | bytes 602120 | tf_op jit(solution)/shard_map/ppermute | solution.py:199
  8.2 2.6 %collective-permute-start.4 = (bf16[784,128]{1,0:T(8,128)(2,1)S(1)}, bf16[784,128]{1,0:T(8,128)(2,1)S(1)}, u32[]{:S(2)}, u32[]{:S(2)}) collective-permute-start(bf16[784,128]{1,0:T(8,128)(2,1)S(1)} %shard_map.68.own_ref.one_ref), channel_id=1, source_target_pairs={{0,8},{1,9},{2,10},{3,11},{4,12},{5,13},{6,14},{7,15},{8,0},{9,1},... | collective-permute-start | bytes 602120 | tf_op jit(solution)/shard_map/ppermute | solution.py:199
  10.8 1.7 %collective-permute-start.8 = (bf16[784,128]{1,0:T(8,128)(2,1)S(1)}, bf16[784,128]{1,0:T(8,128)(2,1)S(1)}, u32[]{:S(2)}, u32[]{:S(2)}) collective-permute-start(bf16[784,128]{1,0:T(8,128)(2,1)S(1)} %shard_map.68.own_ref.one_ref), channel_id=1, source_target_pairs={{0,2},{1,3},{2,0},{3,1},{4,6},{5,7},{6,4},{7,5},{8,10},{9,11},{10,... | collective-permute-start | bytes 602120 | tf_op jit(solution)/shard_map/ppermute | solution.py:199
  12.5 4.6 %collective-permute-done.6.one_ref = bf16[784,128]{1,0:T(8,128)(2,1)S(1)} collective-permute-done((bf16[784,128]{1,0:T(8,128)(2,1)S(1)}, bf16[784,128]{1,0:T(8,128)(2,1)S(1)}, u32[]{:S(2)}, u32[]{:S(2)}) %collective-permute-start.6) | collective-permute-done | bytes 200736 | tf_op jit(solution)/shard_map/ppermute | solution.py:199
  17.1 1.7 %collective-permute-start.7 = (bf16[784,128]{1,0:T(8,128)(2,1)S(1)}, bf16[784,128]{1,0:T(8,128)(2,1)S(1)}, u32[]{:S(2)}, u32[]{:S(2)}) collective-permute-start(bf16[784,128]{1,0:T(8,128)(2,1)S(1)} %collective-permute-done.6.one_ref), channel_id=1, source_target_pairs={{0,2},{1,3},{2,0},{3,1},{4,6},{5,7},{6,4},{7,5},{8,10},{9,11},{10,... | collective-permute-start | bytes 602120 | tf_op jit(solution)/shard_map/ppermute | solution.py:199
  18.8 6.8 %collective-permute-done.4.one_ref = bf16[784,128]{1,0:T(8,128)(2,1)S(1)} collective-permute-done((bf16[784,128]{1,0:T(8,128)(2,1)S(1)}, bf16[784,128]{1,0:T(8,128)(2,1)S(1)}, u32[]{:S(2)}, u32[]{:S(2)}) %collective-permute-start.4) | collective-permute-done | bytes 200736 | tf_op jit(solution)/shard_map/ppermute | solution.py:199
  25.6 1.5 %collective-permute-start.5 = (bf16[784,128]{1,0:T(8,128)(2,1)S(1)}, bf16[784,128]{1,0:T(8,128)(2,1)S(1)}, u32[]{:S(2)}, u32[]{:S(2)}) collective-permute-start(bf16[784,128]{1,0:T(8,128)(2,1)S(1)} %collective-permute-done.4.one_ref), channel_id=1, source_target_pairs={{0,2},{1,3},{2,0},{3,1},{4,6},{5,7},{6,4},{7,5},{8,10},{9,11},{10,... | collective-permute-start | bytes 602120 | tf_op jit(solution)/shard_map/ppermute | solution.py:199
  27.1 0.5 %collective-permute-start.2 = (bf16[784,128]{1,0:T(8,128)(2,1)S(1)}, bf16[784,128]{1,0:T(8,128)(2,1)S(1)}, u32[]{:S(2)}, u32[]{:S(2)}) collective-permute-start(bf16[784,128]{1,0:T(8,128)(2,1)S(1)} %collective-permute-done.1.one_ref), channel_id=1, source_target_pairs={{0,2},{1,3},{2,0},{3,1},{4,6},{5,7},{6,4},{7,5},{8,10},{9,11},{10,... | collective-permute-start | bytes 602120 | tf_op jit(solution)/shard_map/ppermute | solution.py:199
  27.7 2.0 %shard_map.70 = (f32[72,128]{1,0:T(8,128)S(1)}, f32[16,128]{1,0:T(8,128)S(1)}) custom-call(bf16[784,128]{1,0:T(8,128)(2,1)S(1)} %shard_map.68.own_ref.one_ref, bf16[784,128]{1,0:T(8,128)(2,1)S(1)} %collective-permute-done.sib_ref, bf16[784,128]{1,0:T(8,128)(2,1)S(1)} %shard_map.68.own_ref.one_ref, bf16[784,128]{1,0:T(8,128)(2,1)S(1)} %collective-permute-done.8.two_ref, ...), custom_call_target="tpu_custom_call" | custom-call | flops 805306368 | tf_op jit(solution)/shard_map/pallas_call | solution.py:232
  29.7 1.9 %shard_map.71 = (f32[72,128]{1,0:T(8,128)S(1)}, f32[16,128]{1,0:T(8,128)S(1)}) custom-call(bf16[784,128]{1,0:T(8,128)(2,1)S(1)} %shard_map.68.own_ref.one_ref, bf16[784,128]{1,0:T(8,128)(2,1)S(1)} %collective-permute-done.sib_ref, bf16[784,128]{1,0:T(8,128)(2,1)S(1)} %collective-permute-done.6.one_ref, bf16[784,128]{1,0:T(8,128)(2,1)S(1)} %collective-permute-done.7.two_ref, ...), custom_call_target="tpu_custom_call" | custom-call | flops 805306368 | tf_op jit(solution)/shard_map/pallas_call | solution.py:232
  31.6 1.9 %shard_map.72 = (f32[72,128]{1,0:T(8,128)S(1)}, f32[16,128]{1,0:T(8,128)S(1)}) custom-call(bf16[784,128]{1,0:T(8,128)(2,1)S(1)} %shard_map.68.own_ref.one_ref, bf16[784,128]{1,0:T(8,128)(2,1)S(1)} %collective-permute-done.sib_ref, bf16[784,128]{1,0:T(8,128)(2,1)S(1)} %collective-permute-done.4.one_ref, bf16[784,128]{1,0:T(8,128)(2,1)S(1)} %collective-permute-done.5.two_ref, ...), custom_call_target="tpu_custom_call" | custom-call | flops 805306368 | tf_op jit(solution)/shard_map/pallas_call | solution.py:232
  33.5 1.9 %shard_map.73 = (f32[72,128]{1,0:T(8,128)S(1)}, f32[16,128]{1,0:T(8,128)S(1)}) custom-call(bf16[784,128]{1,0:T(8,128)(2,1)S(1)} %shard_map.68.own_ref.one_ref, bf16[784,128]{1,0:T(8,128)(2,1)S(1)} %collective-permute-done.sib_ref, bf16[784,128]{1,0:T(8,128)(2,1)S(1)} %collective-permute-done.1.one_ref, bf16[784,128]{1,0:T(8,128)(2,1)S(1)} %collective-permute-done.2.two_ref, ...), custom_call_target="tpu_custom_call" | custom-call | flops 805306368 | tf_op jit(solution)/shard_map/pallas_call | solution.py:232
  35.4 1.5 %collective-permute-start.9 = (f32[72,128]{1,0:T(8,128)S(1)}, f32[72,128]{1,0:T(8,128)S(1)}, u32[]{:S(2)}, u32[]{:S(2)}) collective-permute-start(f32[72,128]{1,0:T(8,128)S(1)} %get-tuple-element.18), channel_id=1, source_target_pairs={{0,2},{1,3},{2,0},{3,1},{4,6},{5,7},{6,4},{7,5},{8,10},{9,11},{10,... | collective-permute-start | bytes 110600 | tf_op jit(solution)/shard_map/ppermute | solution.py:199
  37.0 2.5 %collective-permute-done.9 = f32[72,128]{1,0:T(8,128)S(1)} collective-permute-done((f32[72,128]{1,0:T(8,128)S(1)}, f32[72,128]{1,0:T(8,128)S(1)}, u32[]{:S(2)}, u32[]{:S(2)}) %collective-permute-start.9) | collective-permute-done | bytes 36896 | tf_op jit(solution)/shard_map/ppermute | solution.py:199
  39.4 3.2 %collective-permute-start.10 = (f32[72,128]{1,0:T(8,128)S(1)}, f32[72,128]{1,0:T(8,128)S(1)}, u32[]{:S(2)}, u32[]{:S(2)}) collective-permute-start(f32[72,128]{1,0:T(8,128)S(1)} %add.9), channel_id=1, source_target_pairs={{0,4},{1,5},{2,6},{3,7},{4,0},{5,1},{6,2},{7,3},{8,12},{9,13},{10,... | collective-permute-start | bytes 110600 | tf_op jit(solution)/shard_map/ppermute | solution.py:199
  42.6 1.9 %collective-permute-done.10 = f32[72,128]{1,0:T(8,128)S(1)} collective-permute-done((f32[72,128]{1,0:T(8,128)S(1)}, f32[72,128]{1,0:T(8,128)S(1)}, u32[]{:S(2)}, u32[]{:S(2)}) %collective-permute-start.10) | collective-permute-done | bytes 36896 | tf_op jit(solution)/shard_map/ppermute | solution.py:199
  44.6 3.0 %collective-permute-start.11 = (f32[72,128]{1,0:T(8,128)S(1)}, f32[72,128]{1,0:T(8,128)S(1)}, u32[]{:S(2)}, u32[]{:S(2)}) collective-permute-start(f32[72,128]{1,0:T(8,128)S(1)} %add.10), channel_id=1, source_target_pairs={{0,8},{1,9},{2,10},{3,11},{4,12},{5,13},{6,14},{7,15},{8,0},{9,1},... | collective-permute-start | bytes 110600 | tf_op jit(solution)/shard_map/ppermute | solution.py:199
  47.6 1.9 %collective-permute-done.11 = f32[72,128]{1,0:T(8,128)S(1)} collective-permute-done((f32[72,128]{1,0:T(8,128)S(1)}, f32[72,128]{1,0:T(8,128)S(1)}, u32[]{:S(2)}, u32[]{:S(2)}) %collective-permute-start.11) | collective-permute-done | bytes 36896 | tf_op jit(solution)/shard_map/ppermute | solution.py:199
  50.1 0.8 %collective-permute-done.13.theirs_ref = f32[8,128]{1,0:T(8,128)S(1)} collective-permute-done((f32[8,128]{1,0:T(8,128)S(1)}, f32[8,128]{1,0:T(8,128)S(1)}, u32[]{:S(2)}, u32[]{:S(2)}) %collective-permute-start.13) | collective-permute-done | bytes 4128 | tf_op jit(solution)/shard_map/ppermute | solution.py:199
  50.9 0.8 %shard_map.74 = (f32[1,128]{1,0:T(1,128)S(1)}, f32[8,128]{1,0:T(8,128)}) custom-call(f32[72,128]{1,0:T(8,128)S(1)} %add.11.q_ref, f32[72,128]{1,0:T(8,128)S(1)} %collective-permute-done.12.other_ref, f32[8,128]{1,0:T(8,128)S(1)} %get-tuple-element.23.mine_ref, f32[8,128]{1,0:T(8,128)S(1)} %collective-permute-done.13.theirs_ref), custom_call_target="tpu_custom_call" | custom-call | tf_op jit(solution)/shard_map/pallas_call | solution.py:245
  (25 shorter events, 1.8 us)
Async XLA Ops:
  0.6 4.3 %copy-start.3 = (s32[128]{0:T(128)S(1)}, s32[128]{0:T(128)}, u32[]{:S(2)}) copy-start(s32[128]{0:T(128)} %param.6) | copy-start | bytes 1540
  1.3 1.3 %copy-start = (bf16[768,768]{1,0:T(8,128)(2,1)S(1)}, bf16[768,768]{1,0:T(8,128)(2,1)}, u32[]{:S(2)}) copy-start(bf16[768,768]{1,0:T(8,128)(2,1)} %train_ref.1) | copy-start | bytes 3538948
  2.6 0.9 %copy-start.1 = (bf16[768,128]{1,0:T(8,128)(2,1)S(1)}, bf16[768,128]{1,0:T(8,128)(2,1)}, u32[]{:S(2)}) copy-start(bf16[768,128]{1,0:T(8,128)(2,1)} %lanczos_ref.1) | copy-start | bytes 589828
  3.5 1.4 %copy-start.2 = (bf16[128,768]{1,0:T(8,128)(2,1)S(1)}, bf16[128,768]{1,0:T(8,128)(2,1)}, u32[]{:S(2)}) copy-start(bf16[128,768]{1,0:T(8,128)(2,1)} %cand_ref.1) | copy-start | bytes 589828
  4.4 23.2 %collective-permute-start.3 = (bf16[912,768]{1,0:T(8,128)(2,1)S(1)}, bf16[912,768]{1,0:T(8,128)(2,1)S(1)}, u32[]{:S(2)}, u32[]{:S(2)}) collective-permute-start(bf16[912,768]{1,0:T(8,128)(2,1)S(1)} %shard_map.69.town_ref), channel_id=1, source_target_pairs={{0,1},{1,0},{2,3},{3,2},{4,5},{5,4},{6,7},{7,6},{8,9},{9,8},{10,11... | collective-permute-start | bytes 4202504 | tf_op jit(solution)/shard_map/ppermute | solution.py:199
  5.1 5.7 %collective-permute-start = (bf16[784,128]{1,0:T(8,128)(2,1)S(1)}, bf16[784,128]{1,0:T(8,128)(2,1)S(1)}, u32[]{:S(2)}, u32[]{:S(2)}) collective-permute-start(bf16[784,128]{1,0:T(8,128)(2,1)S(1)} %shard_map.68.own_ref.one_ref), channel_id=1, source_target_pairs={{0,1},{1,0},{2,3},{3,2},{4,5},{5,4},{6,7},{7,6},{8,9},{9,8},{10,11... | collective-permute-start | bytes 602120 | tf_op jit(solution)/shard_map/ppermute | solution.py:199
  5.2 11.9 %collective-permute-start.6 = (bf16[784,128]{1,0:T(8,128)(2,1)S(1)}, bf16[784,128]{1,0:T(8,128)(2,1)S(1)}, u32[]{:S(2)}, u32[]{:S(2)}) collective-permute-start(bf16[784,128]{1,0:T(8,128)(2,1)S(1)} %shard_map.68.own_ref.one_ref), channel_id=1, source_target_pairs={{0,4},{1,5},{2,6},{3,7},{4,0},{5,1},{6,2},{7,3},{8,12},{9,13},{10,... | collective-permute-start | bytes 602120 | tf_op jit(solution)/shard_map/ppermute | solution.py:199
  8.2 17.4 %collective-permute-start.4 = (bf16[784,128]{1,0:T(8,128)(2,1)S(1)}, bf16[784,128]{1,0:T(8,128)(2,1)S(1)}, u32[]{:S(2)}, u32[]{:S(2)}) collective-permute-start(bf16[784,128]{1,0:T(8,128)(2,1)S(1)} %shard_map.68.own_ref.one_ref), channel_id=1, source_target_pairs={{0,8},{1,9},{2,10},{3,11},{4,12},{5,13},{6,14},{7,15},{8,0},{9,1},... | collective-permute-start | bytes 602120 | tf_op jit(solution)/shard_map/ppermute | solution.py:199
  10.8 16.3 %collective-permute-start.1 = (bf16[784,128]{1,0:T(8,128)(2,1)S(1)}, bf16[784,128]{1,0:T(8,128)(2,1)S(1)}, u32[]{:S(2)}, u32[]{:S(2)}) collective-permute-start(bf16[784,128]{1,0:T(8,128)(2,1)S(1)} %shard_map.68.own_ref.one_ref), channel_id=1, source_target_pairs={{0,12},{1,13},{2,14},{3,15},{4,8},{5,9},{6,10},{7,11},{8,4},{9,5},... | collective-permute-start | bytes 602120 | tf_op jit(solution)/shard_map/ppermute | solution.py:199
  10.8 16.8 %collective-permute-start.8 = (bf16[784,128]{1,0:T(8,128)(2,1)S(1)}, bf16[784,128]{1,0:T(8,128)(2,1)S(1)}, u32[]{:S(2)}, u32[]{:S(2)}) collective-permute-start(bf16[784,128]{1,0:T(8,128)(2,1)S(1)} %shard_map.68.own_ref.one_ref), channel_id=1, source_target_pairs={{0,2},{1,3},{2,0},{3,1},{4,6},{5,7},{6,4},{7,5},{8,10},{9,11},{10,... | collective-permute-start | bytes 602120 | tf_op jit(solution)/shard_map/ppermute | solution.py:199
  17.1 12.6 %collective-permute-start.7 = (bf16[784,128]{1,0:T(8,128)(2,1)S(1)}, bf16[784,128]{1,0:T(8,128)(2,1)S(1)}, u32[]{:S(2)}, u32[]{:S(2)}) collective-permute-start(bf16[784,128]{1,0:T(8,128)(2,1)S(1)} %collective-permute-done.6.one_ref), channel_id=1, source_target_pairs={{0,2},{1,3},{2,0},{3,1},{4,6},{5,7},{6,4},{7,5},{8,10},{9,11},{10,... | collective-permute-start | bytes 602120 | tf_op jit(solution)/shard_map/ppermute | solution.py:199
  25.6 6.0 %collective-permute-start.5 = (bf16[784,128]{1,0:T(8,128)(2,1)S(1)}, bf16[784,128]{1,0:T(8,128)(2,1)S(1)}, u32[]{:S(2)}, u32[]{:S(2)}) collective-permute-start(bf16[784,128]{1,0:T(8,128)(2,1)S(1)} %collective-permute-done.4.one_ref), channel_id=1, source_target_pairs={{0,2},{1,3},{2,0},{3,1},{4,6},{5,7},{6,4},{7,5},{8,10},{9,11},{10,... | collective-permute-start | bytes 602120 | tf_op jit(solution)/shard_map/ppermute | solution.py:199
  27.1 6.4 %collective-permute-start.2 = (bf16[784,128]{1,0:T(8,128)(2,1)S(1)}, bf16[784,128]{1,0:T(8,128)(2,1)S(1)}, u32[]{:S(2)}, u32[]{:S(2)}) collective-permute-start(bf16[784,128]{1,0:T(8,128)(2,1)S(1)} %collective-permute-done.1.one_ref), channel_id=1, source_target_pairs={{0,2},{1,3},{2,0},{3,1},{4,6},{5,7},{6,4},{7,5},{8,10},{9,11},{10,... | collective-permute-start | bytes 602120 | tf_op jit(solution)/shard_map/ppermute | solution.py:199
  35.4 4.0 %collective-permute-start.9 = (f32[72,128]{1,0:T(8,128)S(1)}, f32[72,128]{1,0:T(8,128)S(1)}, u32[]{:S(2)}, u32[]{:S(2)}) collective-permute-start(f32[72,128]{1,0:T(8,128)S(1)} %get-tuple-element.18), channel_id=1, source_target_pairs={{0,2},{1,3},{2,0},{3,1},{4,6},{5,7},{6,4},{7,5},{8,10},{9,11},{10,... | collective-permute-start | bytes 110600 | tf_op jit(solution)/shard_map/ppermute | solution.py:199
  39.4 5.1 %collective-permute-start.10 = (f32[72,128]{1,0:T(8,128)S(1)}, f32[72,128]{1,0:T(8,128)S(1)}, u32[]{:S(2)}, u32[]{:S(2)}) collective-permute-start(f32[72,128]{1,0:T(8,128)S(1)} %add.9), channel_id=1, source_target_pairs={{0,4},{1,5},{2,6},{3,7},{4,0},{5,1},{6,2},{7,3},{8,12},{9,13},{10,... | collective-permute-start | bytes 110600 | tf_op jit(solution)/shard_map/ppermute | solution.py:199
  44.6 5.0 %collective-permute-start.11 = (f32[72,128]{1,0:T(8,128)S(1)}, f32[72,128]{1,0:T(8,128)S(1)}, u32[]{:S(2)}, u32[]{:S(2)}) collective-permute-start(f32[72,128]{1,0:T(8,128)S(1)} %add.10), channel_id=1, source_target_pairs={{0,8},{1,9},{2,10},{3,11},{4,12},{5,13},{6,14},{7,15},{8,0},{9,1},... | collective-permute-start | bytes 110600 | tf_op jit(solution)/shard_map/ppermute | solution.py:199
  49.5 1.3 %collective-permute-start.12 = (f32[72,128]{1,0:T(8,128)S(1)}, f32[72,128]{1,0:T(8,128)S(1)}, u32[]{:S(2)}, u32[]{:S(2)}) collective-permute-start(f32[72,128]{1,0:T(8,128)S(1)} %add.11.q_ref), channel_id=1, source_target_pairs={{0,1},{1,0},{2,3},{3,2},{4,5},{5,4},{6,7},{7,6},{8,9},{9,8},{10,11... | collective-permute-start | bytes 110600 | tf_op jit(solution)/shard_map/ppermute | solution.py:199
  49.6 1.3 %collective-permute-start.13 = (f32[8,128]{1,0:T(8,128)S(1)}, f32[8,128]{1,0:T(8,128)S(1)}, u32[]{:S(2)}, u32[]{:S(2)}) collective-permute-start(f32[8,128]{1,0:T(8,128)S(1)} %get-tuple-element.22), channel_id=1, source_target_pairs={{0,1},{1,0},{2,3},{3,2},{4,5},{5,4},{6,7},{7,6},{8,9},{9,8},{10,11... | collective-permute-start | bytes 12296 | tf_op jit(solution)/shard_map/ppermute | solution.py:199

commit v2 on v0

v2 whole, which is shorter than its diff:
```python
import functools

import jax
import jax.numpy as jnp
from jax import lax
from jax.experimental import pallas as pl
from jax.experimental.pallas import tpu as pltpu
from jax.sharding import PartitionSpec as P

SPB = 8
EPSILON = 1e-06
LANES = 128
TAIL = 16
VMEM = pl.BlockSpec(memory_space=pltpu.VMEM)
HBM = pl.BlockSpec(memory_space=pltpu.HBM)


def unit_rows(values):
    wide = values.astype(jnp.float32)
    scale = lax.rsqrt(jnp.mean(wide * wide, axis=1, keepdims=True) + EPSILON)
    return (wide * scale).astype(jnp.bfloat16)


def product(left, right, dims=((1,), (0,))):
    return lax.dot_general(
        left, right, (dims, ((), ())), preferred_element_type=jnp.float32
    )


def thirds(value):
    parts = []
    for _ in range(3):
        part = value.astype(jnp.bfloat16)
        parts.append(part)
        value = value - part.astype(jnp.float32)
    return parts


def pack_cand(cand_ref, ids_ref, out_ref, raw, ids, sems):
    rows, width = raw.shape
    copies = [
        pltpu.make_async_copy(cand_ref, raw, sems.at[0]),
        pltpu.make_async_copy(ids_ref, ids, sems.at[1]),
    ]
    for copy in copies:
        copy.start()
    for copy in copies:
        copy.wait()
    out_ref[:width, :] = unit_rows(raw[...]).T
    within = (ids[...] - ids[0, 0]).astype(jnp.float32)
    out_ref[width:, :] = jnp.broadcast_to(within, (TAIL, rows)).astype(jnp.bfloat16)


def pack_train(*refs):
    for train_ref, lanczos_ref, weight_ref, out_ref in (
        refs[:3] + refs[6:7],
        refs[3:6] + refs[7:],
    ):
        count, rank = lanczos_ref.shape
        step = count // 6
        for i in range(6):
            part = slice(i * step, (i + 1) * step)
            out_ref[part, :] = unit_rows(train_ref[part, :])
        out_ref[count : count + rank, :] = lanczos_ref[...].T
        out_ref[count + rank :, :] = jnp.broadcast_to(
            weight_ref[...].astype(jnp.float32).reshape(1, count), (TAIL, count)
        ).astype(jnp.bfloat16)


def copy_after(value_ref, _, out_ref):
    out_ref[...] = value_ref[...]


def quartic(products, width):
    cosine = products * (1.0 / width)
    square = cosine * cosine
    return square * square


def member_of(ref, base, count):
    ids = ref[ref.shape[0] - TAIL :, :][:1].astype(jnp.int32) + base
    row = lax.broadcasted_iota(jnp.int32, (count, ids.shape[1]), 0)
    return (row == ids).astype(jnp.bfloat16)


def project(masks, chips, width, rank, first, one_ref, two_ref, town_ref, tsib_ref, *rest):
    chip = lax.axis_index("train") // 2
    pair = jnp.concatenate([one_ref[:width, :], two_ref[:width, :]], axis=1)
    structs = chips * SPB
    member = jnp.concatenate(
        [
            member_of(ref, lax.bitwise_xor(chip, mask) * SPB, structs)
            for ref, mask in zip((one_ref, two_ref), masks)
        ],
        axis=1,
    )
    proj = None
    for ref in (town_ref, tsib_ref):
        count = ref.shape[0] - rank - TAIL
        kernel_rows = quartic(product(ref[:count, :], pair), width).astype(jnp.bfloat16)
        term = product(ref[count:, :], kernel_rows)
        proj = term if proj is None else proj + term
    sums = sum(product(member, part, ((1,), (1,))) for part in thirds(proj))
    size = jnp.sum(member.astype(jnp.float32), axis=1, keepdims=True)
    sums = sums * (1.0 / jnp.maximum(size, 1.0))
    lane = lax.broadcasted_iota(jnp.int32, (SPB, TAIL), 1)
    means = jnp.zeros((SPB, TAIL), jnp.float32)
    for c in range(chips):
        means = jnp.where(lane == c, sums[c * SPB : (c + 1) * SPB, rank:], means)
    means = jnp.concatenate([means, jnp.zeros((SPB, rank - TAIL), jnp.float32)], axis=1)
    total = jnp.concatenate([sums[:, :rank], means], axis=0)
    if first:
        rest[0][...] = total
    else:
        rest[1][...] = rest[0][...] + total


def prior_part(masks, chips, width, first, own_ref, sib_ref, *rest):
    refs, rest = rest[: len(masks)], rest[len(masks) :]
    me = lax.axis_index("train")
    chip, core = me // 2, me % 2
    mine = jnp.concatenate([own_ref[:width, :], sib_ref[:width, :]], axis=1)
    none = jnp.zeros((SPB, own_ref.shape[1]), jnp.bfloat16)
    left = jnp.concatenate(
        [
            jnp.concatenate([member_of(own_ref, 0, SPB), none], axis=1),
            jnp.concatenate([none, member_of(sib_ref, 0, SPB)], axis=1),
        ],
        axis=0,
    )
    left_size = jnp.sum(left.astype(jnp.float32), axis=1, keepdims=True)
    total = None
    for i in range(0, len(masks), 2):
        two = refs[i : i + 2]
        pair = jnp.concatenate([ref[:width, :] for ref in two], axis=1)
        wide = jnp.concatenate(
            [
                member_of(ref, (lax.bitwise_xor(chip, mask) * 2 + core) * SPB, 2 * chips * SPB)
                for ref, mask in zip(two, masks[i : i + 2])
            ],
            axis=1,
        )
        wide_size = jnp.maximum(
            jnp.sum(wide.astype(jnp.float32), axis=1, keepdims=True), 1.0
        )
        pairs = quartic(product(mine, pair, ((0,), (0,))), width)
        half = sum(product(left, part) for part in thirds(pairs)) / left_size
        weight = thirds(wide.astype(jnp.float32) / wide_size)
        term = sum(
            product(a, b, ((1,), (1,)))
            for i, a in enumerate(thirds(half))
            for b in weight[: 3 - i]
        )
        total = term if total is None else total + term
    if first:
        rest[0][...] = total
    else:
        rest[1][...] = rest[0][...] + total


def finish(q_ref, other_ref, mine_ref, theirs_ref, mean_ref, cov_ref, all_ref):
    structs = q_ref.shape[0] - SPB
    me = lax.axis_index("train")
    chip, core = me // 2, me % 2
    for p in range(structs // SPB):
        rows = slice(p * SPB, (p + 1) * SPB)
        here = pl.multiple_of((2 * p + core) * SPB, SPB)
        there = pl.multiple_of((2 * p + 1 - core) * SPB, SPB)
        all_ref[pl.ds(here, SPB), :] = q_ref[rows, :]
        all_ref[pl.ds(there, SPB), :] = other_ref[rows, :]
    own = thirds(q_ref[pl.ds(pl.multiple_of(chip * SPB, SPB), SPB), :])
    every = thirds(all_ref[...])
    square = sum(
        product(a, b, ((1,), (1,))) for i, a in enumerate(own) for b in every[: 3 - i]
    )
    cov_ref[...] = mine_ref[...] + theirs_ref[...] - square
    lane = lax.broadcasted_iota(jnp.int32, (SPB, LANES), 1)
    row = lax.broadcasted_iota(jnp.int32, (SPB, LANES), 0)
    means = q_ref[structs:, :]
    column = jnp.sum(jnp.where(lane == chip, means, 0.0), axis=1, keepdims=True)
    mean_ref[...] = jnp.sum(jnp.where(lane == row, column, 0.0), axis=0)[:SPB]


def call(kernel, shapes, count, flops=0, scratch=()):
    many = isinstance(shapes, (tuple, list))
    return pl.pallas_call(
        kernel,
        out_shape=shapes,
        in_specs=[VMEM] * count,
        out_specs=[VMEM] * len(shapes) if many else VMEM,
        scratch_shapes=scratch,
        cost_estimate=pl.CostEstimate(flops=flops, bytes_accessed=0, transcendentals=0),
        compiler_params=pltpu.CompilerParams(vmem_limit_bytes=24 * 2**20),
    )


def body(size, cand_desc, struct_id, train_desc, lanczos, mean_weight):
    rows, width = cand_desc.shape
    count, rank = lanczos.shape
    chips = size // 2
    structs = chips * SPB

    def swap(value, mask):
        return lax.ppermute(value, "train", [(i, i ^ mask) for i in range(size)])

    block_shape = jax.ShapeDtypeStruct((width + TAIL, rows), jnp.bfloat16)
    own = pl.pallas_call(
        pack_cand,
        out_shape=block_shape,
        in_specs=[HBM, HBM],
        out_specs=VMEM,
        scratch_shapes=[
            pltpu.VMEM((rows, width), jnp.bfloat16),
            pltpu.VMEM((1, rows), jnp.int32),
            pltpu.SemaphoreType.DMA((2,)),
        ],
        compiler_params=pltpu.CompilerParams(vmem_limit_bytes=58 * 2**20),
    )(cand_desc, struct_id.reshape(1, rows))

    def again(value, other):
        return call(copy_after, block_shape, 2)(value, other)

    q_shape = jax.ShapeDtypeStruct((structs + SPB, rank), jnp.float32)
    prior_shape = jax.ShapeDtypeStruct((2 * SPB, 2 * structs), jnp.float32)

    def add_projection(masks, state, *pair):
        state = () if state is None else (state,)
        kernel = functools.partial(project, masks, chips, width, rank, not state)
        return call(
            kernel,
            q_shape,
            4 + len(state),
            flops=2 * 2 * rows * 2 * count * (width + 2 * rank),
        )(*pair, train_own, train_sib, *state)

    def add_prior(masks, state, *refs):
        state = () if state is None else (state,)
        kernel = functools.partial(prior_part, masks, chips, width, not state)
        return call(
            kernel,
            prior_shape,
            2 + len(refs) + len(state),
            flops=2 * 2 * rows * len(refs) * rows * (width + 2 * rank),
        )(own, sib, *refs, *state)

    train = (train_desc, lanczos, mean_weight)
    train_shape = jax.ShapeDtypeStruct((count + rank + TAIL, width), jnp.bfloat16)
    train_own, train_sib = call(pack_train, (train_shape, train_shape), 6)(
        *train, *[swap(value, 1) for value in train]
    )
    blocks = {0: own}
    if size == 16:
        for mask in (1, 4, 2):
            blocks[mask] = swap(own, 2 * mask)
        blocks[6] = swap(again(own, train_own), 12)
        blocks[3] = swap(blocks[2], 2)
        blocks[5] = swap(blocks[4], 2)
        blocks[7] = swap(blocks[6], 2)
    else:
        for mask in range(1, chips):
            blocks[mask] = swap(own, 2 * mask)
    sib = swap(own, 1)
    q = prior = None
    for mask in range(0, chips, 2):
        masks = (mask, mask + 1)
        q = add_projection(masks, q, blocks[mask], blocks[mask + 1])
    prior = add_prior(tuple(range(chips)), None, *[blocks[m] for m in range(chips)])

    theirs = swap(prior[SPB:], 1)
    mask = 2
    while mask < size:
        q = q + swap(q, mask)
        mask *= 2
    other = swap(q, 1)
    mean, covariance = call(
        finish,
        (
            jax.ShapeDtypeStruct((SPB,), jnp.float32),
            jax.ShapeDtypeStruct((SPB, 2 * structs), jnp.float32),
        ),
        4,
        scratch=[pltpu.VMEM((2 * structs, rank), jnp.float32)],
    )(q, other, prior[:SPB], theirs)
    return mean, covariance[None]


def solution(mesh):
    placed = (
        P(("pool", "cand", "train"), None),
        P(("pool", "cand", "train")),
        P(("pool", "train"), None),
        P(("pool", "train"), None),
        P(("pool", "train")),
    )
    return jax.shard_map(
        functools.partial(body, mesh.shape["train"]),
        mesh=mesh,
        in_specs=placed,
        out_specs=(P(("pool", "cand", "train")), P(("pool", "cand"), "train", None)),
        check_vma=False,
    )
```

time: 157 us -> 50.6 us (0.32)
  blocking collectives: 69.3 us -> 0 us
  waiting for transfers between devices: 46.6 us -> 18.3 us
  matrix products: 20 us -> 0 us
  starting transfers between devices: 0.08 us -> 17.7 us
  between operations: 14.8 us -> 0.74 us
  Pallas kernels: 0 us -> 10.7 us
  other arithmetic: 5.04 us -> 0.02 us
  local copies, waits for them, and re-layouts: 0.99 us -> 2.88 us
    all_gather x1 -> x0, waiting for transfers between devices: 46.1 us -> none  [body(): lax.all_gather(cand_unit, 'train', axis=0, tiled=True)]
    all_gather x2 -> x0, blocking collectives: 38.7 us -> none  [the longest x1 19.6 us: body(): all_q = lax.all_gather(own_q, 'train', axis=0, tiled=True)]
    unnamed x1 -> x0, blocking collectives: 30.6 us -> none
    dot_general x18 -> x0, matrix products: 20 us -> none  [the longest x5 10.9 us: kernel_block(): lax.dot_general(left, right, (((1,), (1,)), ((), ())), preferred_element_...]
    ppermute x0 -> x16, waiting for transfers between devices: none -> 18.3 us  [swap(): return lax.ppermute(value, 'train', [(i, i ^ mask) for i in range(size)])]
    ppermute x0 -> x16, starting transfers between devices: none -> 17.7 us  [swap(): return lax.ppermute(value, 'train', [(i, i ^ mask) for i in range(size)])]
    pallas_call x0 -> x9, Pallas kernels: none -> 10.7 us  [the longest x4 5.39 us: add_projection(): call(kernel, q_shape, 4 + len(state), flops=2 * 2 * rows * 2 * count * (w...]
    reduce_sum x4 -> x0, other arithmetic: 2.95 us -> none  [the longest x2 2.74 us: unit_rows(): scale = lax.rsqrt(jnp.mean(wide * wide, axis=1, keepdims=True) + EPSILON)]
  transfers between devices with their start and end apart: 2 -> 16, of which waited for: 2 -> 11; matrix products, arithmetic and copies ran while one was open for 5% -> 0% of each run, Pallas kernels for 0% -> 20%
where the time goes in v2:
time: 50.6 us; the launch traced here: 50.4 us
  waiting for transfers between devices  18.3 us (36%)
  starting transfers between devices  17.7 us (35%)
  Pallas kernels  10.7 us (21%)
  local copies, waits for them, and re-layouts  2.88 us (6%)
  between operations  0.74 us (1%)
    ppermute x16, waiting for transfers between devices, swap(): return lax.ppermute(value, 'train', [(i, i ^ mask) for i in range(size)])  18.3 us
    ppermute x16, starting transfers between devices, swap(): return lax.ppermute(value, 'train', [(i, i ^ mask) for i in range(size)])  17.7 us
    pallas_call x4, Pallas kernels, add_projection(): call(kernel, q_shape, 4 + len(state), flops=2 * 2 * rows * 2 * count * (w...  5.39 us
    unnamed x8, local copies, waits for them, and re-layouts  2.88 us
    pallas_call x1, Pallas kernels, add_prior(): call(kernel, prior_shape, 2 + len(refs) + len(state), flops=2 * 2 * rows...  1.84 us
    pallas_call x1, Pallas kernels, body(): pl.pallas_call(pack_cand, out_shape=block_shape, in_specs=[HBM, HBM], out...  1.84 us
  transfers between devices with their start and end apart: 16, of which 11 were waited for; matrix products, arithmetic and copies ran while one was open for 0% of the time, Pallas kernels for 20%

profile of v2, /device:TPU:0, one launch (start us, length us, event | category | flops | bytes accessed | tf_op | source)
XLA Modules:
  0.0 50.4 jit_solution(18382261292464888677)
XLA Ops:
  1.2 1.8 %shard_map.68.value_ref.one_ref.own_ref.rest_0_ = bf16[784,128]{1,0:T(8,128)(2,1)} custom-call(bf16[128,768]{1,0:T(8,128)(2,1)} %cand_ref.1, s32[1,128]{1,0:T(1,128)} %bitcast.2), custom_call_target="tpu_custom_call" | custom-call | tf_op jit(solution)/shard_map/pallas_call | solution.py:207
  3.1 3.1 %collective-permute-start.7 = (bf16[784,128]{1,0:T(8,128)(2,1)}, bf16[784,128]{1,0:T(8,128)(2,1)S(1)}, u32[]{:S(2)}, u32[]{:S(2)}) collective-permute-start(bf16[784,128]{1,0:T(8,128)(2,1)} %shard_map.68.value_ref.one_ref.own_ref.rest_0_), channel_id=1, source_target_pairs={{0,4},{1,5},{2,6},{3,7},{4,0},{5,1},{6,2},{7,3},{8,12},{9,13},{10,... | collective-permute-start | bytes 602120 | tf_op jit(solution)/shard_map/ppermute | solution.py:204
  6.2 2.6 %collective-permute-start.5 = (bf16[784,128]{1,0:T(8,128)(2,1)}, bf16[784,128]{1,0:T(8,128)(2,1)S(1)}, u32[]{:S(2)}, u32[]{:S(2)}) collective-permute-start(bf16[784,128]{1,0:T(8,128)(2,1)} %shard_map.68.value_ref.one_ref.own_ref.rest_0_), channel_id=1, source_target_pairs={{0,8},{1,9},{2,10},{3,11},{4,12},{5,13},{6,14},{7,15},{8,0},{9,1},... | collective-permute-start | bytes 602120 | tf_op jit(solution)/shard_map/ppermute | solution.py:204
  8.7 1.4 %collective-permute-done.2.refs_5_ = bf16[768]{0:T(1024)(128)(2,1)S(1)} collective-permute-done((bf16[768]{0:T(1024)(128)(2,1)}, bf16[768]{0:T(1024)(128)(2,1)S(1)}, u32[]{:S(2)}, u32[]{:S(2)}) %collective-permute-start.2) | collective-permute-done | bytes 1568 | tf_op jit(solution)/shard_map/ppermute | solution.py:204
  10.1 1.3 %copy-done.1 = bf16[768,768]{1,0:T(8,128)(2,1)S(1)} copy-done((bf16[768,768]{1,0:T(8,128)(2,1)S(1)}, bf16[768,768]{1,0:T(8,128)(2,1)}, u32[]{:S(2)}) %copy-start.1) | copy-done | bytes 1179672
  11.4 0.9 %copy-done.2 = bf16[768,128]{1,0:T(8,128)(2,1)S(1)} copy-done((bf16[768,128]{1,0:T(8,128)(2,1)S(1)}, bf16[768,128]{1,0:T(8,128)(2,1)}, u32[]{:S(2)}) %copy-start.2) | copy-done | bytes 196632
  13.9 1.7 %collective-permute-start.9 = (bf16[784,128]{1,0:T(8,128)(2,1)S(1)}, bf16[784,128]{1,0:T(8,128)(2,1)S(1)}, u32[]{:S(2)}, u32[]{:S(2)}) collective-permute-start(bf16[784,128]{1,0:T(8,128)(2,1)S(1)} %copy-done), channel_id=1, source_target_pairs={{0,2},{1,3},{2,0},{3,1},{4,6},{5,7},{6,4},{7,5},{8,10},{9,11},{10,... | collective-permute-start | bytes 602120 | tf_op jit(solution)/shard_map/ppermute | solution.py:204
  15.8 1.7 %collective-permute-start.8 = (bf16[784,128]{1,0:T(8,128)(2,1)S(1)}, bf16[784,128]{1,0:T(8,128)(2,1)S(1)}, u32[]{:S(2)}, u32[]{:S(2)}) collective-permute-start(bf16[784,128]{1,0:T(8,128)(2,1)S(1)} %collective-permute-done.7.one_ref.rest_2_), channel_id=1, source_target_pairs={{0,2},{1,3},{2,0},{3,1},{4,6},{5,7},{6,4},{7,5},{8,10},{9,11},{10,... | collective-permute-start | bytes 602120 | tf_op jit(solution)/shard_map/ppermute | solution.py:204
  17.4 1.0 %collective-permute-done.5.one_ref.rest_4_ = bf16[784,128]{1,0:T(8,128)(2,1)S(1)} collective-permute-done((bf16[784,128]{1,0:T(8,128)(2,1)}, bf16[784,128]{1,0:T(8,128)(2,1)S(1)}, u32[]{:S(2)}, u32[]{:S(2)}) %collective-permute-start.5) | collective-permute-done | bytes 200736 | tf_op jit(solution)/shard_map/ppermute | solution.py:204
  18.4 1.5 %collective-permute-start.6 = (bf16[784,128]{1,0:T(8,128)(2,1)S(1)}, bf16[784,128]{1,0:T(8,128)(2,1)S(1)}, u32[]{:S(2)}, u32[]{:S(2)}) collective-permute-start(bf16[784,128]{1,0:T(8,128)(2,1)S(1)} %collective-permute-done.5.one_ref.rest_4_), channel_id=1, source_target_pairs={{0,2},{1,3},{2,0},{3,1},{4,6},{5,7},{6,4},{7,5},{8,10},{9,11},{10,... | collective-permute-start | bytes 602120 | tf_op jit(solution)/shard_map/ppermute | solution.py:204
  19.9 3.0 %collective-permute-done.3.one_ref.rest_6_ = bf16[784,128]{1,0:T(8,128)(2,1)S(1)} collective-permute-done((bf16[784,128]{1,0:T(8,128)(2,1)S(1)}, bf16[784,128]{1,0:T(8,128)(2,1)S(1)}, u32[]{:S(2)}, u32[]{:S(2)}) %collective-permute-start.3) | collective-permute-done | bytes 200736 | tf_op jit(solution)/shard_map/ppermute | solution.py:204
  22.8 1.5 %collective-permute-start.4 = (bf16[784,128]{1,0:T(8,128)(2,1)S(1)}, bf16[784,128]{1,0:T(8,128)(2,1)S(1)}, u32[]{:S(2)}, u32[]{:S(2)}) collective-permute-start(bf16[784,128]{1,0:T(8,128)(2,1)S(1)} %collective-permute-done.3.one_ref.rest_6_), channel_id=1, source_target_pairs={{0,2},{1,3},{2,0},{3,1},{4,6},{5,7},{6,4},{7,5},{8,10},{9,11},{10,... | collective-permute-start | bytes 602120 | tf_op jit(solution)/shard_map/ppermute | solution.py:204
  24.3 1.3 %shard_map.71.rest_0_ = f32[72,128]{1,0:T(8,128)S(1)} custom-call(bf16[784,128]{1,0:T(8,128)(2,1)S(1)} %copy-done, bf16[784,128]{1,0:T(8,128)(2,1)S(1)} %collective-permute-done.9.two_ref.rest_1_, bf16[912,768]{1,0:T(8,128)(2,1)S(1)} %get-tuple-element.6._.town_ref, bf16[912,768]{1,0:T(8,128)(2,1)S(1)} %get-tuple-element.7.tsib_ref), custom_call_target="tpu_custom_call" | custom-call | flops 805306368 | tf_op jit(solution)/shard_map/pallas_call | solution.py:229
  26.1 1.3 %shard_map.72.rest_0_ = f32[72,128]{1,0:T(8,128)S(1)} custom-call(bf16[784,128]{1,0:T(8,128)(2,1)S(1)} %collective-permute-done.7.one_ref.rest_2_, bf16[784,128]{1,0:T(8,128)(2,1)S(1)} %collective-permute-done.8.two_ref.rest_3_, bf16[912,768]{1,0:T(8,128)(2,1)S(1)} %get-tuple-element.6._.town_ref, bf16[912,768]{1,0:T(8,128)(2,1)S(1)} %get-tuple-element.7.tsib_ref, ...), custom_call_target="tpu_custom_call" | custom-call | flops 805306368 | tf_op jit(solution)/shard_map/pallas_call | solution.py:229
  27.5 2.9 %collective-permute-done.6.two_ref.rest_5_ = bf16[784,128]{1,0:T(8,128)(2,1)S(1)} collective-permute-done((bf16[784,128]{1,0:T(8,128)(2,1)S(1)}, bf16[784,128]{1,0:T(8,128)(2,1)S(1)}, u32[]{:S(2)}, u32[]{:S(2)}) %collective-permute-start.6) | collective-permute-done | bytes 200736 | tf_op jit(solution)/shard_map/ppermute | solution.py:204
  30.4 1.3 %shard_map.73.rest_0_ = f32[72,128]{1,0:T(8,128)S(1)} custom-call(bf16[784,128]{1,0:T(8,128)(2,1)S(1)} %collective-permute-done.5.one_ref.rest_4_, bf16[784,128]{1,0:T(8,128)(2,1)S(1)} %collective-permute-done.6.two_ref.rest_5_, bf16[912,768]{1,0:T(8,128)(2,1)S(1)} %get-tuple-element.6._.town_ref, bf16[912,768]{1,0:T(8,128)(2,1)S(1)} %get-tuple-element.7.tsib_ref, ...), custom_call_target="tpu_custom_call" | custom-call | flops 805306368 | tf_op jit(solution)/shard_map/pallas_call | solution.py:229
  31.8 2.2 %collective-permute-done.4.two_ref.rest_7_ = bf16[784,128]{1,0:T(8,128)(2,1)S(1)} collective-permute-done((bf16[784,128]{1,0:T(8,128)(2,1)S(1)}, bf16[784,128]{1,0:T(8,128)(2,1)S(1)}, u32[]{:S(2)}, u32[]{:S(2)}) %collective-permute-start.4) | collective-permute-done | bytes 200736 | tf_op jit(solution)/shard_map/ppermute | solution.py:204
  34.0 1.3 %shard_map.74 = f32[72,128]{1,0:T(8,128)S(1)} custom-call(bf16[784,128]{1,0:T(8,128)(2,1)S(1)} %collective-permute-done.3.one_ref.rest_6_, bf16[784,128]{1,0:T(8,128)(2,1)S(1)} %collective-permute-done.4.two_ref.rest_7_, bf16[912,768]{1,0:T(8,128)(2,1)S(1)} %get-tuple-element.6._.town_ref, bf16[912,768]{1,0:T(8,128)(2,1)S(1)} %get-tuple-element.7.tsib_ref, ...), custom_call_target="tpu_custom_call" | custom-call | flops 805306368 | tf_op jit(solution)/shard_map/pallas_call | solution.py:229
  35.3 1.6 %collective-permute-start.10 = (f32[72,128]{1,0:T(8,128)S(1)}, f32[72,128]{1,0:T(8,128)S(1)}, u32[]{:S(2)}, u32[]{:S(2)}) collective-permute-start(f32[72,128]{1,0:T(8,128)S(1)} %shard_map.74), channel_id=1, source_target_pairs={{0,2},{1,3},{2,0},{3,1},{4,6},{5,7},{6,4},{7,5},{8,10},{9,11},{10,... | collective-permute-start | bytes 110600 | tf_op jit(solution)/shard_map/ppermute | solution.py:204
  36.9 2.5 %collective-permute-done.10 = f32[72,128]{1,0:T(8,128)S(1)} collective-permute-done((f32[72,128]{1,0:T(8,128)S(1)}, f32[72,128]{1,0:T(8,128)S(1)}, u32[]{:S(2)}, u32[]{:S(2)}) %collective-permute-start.10) | collective-permute-done | bytes 36896 | tf_op jit(solution)/shard_map/ppermute | solution.py:204
  39.9 3.4 %collective-permute-done.11 = f32[72,128]{1,0:T(8,128)S(1)} collective-permute-done((f32[72,128]{1,0:T(8,128)S(1)}, f32[72,128]{1,0:T(8,128)S(1)}, u32[]{:S(2)}, u32[]{:S(2)}) %collective-permute-start.11) | collective-permute-done | bytes 36896 | tf_op jit(solution)/shard_map/ppermute | solution.py:204
  43.3 2.4 %collective-permute-start.12 = (f32[72,128]{1,0:T(8,128)S(1)}, f32[72,128]{1,0:T(8,128)S(1)}, u32[]{:S(2)}, u32[]{:S(2)}) collective-permute-start(f32[72,128]{1,0:T(8,128)S(1)} %add.10), channel_id=1, source_target_pairs={{0,8},{1,9},{2,10},{3,11},{4,12},{5,13},{6,14},{7,15},{8,0},{9,1},... | collective-permute-start | bytes 110600 | tf_op jit(solution)/shard_map/ppermute | solution.py:204
  45.7 1.8 %shard_map.75 = f32[16,128]{1,0:T(8,128)S(1)} custom-call(bf16[784,128]{1,0:T(8,128)(2,1)S(1)} %copy-done, bf16[784,128]{1,0:T(8,128)(2,1)S(1)} %collective-permute-done.14.sib_ref, bf16[784,128]{1,0:T(8,128)(2,1)S(1)} %copy-done, bf16[784,128]{1,0:T(8,128)(2,1)S(1)} %collective-permute-done.9.two_ref.rest_1_, ...), custom_call_target="tpu_custom_call" | custom-call | flops 536870912 | tf_op jit(solution)/shard_map/pallas_call | solution.py:239
  49.5 0.8 %shard_map.76 = (f32[8]{0:T(128)}, f32[8,128]{1,0:T(8,128)}) custom-call(f32[72,128]{1,0:T(8,128)S(1)} %add.11.q_ref, f32[72,128]{1,0:T(8,128)S(1)} %collective-permute-done.13.other_ref, f32[8,128]{1,0:T(8,128)S(1)} %get-tuple-element.11.mine_ref, f32[8,128]{1,0:T(8,128)S(1)} %collective-permute-done.15.theirs_ref), custom_call_target="tpu_custom_call" | custom-call | tf_op jit(solution)/shard_map/pallas_call | solution.py:275
  (29 shorter events, 5.3 us)
Async XLA Ops:
  0.6 9.5 %collective-permute-start = (bf16[768,768]{1,0:T(8,128)(2,1)}, bf16[768,768]{1,0:T(8,128)(2,1)S(1)}, u32[]{:S(2)}, u32[]{:S(2)}) collective-permute-start(bf16[768,768]{1,0:T(8,128)(2,1)} %refs_0_.1), channel_id=1, source_target_pairs={{0,1},{1,0},{2,3},{3,2},{4,5},{5,4},{6,7},{7,6},{8,9},{9,8},{10,11... | collective-permute-start | bytes 3538952 | tf_op jit(solution)/shard_map/ppermute | solution.py:204
  1.1 9.0 %collective-permute-start.1 = (bf16[768,128]{1,0:T(8,128)(2,1)}, bf16[768,128]{1,0:T(8,128)(2,1)S(1)}, u32[]{:S(2)}, u32[]{:S(2)}) collective-permute-start(bf16[768,128]{1,0:T(8,128)(2,1)} %refs_1_.1), channel_id=1, source_target_pairs={{0,1},{1,0},{2,3},{3,2},{4,5},{5,4},{6,7},{7,6},{8,9},{9,8},{10,11... | collective-permute-start | bytes 589832 | tf_op jit(solution)/shard_map/ppermute | solution.py:204
  3.1 10.7 %copy-start = (bf16[784,128]{1,0:T(8,128)(2,1)S(1)}, bf16[784,128]{1,0:T(8,128)(2,1)}, u32[]{:S(2)}) copy-start(bf16[784,128]{1,0:T(8,128)(2,1)} %shard_map.68.value_ref.one_ref.own_ref.rest_0_) | copy-start | bytes 602116
  3.1 12.7 %collective-permute-start.7 = (bf16[784,128]{1,0:T(8,128)(2,1)}, bf16[784,128]{1,0:T(8,128)(2,1)S(1)}, u32[]{:S(2)}, u32[]{:S(2)}) collective-permute-start(bf16[784,128]{1,0:T(8,128)(2,1)} %shard_map.68.value_ref.one_ref.own_ref.rest_0_), channel_id=1, source_target_pairs={{0,4},{1,5},{2,6},{3,7},{4,0},{5,1},{6,2},{7,3},{8,12},{9,13},{10,... | collective-permute-start | bytes 602120 | tf_op jit(solution)/shard_map/ppermute | solution.py:204
  6.2 12.2 %collective-permute-start.5 = (bf16[784,128]{1,0:T(8,128)(2,1)}, bf16[784,128]{1,0:T(8,128)(2,1)S(1)}, u32[]{:S(2)}, u32[]{:S(2)}) collective-permute-start(bf16[784,128]{1,0:T(8,128)(2,1)} %shard_map.68.value_ref.one_ref.own_ref.rest_0_), channel_id=1, source_target_pairs={{0,8},{1,9},{2,10},{3,11},{4,12},{5,13},{6,14},{7,15},{8,0},{9,1},... | collective-permute-start | bytes 602120 | tf_op jit(solution)/shard_map/ppermute | solution.py:204
  8.7 1.4 %collective-permute-start.2 = (bf16[768]{0:T(1024)(128)(2,1)}, bf16[768]{0:T(1024)(128)(2,1)S(1)}, u32[]{:S(2)}, u32[]{:S(2)}) collective-permute-start(bf16[768]{0:T(1024)(128)(2,1)} %refs_2_.1), channel_id=1, source_target_pairs={{0,1},{1,0},{2,3},{3,2},{4,5},{5,4},{6,7},{7,6},{8,9},{9,8},{10,11... | collective-permute-start | bytes 4616 | tf_op jit(solution)/shard_map/ppermute | solution.py:204
  10.1 1.3 %copy-start.1 = (bf16[768,768]{1,0:T(8,128)(2,1)S(1)}, bf16[768,768]{1,0:T(8,128)(2,1)}, u32[]{:S(2)}) copy-start(bf16[768,768]{1,0:T(8,128)(2,1)} %refs_0_.1) | copy-start | bytes 3538948
  11.4 0.9 %copy-start.2 = (bf16[768,128]{1,0:T(8,128)(2,1)S(1)}, bf16[768,128]{1,0:T(8,128)(2,1)}, u32[]{:S(2)}) copy-start(bf16[768,128]{1,0:T(8,128)(2,1)} %refs_1_.1) | copy-start | bytes 589828
  12.3 0.7 %copy-start.3 = (bf16[768]{0:T(1024)(128)(2,1)S(1)}, bf16[768]{0:T(1024)(128)(2,1)}, u32[]{:S(2)}) copy-start(bf16[768]{0:T(1024)(128)(2,1)} %refs_2_.1) | copy-start | bytes 4612
  13.9 9.0 %collective-permute-start.3 = (bf16[784,128]{1,0:T(8,128)(2,1)S(1)}, bf16[784,128]{1,0:T(8,128)(2,1)S(1)}, u32[]{:S(2)}, u32[]{:S(2)}) collective-permute-start(bf16[784,128]{1,0:T(8,128)(2,1)S(1)} %shard_map.70), channel_id=1, source_target_pairs={{0,12},{1,13},{2,14},{3,15},{4,8},{5,9},{6,10},{7,11},{8,4},{9,5},... | collective-permute-start | bytes 602120 | tf_op jit(solution)/shard_map/ppermute | solution.py:204
  13.9 10.4 %collective-permute-start.9 = (bf16[784,128]{1,0:T(8,128)(2,1)S(1)}, bf16[784,128]{1,0:T(8,128)(2,1)S(1)}, u32[]{:S(2)}, u32[]{:S(2)}) collective-permute-start(bf16[784,128]{1,0:T(8,128)(2,1)S(1)} %copy-done), channel_id=1, source_target_pairs={{0,2},{1,3},{2,0},{3,1},{4,6},{5,7},{6,4},{7,5},{8,10},{9,11},{10,... | collective-permute-start | bytes 602120 | tf_op jit(solution)/shard_map/ppermute | solution.py:204
  15.8 10.4 %collective-permute-start.8 = (bf16[784,128]{1,0:T(8,128)(2,1)S(1)}, bf16[784,128]{1,0:T(8,128)(2,1)S(1)}, u32[]{:S(2)}, u32[]{:S(2)}) collective-permute-start(bf16[784,128]{1,0:T(8,128)(2,1)S(1)} %collective-permute-done.7.one_ref.rest_2_), channel_id=1, source_target_pairs={{0,2},{1,3},{2,0},{3,1},{4,6},{5,7},{6,4},{7,5},{8,10},{9,11},{10,... | collective-permute-start | bytes 602120 | tf_op jit(solution)/shard_map/ppermute | solution.py:204
  18.4 12.0 %collective-permute-start.6 = (bf16[784,128]{1,0:T(8,128)(2,1)S(1)}, bf16[784,128]{1,0:T(8,128)(2,1)S(1)}, u32[]{:S(2)}, u32[]{:S(2)}) collective-permute-start(bf16[784,128]{1,0:T(8,128)(2,1)S(1)} %collective-permute-done.5.one_ref.rest_4_), channel_id=1, source_target_pairs={{0,2},{1,3},{2,0},{3,1},{4,6},{5,7},{6,4},{7,5},{8,10},{9,11},{10,... | collective-permute-start | bytes 602120 | tf_op jit(solution)/shard_map/ppermute | solution.py:204
  19.9 25.8 %collective-permute-start.14 = (bf16[784,128]{1,0:T(8,128)(2,1)S(1)}, bf16[784,128]{1,0:T(8,128)(2,1)S(1)}, u32[]{:S(2)}, u32[]{:S(2)}) collective-permute-start(bf16[784,128]{1,0:T(8,128)(2,1)S(1)} %copy-done), channel_id=1, source_target_pairs={{0,1},{1,0},{2,3},{3,2},{4,5},{5,4},{6,7},{7,6},{8,9},{9,8},{10,11... | collective-permute-start | bytes 602120 | tf_op jit(solution)/shard_map/ppermute | solution.py:204
  22.8 11.1 %collective-permute-start.4 = (bf16[784,128]{1,0:T(8,128)(2,1)S(1)}, bf16[784,128]{1,0:T(8,128)(2,1)S(1)}, u32[]{:S(2)}, u32[]{:S(2)}) collective-permute-start(bf16[784,128]{1,0:T(8,128)(2,1)S(1)} %collective-permute-done.3.one_ref.rest_6_), channel_id=1, source_target_pairs={{0,2},{1,3},{2,0},{3,1},{4,6},{5,7},{6,4},{7,5},{8,10},{9,11},{10,... | collective-permute-start | bytes 602120 | tf_op jit(solution)/shard_map/ppermute | solution.py:204
  35.3 4.0 %collective-permute-start.10 = (f32[72,128]{1,0:T(8,128)S(1)}, f32[72,128]{1,0:T(8,128)S(1)}, u32[]{:S(2)}, u32[]{:S(2)}) collective-permute-start(f32[72,128]{1,0:T(8,128)S(1)} %shard_map.74), channel_id=1, source_target_pairs={{0,2},{1,3},{2,0},{3,1},{4,6},{5,7},{6,4},{7,5},{8,10},{9,11},{10,... | collective-permute-start | bytes 110600 | tf_op jit(solution)/shard_map/ppermute | solution.py:204
  39.4 4.0 %collective-permute-start.11 = (f32[72,128]{1,0:T(8,128)S(1)}, f32[72,128]{1,0:T(8,128)S(1)}, u32[]{:S(2)}, u32[]{:S(2)}) collective-permute-start(f32[72,128]{1,0:T(8,128)S(1)} %add.9), channel_id=1, source_target_pairs={{0,4},{1,5},{2,6},{3,7},{4,0},{5,1},{6,2},{7,3},{8,12},{9,13},{10,... | collective-permute-start | bytes 110600 | tf_op jit(solution)/shard_map/ppermute | solution.py:204
  43.3 4.9 %collective-permute-start.12 = (f32[72,128]{1,0:T(8,128)S(1)}, f32[72,128]{1,0:T(8,128)S(1)}, u32[]{:S(2)}, u32[]{:S(2)}) collective-permute-start(f32[72,128]{1,0:T(8,128)S(1)} %add.10), channel_id=1, source_target_pairs={{0,8},{1,9},{2,10},{3,11},{4,12},{5,13},{6,14},{7,15},{8,0},{9,1},... | collective-permute-start | bytes 110600 | tf_op jit(solution)/shard_map/ppermute | solution.py:204
  48.2 1.3 %collective-permute-start.13 = (f32[72,128]{1,0:T(8,128)S(1)}, f32[72,128]{1,0:T(8,128)S(1)}, u32[]{:S(2)}, u32[]{:S(2)}) collective-permute-start(f32[72,128]{1,0:T(8,128)S(1)} %add.11.q_ref), channel_id=1, source_target_pairs={{0,1},{1,0},{2,3},{3,2},{4,5},{5,4},{6,7},{7,6},{8,9},{9,8},{10,11... | collective-permute-start | bytes 110600 | tf_op jit(solution)/shard_map/ppermute | solution.py:204
  48.2 1.3 %collective-permute-start.15 = (f32[8,128]{1,0:T(8,128)S(1)}, f32[8,128]{1,0:T(8,128)S(1)}, u32[]{:S(2)}, u32[]{:S(2)}) collective-permute-start(f32[8,128]{1,0:T(8,128)S(1)} %get-tuple-element.10), channel_id=1, source_target_pairs={{0,1},{1,0},{2,3},{3,2},{4,5},{5,4},{6,7},{7,6},{8,9},{9,8},{10,11... | collective-permute-start | bytes 12296 | tf_op jit(solution)/shard_map/ppermute | solution.py:204

commit v3 on v2

--- a/solution.py
+++ b/solution.py
@@ -67,8 +67,11 @@
         ).astype(jnp.bfloat16)
 
 
-def copy_after(value_ref, _, out_ref):
-    out_ref[...] = value_ref[...]
+def copy_after(value_ref, _, *out_refs):
+    start = 0
+    for ref in out_refs:
+        ref[...] = value_ref[start : start + ref.shape[0], :]
+        start += ref.shape[0]
 
 
 def quartic(products, width):
@@ -83,14 +86,19 @@
     return (row == ids).astype(jnp.bfloat16)
 
 
-def project(masks, chips, width, rank, first, one_ref, two_ref, town_ref, tsib_ref, *rest):
+def project(masks, chips, width, rank, first, parts, *rest):
+    refs, (town_ref, tsib_ref, *rest) = rest[: 2 * parts], rest[2 * parts :]
     chip = lax.axis_index("train") // 2
-    pair = jnp.concatenate([one_ref[:width, :], two_ref[:width, :]], axis=1)
+    one, two = (
+        jnp.concatenate([ref[...] for ref in refs[i : i + parts]], axis=0)
+        for i in (0, parts)
+    )
+    pair = jnp.concatenate([one[:width, :], two[:width, :]], axis=1)
     structs = chips * SPB
     member = jnp.concatenate(
         [
             member_of(ref, lax.bitwise_xor(chip, mask) * SPB, structs)
-            for ref, mask in zip((one_ref, two_ref), masks)
+            for ref, mask in zip((one, two), masks)
         ],
         axis=1,
     )
@@ -115,8 +123,11 @@
         rest[1][...] = rest[0][...] + total
 
 
-def prior_part(masks, chips, width, first, own_ref, sib_ref, *rest):
-    refs, rest = rest[: len(masks)], rest[len(masks) :]
+def prior_part(masks, chips, width, first, cuts, own_ref, sib_ref, *rest):
+    refs = []
+    for cut in cuts:
+        refs.append(jnp.concatenate([ref[...] for ref in rest[:cut]], axis=0))
+        rest = rest[cut:]
     me = lax.axis_index("train")
     chip, core = me // 2, me % 2
     mine = jnp.concatenate([own_ref[:width, :], sib_ref[:width, :]], axis=1)
@@ -217,25 +228,55 @@
         compiler_params=pltpu.CompilerParams(vmem_limit_bytes=58 * 2**20),
     )(cand_desc, struct_id.reshape(1, rows))
 
-    def again(value, other):
-        return call(copy_after, block_shape, 2)(value, other)
+    def again(value, other, pieces):
+        shapes = [
+            jax.ShapeDtypeStruct((piece, value.shape[1]), value.dtype) for piece in pieces
+        ]
+        return pl.pallas_call(
+            copy_after,
+            out_shape=shapes,
+            in_specs=[VMEM, pl.BlockSpec(memory_space=pl.ANY)],
+            out_specs=[VMEM] * len(shapes),
+            compiler_params=pltpu.CompilerParams(vmem_limit_bytes=24 * 2**20),
+        )(value, other)
+
+    def again_last(value, *others):
+        return pl.pallas_call(
+            lambda *refs: copy_after(refs[-2], None, refs[-1]),
+            out_shape=block_shape,
+            in_specs=[pl.BlockSpec(memory_space=pl.ANY)] * len(others) + [VMEM],
+            out_specs=VMEM,
+            compiler_params=pltpu.CompilerParams(vmem_limit_bytes=24 * 2**20),
+        )(*others, value)
+
+    def again_first(value, *others):
+        return pl.pallas_call(
+            lambda *refs: copy_after(refs[0], None, refs[-1]),
+            out_shape=block_shape,
+            in_specs=[VMEM] + [pl.BlockSpec(memory_space=pl.ANY)] * len(others),
+            out_specs=VMEM,
+            compiler_params=pltpu.CompilerParams(vmem_limit_bytes=24 * 2**20),
+        )(value, *others)
 
     q_shape = jax.ShapeDtypeStruct((structs + SPB, rank), jnp.float32)
     prior_shape = jax.ShapeDtypeStruct((2 * SPB, 2 * structs), jnp.float32)
 
     def add_projection(masks, state, *pair):
         state = () if state is None else (state,)
-        kernel = functools.partial(project, masks, chips, width, rank, not state)
+        parts = len(pair) // 2
+        kernel = functools.partial(project, masks, chips, width, rank, not state, parts)
         return call(
             kernel,
             q_shape,
-            4 + len(state),
+            2 + len(pair) + len(state),
             flops=2 * 2 * rows * 2 * count * (width + 2 * rank),
         )(*pair, train_own, train_sib, *state)
 
     def add_prior(masks, state, *refs):
         state = () if state is None else (state,)
-        kernel = functools.partial(prior_part, masks, chips, width, not state)
+        cuts = tuple(len(ref) for ref in refs)
+        refs = [part for ref in refs for part in ref]
+        kernel = functools.partial(prior_part, masks, chips, width, not state, cuts)
         return call(
             kernel,
             prior_shape,
@@ -243,27 +284,32 @@
             flops=2 * 2 * rows * len(refs) * rows * (width + 2 * rank),
         )(own, sib, *refs, *state)
 
+    blocks = {0: own}
+    if size == 16:
+        for mask in (4, 1, 2):
+            blocks[mask] = swap(own, 2 * mask)
+    else:
+        for mask in range(1, chips):
+            blocks[mask] = swap(own, 2 * mask)
     train = (train_desc, lanczos, mean_weight)
     train_shape = jax.ShapeDtypeStruct((count + rank + TAIL, width), jnp.bfloat16)
     train_own, train_sib = call(pack_train, (train_shape, train_shape), 6)(
         *train, *[swap(value, 1) for value in train]
     )
-    blocks = {0: own}
     if size == 16:
-        for mask in (1, 4, 2):
-            blocks[mask] = swap(own, 2 * mask)
-        blocks[6] = swap(again(own, train_own), 12)
-        blocks[3] = swap(blocks[2], 2)
-        blocks[5] = swap(blocks[4], 2)
+        far = again_first(blocks[4], blocks[1], blocks[2], train_own)
+        blocks[6] = swap(far, 4)
+        blocks[5] = swap(far, 2)
+        blocks[3] = swap(blocks[1], 4)
         blocks[7] = swap(blocks[6], 2)
-    else:
-        for mask in range(1, chips):
-            blocks[mask] = swap(own, 2 * mask)
+    blocks = {m: b if isinstance(b, (tuple, list)) else (b,) for m, b in blocks.items()}
     sib = swap(own, 1)
     q = prior = None
-    for mask in range(0, chips, 2):
-        masks = (mask, mask + 1)
-        q = add_projection(masks, q, blocks[mask], blocks[mask + 1])
+    groups = [(m, m + 1) for m in range(0, chips, 2)]
+    if size == 16:
+        groups = [(0, 1), (4, 5), (2, 6), (3, 7)]
+    for masks in groups:
+        q = add_projection(masks, q, *blocks[masks[0]], *blocks[masks[1]])
     prior = add_prior(tuple(range(chips)), None, *[blocks[m] for m in range(chips)])
 
     theirs = swap(prior[SPB:], 1)

time: 50.6 us -> 48.1 us (0.951)
  starting transfers between devices: 17.7 us -> 15.8 us
    ppermute x16, starting transfers between devices: 17.7 us -> 15.8 us  [swap(): return lax.ppermute(value, 'train', [(i, i ^ mask) for i in range(size)])]
    ppermute x16, waiting for transfers between devices: 18.3 us -> 17.8 us  [swap(): return lax.ppermute(value, 'train', [(i, i ^ mask) for i in range(size)])]
  transfers between devices with their start and end apart: 16 -> 16, of which waited for: 11 -> 10; matrix products, arithmetic and copies ran while one was open for 0% -> 0% of each run, Pallas kernels for 20% -> 21%
where the time goes in v3:
time: 48.1 us; the launch traced here: 47.9 us
  waiting for transfers between devices  17.8 us (37%)
  starting transfers between devices  15.8 us (33%)
  Pallas kernels  10.7 us (22%)
  local copies, waits for them, and re-layouts  2.89 us (6%)
  between operations  0.74 us (2%)
    ppermute x16, waiting for transfers between devices, swap(): return lax.ppermute(value, 'train', [(i, i ^ mask) for i in range(size)])  17.8 us
    ppermute x16, starting transfers between devices, swap(): return lax.ppermute(value, 'train', [(i, i ^ mask) for i in range(size)])  15.8 us
    pallas_call x4, Pallas kernels, add_projection(): call(kernel, q_shape, 2 + len(pair) + len(state), flops=2 * 2 * rows * 2...  5.39 us
    unnamed x8, local copies, waits for them, and re-layouts  2.88 us
    pallas_call x1, Pallas kernels, add_prior(): call(kernel, prior_shape, 2 + len(refs) + len(state), flops=2 * 2 * rows...  1.84 us
    pallas_call x1, Pallas kernels, body(): pl.pallas_call(pack_cand, out_shape=block_shape, in_specs=[HBM, HBM], out...  1.84 us
  transfers between devices with their start and end apart: 16, of which 10 were waited for; matrix products, arithmetic and copies ran while one was open for 0% of the time, Pallas kernels for 21%

profile of v3, /device:TPU:0, one launch (start us, length us, event | category | flops | bytes accessed | tf_op | source)
XLA Modules:
  0.0 47.9 jit_solution(1093144806079918078)
XLA Ops:
  1.1 1.8 %shard_map.68.rest_0_.own_ref = bf16[784,128]{1,0:T(8,128)(2,1)} custom-call(bf16[128,768]{1,0:T(8,128)(2,1)} %cand_ref.1, s32[1,128]{1,0:T(1,128)} %bitcast.2), custom_call_target="tpu_custom_call" | custom-call | tf_op jit(solution)/shard_map/pallas_call | solution.py:218
  3.0 2.6 %collective-permute-start = (bf16[784,128]{1,0:T(8,128)(2,1)}, bf16[784,128]{1,0:T(8,128)(2,1)S(1)}, u32[]{:S(2)}, u32[]{:S(2)}) collective-permute-start(bf16[784,128]{1,0:T(8,128)(2,1)} %shard_map.68.rest_0_.own_ref), channel_id=1, source_target_pairs={{0,2},{1,3},{2,0},{3,1},{4,6},{5,7},{6,4},{7,5},{8,10},{9,11},{10,... | collective-permute-start | bytes 602120 | tf_op jit(solution)/shard_map/ppermute | solution.py:215
  5.6 2.6 %collective-permute-start.2 = (bf16[784,128]{1,0:T(8,128)(2,1)}, bf16[784,128]{1,0:T(8,128)(2,1)S(1)}, u32[]{:S(2)}, u32[]{:S(2)}) collective-permute-start(bf16[784,128]{1,0:T(8,128)(2,1)} %shard_map.68.rest_0_.own_ref), channel_id=1, source_target_pairs={{0,8},{1,9},{2,10},{3,11},{4,12},{5,13},{6,14},{7,15},{8,0},{9,1},... | collective-permute-start | bytes 602120 | tf_op jit(solution)/shard_map/ppermute | solution.py:215
  8.2 1.6 %collective-permute-start.3 = (bf16[784,128]{1,0:T(8,128)(2,1)}, bf16[784,128]{1,0:T(8,128)(2,1)S(1)}, u32[]{:S(2)}, u32[]{:S(2)}) collective-permute-start(bf16[784,128]{1,0:T(8,128)(2,1)} %shard_map.68.rest_0_.own_ref), channel_id=1, source_target_pairs={{0,4},{1,5},{2,6},{3,7},{4,0},{5,1},{6,2},{7,3},{8,12},{9,13},{10,... | collective-permute-start | bytes 602120 | tf_op jit(solution)/shard_map/ppermute | solution.py:215
  9.7 1.4 %collective-permute-done.6.refs_5_ = bf16[768]{0:T(1024)(128)(2,1)S(1)} collective-permute-done((bf16[768]{0:T(1024)(128)(2,1)}, bf16[768]{0:T(1024)(128)(2,1)S(1)}, u32[]{:S(2)}, u32[]{:S(2)}) %collective-permute-start.6) | collective-permute-done | bytes 1568 | tf_op jit(solution)/shard_map/ppermute | solution.py:215
  11.3 1.5 %collective-permute-done.5.refs_4_ = bf16[768,128]{1,0:T(8,128)(2,1)S(1)} collective-permute-done((bf16[768,128]{1,0:T(8,128)(2,1)}, bf16[768,128]{1,0:T(8,128)(2,1)S(1)}, u32[]{:S(2)}, u32[]{:S(2)}) %collective-permute-start.5) | collective-permute-done | bytes 196640 | tf_op jit(solution)/shard_map/ppermute | solution.py:215
  12.8 1.3 %copy-done.1 = bf16[768,768]{1,0:T(8,128)(2,1)S(1)} copy-done((bf16[768,768]{1,0:T(8,128)(2,1)S(1)}, bf16[768,768]{1,0:T(8,128)(2,1)}, u32[]{:S(2)}) %copy-start.1) | copy-done | bytes 1179672
  14.0 0.9 %copy-done.2 = bf16[768,128]{1,0:T(8,128)(2,1)S(1)} copy-done((bf16[768,128]{1,0:T(8,128)(2,1)S(1)}, bf16[768,128]{1,0:T(8,128)(2,1)}, u32[]{:S(2)}) %copy-start.2) | copy-done | bytes 196632
  15.6 0.8 %shard_map.69 = (bf16[912,768]{1,0:T(8,128)(2,1)S(1)}, bf16[912,768]{1,0:T(8,128)(2,1)S(1)}) custom-call(bf16[768,768]{1,0:T(8,128)(2,1)S(1)} %copy-done.1, bf16[768,128]{1,0:T(8,128)(2,1)S(1)} %copy-done.2, bf16[768]{0:T(1024)(128)(2,1)S(1)} %copy-done.3, bf16[768,768]{1,0:T(8,128)(2,1)S(1)} %collective-permute-done.4.refs_3_, ...), custom_call_target="tpu_custom_call" | custom-call | tf_op jit(solution)/shard_map/pallas_call | solution.py:296
  16.5 1.7 %collective-permute-done.2.refs_0_.rest_0_.rest_4_ = bf16[784,128]{1,0:T(8,128)(2,1)S(1)} collective-permute-done((bf16[784,128]{1,0:T(8,128)(2,1)}, bf16[784,128]{1,0:T(8,128)(2,1)S(1)}, u32[]{:S(2)}, u32[]{:S(2)}) %collective-permute-start.2) | collective-permute-done | bytes 200736 | tf_op jit(solution)/shard_map/ppermute | solution.py:215
  18.4 1.5 %collective-permute-start.7 = (bf16[784,128]{1,0:T(8,128)(2,1)S(1)}, bf16[784,128]{1,0:T(8,128)(2,1)S(1)}, u32[]{:S(2)}, u32[]{:S(2)}) collective-permute-start(bf16[784,128]{1,0:T(8,128)(2,1)S(1)} %shard_map.70), channel_id=1, source_target_pairs={{0,4},{1,5},{2,6},{3,7},{4,0},{5,1},{6,2},{7,3},{8,12},{9,13},{10,... | collective-permute-start | bytes 602120 | tf_op jit(solution)/shard_map/ppermute | solution.py:215
  21.0 4.5 %collective-permute-done.7.rest_1_.rest_6_ = bf16[784,128]{1,0:T(8,128)(2,1)S(1)} collective-permute-done((bf16[784,128]{1,0:T(8,128)(2,1)S(1)}, bf16[784,128]{1,0:T(8,128)(2,1)S(1)}, u32[]{:S(2)}, u32[]{:S(2)}) %collective-permute-start.7) | collective-permute-done | bytes 200736 | tf_op jit(solution)/shard_map/ppermute | solution.py:215
  25.6 1.3 %shard_map.71.rest_4_ = f32[72,128]{1,0:T(8,128)S(1)} custom-call(bf16[784,128]{1,0:T(8,128)(2,1)S(1)} %copy-done, bf16[784,128]{1,0:T(8,128)(2,1)S(1)} %collective-permute-done.refs_1_.rest_1_, bf16[912,768]{1,0:T(8,128)(2,1)S(1)} %get-tuple-element.6.refs_3_.rest_2_, bf16[912,768]{1,0:T(8,128)(2,1)S(1)} %get-tuple-element.7.rest_3_), custom_call_target="tpu_custom_call" | custom-call | flops 805306368 | tf_op jit(solution)/shard_map/pallas_call | solution.py:268
  26.9 1.4 %shard_map.72.rest_4_ = f32[72,128]{1,0:T(8,128)S(1)} custom-call(bf16[784,128]{1,0:T(8,128)(2,1)S(1)} %collective-permute-done.2.refs_0_.rest_0_.rest_4_, bf16[784,128]{1,0:T(8,128)(2,1)S(1)} %collective-permute-done.9.rest_1_.rest_5_, bf16[912,768]{1,0:T(8,128)(2,1)S(1)} %get-tuple-element.6.refs_3_.rest_2_, ...), custom_call_target="tpu_custom_call" | custom-call | flops 805306368 | tf_op jit(solution)/shard_map/pallas_call | solution.py:268
  28.3 1.3 %shard_map.73.rest_4_ = f32[72,128]{1,0:T(8,128)S(1)} custom-call(bf16[784,128]{1,0:T(8,128)(2,1)S(1)} %collective-permute-done.3.refs_2_.rest_0_.rest_2_, bf16[784,128]{1,0:T(8,128)(2,1)S(1)} %collective-permute-done.7.rest_1_.rest_6_, bf16[912,768]{1,0:T(8,128)(2,1)S(1)} %get-tuple-element.6.refs_3_.rest_2_, ...), custom_call_target="tpu_custom_call" | custom-call | flops 805306368 | tf_op jit(solution)/shard_map/pallas_call | solution.py:268
  29.7 1.5 %collective-permute-done.8.rest_1_.rest_7_ = bf16[784,128]{1,0:T(8,128)(2,1)S(1)} collective-permute-done((bf16[784,128]{1,0:T(8,128)(2,1)S(1)}, bf16[784,128]{1,0:T(8,128)(2,1)S(1)}, u32[]{:S(2)}, u32[]{:S(2)}) %collective-permute-start.8) | collective-permute-done | bytes 200736 | tf_op jit(solution)/shard_map/ppermute | solution.py:215
  31.2 1.3 %shard_map.74 = f32[72,128]{1,0:T(8,128)S(1)} custom-call(bf16[784,128]{1,0:T(8,128)(2,1)S(1)} %collective-permute-done.1.rest_0_.rest_3_, bf16[784,128]{1,0:T(8,128)(2,1)S(1)} %collective-permute-done.8.rest_1_.rest_7_, bf16[912,768]{1,0:T(8,128)(2,1)S(1)} %get-tuple-element.6.refs_3_.rest_2_, bf16[912,768]{1,0:T(8,128)(2,1)S(1)} %get-tuple-element.7.rest_3_, ...), custom_call_target="tpu_custom_call" | custom-call | flops 805306368 | tf_op jit(solution)/shard_map/pallas_call | solution.py:268
  33.0 3.5 %collective-permute-done.10 = f32[72,128]{1,0:T(8,128)S(1)} collective-permute-done((f32[72,128]{1,0:T(8,128)S(1)}, f32[72,128]{1,0:T(8,128)S(1)}, u32[]{:S(2)}, u32[]{:S(2)}) %collective-permute-start.10) | collective-permute-done | bytes 36896 | tf_op jit(solution)/shard_map/ppermute | solution.py:215
  36.6 2.3 %collective-permute-start.11 = (f32[72,128]{1,0:T(8,128)S(1)}, f32[72,128]{1,0:T(8,128)S(1)}, u32[]{:S(2)}, u32[]{:S(2)}) collective-permute-start(f32[72,128]{1,0:T(8,128)S(1)} %add.9), channel_id=1, source_target_pairs={{0,4},{1,5},{2,6},{3,7},{4,0},{5,1},{6,2},{7,3},{8,12},{9,13},{10,... | collective-permute-start | bytes 110600 | tf_op jit(solution)/shard_map/ppermute | solution.py:215
  38.9 1.9 %collective-permute-done.11 = f32[72,128]{1,0:T(8,128)S(1)} collective-permute-done((f32[72,128]{1,0:T(8,128)S(1)}, f32[72,128]{1,0:T(8,128)S(1)}, u32[]{:S(2)}, u32[]{:S(2)}) %collective-permute-start.11) | collective-permute-done | bytes 36896 | tf_op jit(solution)/shard_map/ppermute | solution.py:215
  40.9 2.3 %collective-permute-start.12 = (f32[72,128]{1,0:T(8,128)S(1)}, f32[72,128]{1,0:T(8,128)S(1)}, u32[]{:S(2)}, u32[]{:S(2)}) collective-permute-start(f32[72,128]{1,0:T(8,128)S(1)} %add.10), channel_id=1, source_target_pairs={{0,8},{1,9},{2,10},{3,11},{4,12},{5,13},{6,14},{7,15},{8,0},{9,1},... | collective-permute-start | bytes 110600 | tf_op jit(solution)/shard_map/ppermute | solution.py:215
  43.2 1.8 %shard_map.75 = f32[16,128]{1,0:T(8,128)S(1)} custom-call(bf16[784,128]{1,0:T(8,128)(2,1)S(1)} %copy-done, bf16[784,128]{1,0:T(8,128)(2,1)S(1)} %collective-permute-done.14.sib_ref, bf16[784,128]{1,0:T(8,128)(2,1)S(1)} %copy-done, bf16[784,128]{1,0:T(8,128)(2,1)S(1)} %collective-permute-done.refs_1_.rest_1_, ...), custom_call_target="tpu_custom_call" | custom-call | flops 536870912 | tf_op jit(solution)/shard_map/pallas_call | solution.py:280
  46.2 0.8 %collective-permute-done.15.theirs_ref = f32[8,128]{1,0:T(8,128)S(1)} collective-permute-done((f32[8,128]{1,0:T(8,128)S(1)}, f32[8,128]{1,0:T(8,128)S(1)}, u32[]{:S(2)}, u32[]{:S(2)}) %collective-permute-start.15) | collective-permute-done | bytes 4128 | tf_op jit(solution)/shard_map/ppermute | solution.py:215
  47.1 0.8 %shard_map.76 = (f32[8]{0:T(128)}, f32[8,128]{1,0:T(8,128)}) custom-call(f32[72,128]{1,0:T(8,128)S(1)} %add.11.q_ref, f32[72,128]{1,0:T(8,128)S(1)} %collective-permute-done.13.other_ref, f32[8,128]{1,0:T(8,128)S(1)} %get-tuple-element.11.mine_ref, f32[8,128]{1,0:T(8,128)S(1)} %collective-permute-done.15.theirs_ref), custom_call_target="tpu_custom_call" | custom-call | tf_op jit(solution)/shard_map/pallas_call | solution.py:321
  (29 shorter events, 4.5 us)
Async XLA Ops:
  0.6 12.1 %collective-permute-start.4 = (bf16[768,768]{1,0:T(8,128)(2,1)}, bf16[768,768]{1,0:T(8,128)(2,1)S(1)}, u32[]{:S(2)}, u32[]{:S(2)}) collective-permute-start(bf16[768,768]{1,0:T(8,128)(2,1)} %refs_0_.1), channel_id=1, source_target_pairs={{0,1},{1,0},{2,3},{3,2},{4,5},{5,4},{6,7},{7,6},{8,9},{9,8},{10,11... | collective-permute-start | bytes 3538952 | tf_op jit(solution)/shard_map/ppermute | solution.py:215
  3.0 13.5 %collective-permute-start = (bf16[784,128]{1,0:T(8,128)(2,1)}, bf16[784,128]{1,0:T(8,128)(2,1)S(1)}, u32[]{:S(2)}, u32[]{:S(2)}) collective-permute-start(bf16[784,128]{1,0:T(8,128)(2,1)} %shard_map.68.rest_0_.own_ref), channel_id=1, source_target_pairs={{0,2},{1,3},{2,0},{3,1},{4,6},{5,7},{6,4},{7,5},{8,10},{9,11},{10,... | collective-permute-start | bytes 602120 | tf_op jit(solution)/shard_map/ppermute | solution.py:215
  5.6 12.6 %collective-permute-start.2 = (bf16[784,128]{1,0:T(8,128)(2,1)}, bf16[784,128]{1,0:T(8,128)(2,1)S(1)}, u32[]{:S(2)}, u32[]{:S(2)}) collective-permute-start(bf16[784,128]{1,0:T(8,128)(2,1)} %shard_map.68.rest_0_.own_ref), channel_id=1, source_target_pairs={{0,8},{1,9},{2,10},{3,11},{4,12},{5,13},{6,14},{7,15},{8,0},{9,1},... | collective-permute-start | bytes 602120 | tf_op jit(solution)/shard_map/ppermute | solution.py:215
  8.2 10.2 %collective-permute-start.3 = (bf16[784,128]{1,0:T(8,128)(2,1)}, bf16[784,128]{1,0:T(8,128)(2,1)S(1)}, u32[]{:S(2)}, u32[]{:S(2)}) collective-permute-start(bf16[784,128]{1,0:T(8,128)(2,1)} %shard_map.68.rest_0_.own_ref), channel_id=1, source_target_pairs={{0,4},{1,5},{2,6},{3,7},{4,0},{5,1},{6,2},{7,3},{8,12},{9,13},{10,... | collective-permute-start | bytes 602120 | tf_op jit(solution)/shard_map/ppermute | solution.py:215
  9.7 1.4 %collective-permute-start.6 = (bf16[768]{0:T(1024)(128)(2,1)}, bf16[768]{0:T(1024)(128)(2,1)S(1)}, u32[]{:S(2)}, u32[]{:S(2)}) collective-permute-start(bf16[768]{0:T(1024)(128)(2,1)} %refs_2_.1), channel_id=1, source_target_pairs={{0,1},{1,0},{2,3},{3,2},{4,5},{5,4},{6,7},{7,6},{8,9},{9,8},{10,11... | collective-permute-start | bytes 4616 | tf_op jit(solution)/shard_map/ppermute | solution.py:215
  11.1 1.7 %collective-permute-start.5 = (bf16[768,128]{1,0:T(8,128)(2,1)}, bf16[768,128]{1,0:T(8,128)(2,1)S(1)}, u32[]{:S(2)}, u32[]{:S(2)}) collective-permute-start(bf16[768,128]{1,0:T(8,128)(2,1)} %refs_1_.1), channel_id=1, source_target_pairs={{0,1},{1,0},{2,3},{3,2},{4,5},{5,4},{6,7},{7,6},{8,9},{9,8},{10,11... | collective-permute-start | bytes 589832 | tf_op jit(solution)/shard_map/ppermute | solution.py:215
  12.8 1.3 %copy-start.1 = (bf16[768,768]{1,0:T(8,128)(2,1)S(1)}, bf16[768,768]{1,0:T(8,128)(2,1)}, u32[]{:S(2)}) copy-start(bf16[768,768]{1,0:T(8,128)(2,1)} %refs_0_.1) | copy-start | bytes 3538948
  14.0 0.9 %copy-start.2 = (bf16[768,128]{1,0:T(8,128)(2,1)S(1)}, bf16[768,128]{1,0:T(8,128)(2,1)}, u32[]{:S(2)}) copy-start(bf16[768,128]{1,0:T(8,128)(2,1)} %refs_1_.1) | copy-start | bytes 589828
  15.0 0.7 %copy-start.3 = (bf16[768]{0:T(1024)(128)(2,1)S(1)}, bf16[768]{0:T(1024)(128)(2,1)}, u32[]{:S(2)}) copy-start(bf16[768]{0:T(1024)(128)(2,1)} %refs_2_.1) | copy-start | bytes 4612
  16.4 4.0 %copy-start = (bf16[784,128]{1,0:T(8,128)(2,1)S(1)}, bf16[784,128]{1,0:T(8,128)(2,1)}, u32[]{:S(2)}) copy-start(bf16[784,128]{1,0:T(8,128)(2,1)} %shard_map.68.rest_0_.own_ref) | copy-start | bytes 602116
  18.4 7.1 %collective-permute-start.7 = (bf16[784,128]{1,0:T(8,128)(2,1)S(1)}, bf16[784,128]{1,0:T(8,128)(2,1)S(1)}, u32[]{:S(2)}, u32[]{:S(2)}) collective-permute-start(bf16[784,128]{1,0:T(8,128)(2,1)S(1)} %shard_map.70), channel_id=1, source_target_pairs={{0,4},{1,5},{2,6},{3,7},{4,0},{5,1},{6,2},{7,3},{8,12},{9,13},{10,... | collective-permute-start | bytes 602120 | tf_op jit(solution)/shard_map/ppermute | solution.py:215
  19.9 7.0 %collective-permute-start.9 = (bf16[784,128]{1,0:T(8,128)(2,1)S(1)}, bf16[784,128]{1,0:T(8,128)(2,1)S(1)}, u32[]{:S(2)}, u32[]{:S(2)}) collective-permute-start(bf16[784,128]{1,0:T(8,128)(2,1)S(1)} %shard_map.70), channel_id=1, source_target_pairs={{0,2},{1,3},{2,0},{3,1},{4,6},{5,7},{6,4},{7,5},{8,10},{9,11},{10,... | collective-permute-start | bytes 602120 | tf_op jit(solution)/shard_map/ppermute | solution.py:215
  20.4 22.8 %collective-permute-start.14 = (bf16[784,128]{1,0:T(8,128)(2,1)S(1)}, bf16[784,128]{1,0:T(8,128)(2,1)S(1)}, u32[]{:S(2)}, u32[]{:S(2)}) collective-permute-start(bf16[784,128]{1,0:T(8,128)(2,1)S(1)} %copy-done), channel_id=1, source_target_pairs={{0,1},{1,0},{2,3},{3,2},{4,5},{5,4},{6,7},{7,6},{8,9},{9,8},{10,11... | collective-permute-start | bytes 602120 | tf_op jit(solution)/shard_map/ppermute | solution.py:215
  20.4 9.2 %collective-permute-start.1 = (bf16[784,128]{1,0:T(8,128)(2,1)S(1)}, bf16[784,128]{1,0:T(8,128)(2,1)S(1)}, u32[]{:S(2)}, u32[]{:S(2)}) collective-permute-start(bf16[784,128]{1,0:T(8,128)(2,1)S(1)} %collective-permute-done.refs_1_.rest_1_), channel_id=1, source_target_pairs={{0,4},{1,5},{2,6},{3,7},{4,0},{5,1},{6,2},{7,3},{8,12},{9,13},{10,... | collective-permute-start | bytes 602120 | tf_op jit(solution)/shard_map/ppermute | solution.py:215
  25.5 5.7 %collective-permute-start.8 = (bf16[784,128]{1,0:T(8,128)(2,1)S(1)}, bf16[784,128]{1,0:T(8,128)(2,1)S(1)}, u32[]{:S(2)}, u32[]{:S(2)}) collective-permute-start(bf16[784,128]{1,0:T(8,128)(2,1)S(1)} %collective-permute-done.7.rest_1_.rest_6_), channel_id=1, source_target_pairs={{0,2},{1,3},{2,0},{3,1},{4,6},{5,7},{6,4},{7,5},{8,10},{9,11},{10,... | collective-permute-start | bytes 602120 | tf_op jit(solution)/shard_map/ppermute | solution.py:215
  32.5 4.0 %collective-permute-start.10 = (f32[72,128]{1,0:T(8,128)S(1)}, f32[72,128]{1,0:T(8,128)S(1)}, u32[]{:S(2)}, u32[]{:S(2)}) collective-permute-start(f32[72,128]{1,0:T(8,128)S(1)} %shard_map.74), channel_id=1, source_target_pairs={{0,2},{1,3},{2,0},{3,1},{4,6},{5,7},{6,4},{7,5},{8,10},{9,11},{10,... | collective-permute-start | bytes 110600 | tf_op jit(solution)/shard_map/ppermute | solution.py:215
  36.6 4.3 %collective-permute-start.11 = (f32[72,128]{1,0:T(8,128)S(1)}, f32[72,128]{1,0:T(8,128)S(1)}, u32[]{:S(2)}, u32[]{:S(2)}) collective-permute-start(f32[72,128]{1,0:T(8,128)S(1)} %add.9), channel_id=1, source_target_pairs={{0,4},{1,5},{2,6},{3,7},{4,0},{5,1},{6,2},{7,3},{8,12},{9,13},{10,... | collective-permute-start | bytes 110600 | tf_op jit(solution)/shard_map/ppermute | solution.py:215
  40.9 4.9 %collective-permute-start.12 = (f32[72,128]{1,0:T(8,128)S(1)}, f32[72,128]{1,0:T(8,128)S(1)}, u32[]{:S(2)}, u32[]{:S(2)}) collective-permute-start(f32[72,128]{1,0:T(8,128)S(1)} %add.10), channel_id=1, source_target_pairs={{0,8},{1,9},{2,10},{3,11},{4,12},{5,13},{6,14},{7,15},{8,0},{9,1},... | collective-permute-start | bytes 110600 | tf_op jit(solution)/shard_map/ppermute | solution.py:215
  45.7 1.3 %collective-permute-start.13 = (f32[72,128]{1,0:T(8,128)S(1)}, f32[72,128]{1,0:T(8,128)S(1)}, u32[]{:S(2)}, u32[]{:S(2)}) collective-permute-start(f32[72,128]{1,0:T(8,128)S(1)} %add.11.q_ref), channel_id=1, source_target_pairs={{0,1},{1,0},{2,3},{3,2},{4,5},{5,4},{6,7},{7,6},{8,9},{9,8},{10,11... | collective-permute-start | bytes 110600 | tf_op jit(solution)/shard_map/ppermute | solution.py:215
  45.8 1.3 %collective-permute-start.15 = (f32[8,128]{1,0:T(8,128)S(1)}, f32[8,128]{1,0:T(8,128)S(1)}, u32[]{:S(2)}, u32[]{:S(2)}) collective-permute-start(f32[8,128]{1,0:T(8,128)S(1)} %get-tuple-element.10), channel_id=1, source_target_pairs={{0,1},{1,0},{2,3},{3,2},{4,5},{5,4},{6,7},{7,6},{8,9},{9,8},{10,11... | collective-permute-start | bytes 12296 | tf_op jit(solution)/shard_map/ppermute | solution.py:215

commit v4 on v3

--- a/solution.py
+++ b/solution.py
@@ -86,12 +86,12 @@
     return (row == ids).astype(jnp.bfloat16)
 
 
-def project(masks, chips, width, rank, first, parts, *rest):
-    refs, (town_ref, tsib_ref, *rest) = rest[: 2 * parts], rest[2 * parts :]
+def project(masks, chips, width, rank, first, cut, parts, *rest):
+    refs, (town_ref, tsib_ref, *rest) = rest[:parts], rest[parts:]
     chip = lax.axis_index("train") // 2
     one, two = (
-        jnp.concatenate([ref[...] for ref in refs[i : i + parts]], axis=0)
-        for i in (0, parts)
+        jnp.concatenate([ref[...] for ref in piece], axis=0)
+        for piece in (refs[:cut], refs[cut:])
     )
     pair = jnp.concatenate([one[:width, :], two[:width, :]], axis=1)
     structs = chips * SPB
@@ -169,8 +169,18 @@
         rest[1][...] = rest[0][...] + total
 
 
-def finish(q_ref, other_ref, mine_ref, theirs_ref, mean_ref, cov_ref, all_ref):
-    structs = q_ref.shape[0] - SPB
+def last_sum(q_ref, more_ref, prior_ref, out_ref):
+    rows = q_ref.shape[0]
+    out_ref[:rows, :] = q_ref[...] + more_ref[...]
+    for i in range(prior_ref.shape[1] // LANES):
+        out_ref[rows + i * SPB : rows + (i + 1) * SPB, :] = prior_ref[
+            SPB:, i * LANES : (i + 1) * LANES
+        ]
+
+
+def finish(q_ref, other_ref, prior_ref, mean_ref, cov_ref, all_ref):
+    wide = prior_ref.shape[1]
+    structs = wide // 2
     me = lax.axis_index("train")
     chip, core = me // 2, me % 2
     for p in range(structs // SPB):
@@ -184,10 +194,14 @@
     square = sum(
         product(a, b, ((1,), (1,))) for i, a in enumerate(own) for b in every[: 3 - i]
     )
-    cov_ref[...] = mine_ref[...] + theirs_ref[...] - square
+    start = structs + SPB
+    theirs = [
+        other_ref[start + i * SPB : start + (i + 1) * SPB, :] for i in range(wide // LANES)
+    ]
+    cov_ref[...] = prior_ref[:SPB, :] + jnp.concatenate(theirs, axis=1) - square
     lane = lax.broadcasted_iota(jnp.int32, (SPB, LANES), 1)
     row = lax.broadcasted_iota(jnp.int32, (SPB, LANES), 0)
-    means = q_ref[structs:, :]
+    means = q_ref[structs:start, :]
     column = jnp.sum(jnp.where(lane == chip, means, 0.0), axis=1, keepdims=True)
     mean_ref[...] = jnp.sum(jnp.where(lane == row, column, 0.0), axis=0)[:SPB]
 
@@ -249,6 +263,21 @@
             compiler_params=pltpu.CompilerParams(vmem_limit_bytes=24 * 2**20),
         )(*others, value)
 
+    def again_pieces(value, pieces, *others):
+        shapes = [
+            jax.ShapeDtypeStruct((piece, value.shape[1]), value.dtype) for piece in pieces
+        ]
+        def kernel(*refs):
+            refs[1 + len(others)][...] = refs[0][...]
+            copy_after(refs[0], None, *refs[2 + len(others) :])
+        return pl.pallas_call(
+            kernel,
+            out_shape=[block_shape, *shapes],
+            in_specs=[VMEM] + [pl.BlockSpec(memory_space=pl.ANY)] * len(others),
+            out_specs=[VMEM] * (1 + len(shapes)),
+            compiler_params=pltpu.CompilerParams(vmem_limit_bytes=24 * 2**20),
+        )(value, *others)
+
     def again_first(value, *others):
         return pl.pallas_call(
             lambda *refs: copy_after(refs[0], None, refs[-1]),
@@ -261,10 +290,12 @@
     q_shape = jax.ShapeDtypeStruct((structs + SPB, rank), jnp.float32)
     prior_shape = jax.ShapeDtypeStruct((2 * SPB, 2 * structs), jnp.float32)
 
-    def add_projection(masks, state, *pair):
+    def add_projection(masks, state, one, two):
         state = () if state is None else (state,)
-        parts = len(pair) // 2
-        kernel = functools.partial(project, masks, chips, width, rank, not state, parts)
+        pair = (*one, *two)
+        kernel = functools.partial(
+            project, masks, chips, width, rank, not state, len(one), len(pair)
+        )
         return call(
             kernel,
             q_shape,
@@ -286,7 +317,7 @@
 
     blocks = {0: own}
     if size == 16:
-        for mask in (4, 1, 2):
+        for mask in (2, 4, 1):
             blocks[mask] = swap(own, 2 * mask)
     else:
         for mask in range(1, chips):
@@ -297,36 +328,38 @@
         *train, *[swap(value, 1) for value in train]
     )
     if size == 16:
-        far = again_first(blocks[4], blocks[1], blocks[2], train_own)
+        far = again_first(blocks[4], blocks[2], train_own)
         blocks[6] = swap(far, 4)
         blocks[5] = swap(far, 2)
         blocks[3] = swap(blocks[1], 4)
         blocks[7] = swap(blocks[6], 2)
+        groups = ((0, 1), (2, 4), (5, 6), (3, 7))
+    else:
+        groups = [(m, m + 1) for m in range(0, chips, 2)]
     blocks = {m: b if isinstance(b, (tuple, list)) else (b,) for m, b in blocks.items()}
+    q = None
+    for one, two in groups:
+        q = add_projection((one, two), q, blocks[one], blocks[two])
     sib = swap(own, 1)
-    q = prior = None
-    groups = [(m, m + 1) for m in range(0, chips, 2)]
-    if size == 16:
-        groups = [(0, 1), (4, 5), (2, 6), (3, 7)]
-    for masks in groups:
-        q = add_projection(masks, q, *blocks[masks[0]], *blocks[masks[1]])
     prior = add_prior(tuple(range(chips)), None, *[blocks[m] for m in range(chips)])
 
-    theirs = swap(prior[SPB:], 1)
     mask = 2
-    while mask < size:
+    while mask < size // 2:
         q = q + swap(q, mask)
         mask *= 2
-    other = swap(q, 1)
+    tail = structs + SPB + 2 * structs // LANES * SPB
+    q = call(last_sum, jax.ShapeDtypeStruct((tail, rank), jnp.float32), 3)(
+        q, swap(q, mask), prior
+    )
     mean, covariance = call(
         finish,
         (
             jax.ShapeDtypeStruct((SPB,), jnp.float32),
             jax.ShapeDtypeStruct((SPB, 2 * structs), jnp.float32),
         ),
-        4,
+        3,
         scratch=[pltpu.VMEM((2 * structs, rank), jnp.float32)],
-    )(q, other, prior[:SPB], theirs)
+    )(q, swap(q, 1), prior)
     return mean, covariance[None]
 
 

time: 48.1 us -> 47 us (0.977)
  waiting for transfers between devices: 17.8 us -> 13 us
  starting transfers between devices: 15.8 us -> 19.4 us
    ppermute x16 -> x15, waiting for transfers between devices: 17.8 us -> 13 us  [swap(): return lax.ppermute(value, 'train', [(i, i ^ mask) for i in range(size)])]
    ppermute x16 -> x15, starting transfers between devices: 15.8 us -> 19.4 us  [swap(): return lax.ppermute(value, 'train', [(i, i ^ mask) for i in range(size)])]
  transfers between devices with their start and end apart: 16 -> 15, of which waited for: 10 -> 8; matrix products, arithmetic and copies ran while one was open for 0% -> 0% of each run, Pallas kernels for 21% -> 21%
where the time goes in v4:
time: 47 us; the launch traced here: 46.7 us
  starting transfers between devices  19.4 us (41%)
  waiting for transfers between devices  13 us (28%)
  Pallas kernels  10.8 us (23%)
  local copies, waits for them, and re-layouts  2.88 us (6%)
  between operations  0.73 us (2%)
    ppermute x15, starting transfers between devices, swap(): return lax.ppermute(value, 'train', [(i, i ^ mask) for i in range(size)])  19.4 us
    ppermute x15, waiting for transfers between devices, swap(): return lax.ppermute(value, 'train', [(i, i ^ mask) for i in range(size)])  13 us
    pallas_call x4, Pallas kernels, add_projection(): call(kernel, q_shape, 2 + len(pair) + len(state), flops=2 * 2 * rows * 2...  5.4 us
    unnamed x8, local copies, waits for them, and re-layouts  2.88 us
    pallas_call x1, Pallas kernels, add_prior(): call(kernel, prior_shape, 2 + len(refs) + len(state), flops=2 * 2 * rows...  1.84 us
    pallas_call x1, Pallas kernels, body(): pl.pallas_call(pack_cand, out_shape=block_shape, in_specs=[HBM, HBM], out...  1.83 us
  transfers between devices with their start and end apart: 15, of which 8 were waited for; matrix products, arithmetic and copies ran while one was open for 0% of the time, Pallas kernels for 21%

profile of v4, /device:TPU:0, one launch (start us, length us, event | category | flops | bytes accessed | tf_op | source)
XLA Modules:
  0.0 46.7 jit_solution(14027192433752333594)
XLA Ops:
  1.1 1.8 %shard_map.68.rest_0_.own_ref = bf16[784,128]{1,0:T(8,128)(2,1)} custom-call(bf16[128,768]{1,0:T(8,128)(2,1)} %cand_ref.1, s32[1,128]{1,0:T(1,128)} %bitcast.2), custom_call_target="tpu_custom_call" | custom-call | tf_op jit(solution)/shard_map/pallas_call | solution.py:232
  3.0 3.7 %collective-permute-start.2 = (bf16[784,128]{1,0:T(8,128)(2,1)}, bf16[784,128]{1,0:T(8,128)(2,1)S(1)}, u32[]{:S(2)}, u32[]{:S(2)}) collective-permute-start(bf16[784,128]{1,0:T(8,128)(2,1)} %shard_map.68.rest_0_.own_ref), channel_id=1, source_target_pairs={{0,8},{1,9},{2,10},{3,11},{4,12},{5,13},{6,14},{7,15},{8,0},{9,1},... | collective-permute-start | bytes 602120 | tf_op jit(solution)/shard_map/ppermute | solution.py:229
  6.7 1.6 %collective-permute-start.3 = (bf16[784,128]{1,0:T(8,128)(2,1)}, bf16[784,128]{1,0:T(8,128)(2,1)S(1)}, u32[]{:S(2)}, u32[]{:S(2)}) collective-permute-start(bf16[784,128]{1,0:T(8,128)(2,1)} %shard_map.68.rest_0_.own_ref), channel_id=1, source_target_pairs={{0,4},{1,5},{2,6},{3,7},{4,0},{5,1},{6,2},{7,3},{8,12},{9,13},{10,... | collective-permute-start | bytes 602120 | tf_op jit(solution)/shard_map/ppermute | solution.py:229
  8.7 1.1 %collective-permute-done.6.refs_5_ = bf16[768]{0:T(1024)(128)(2,1)S(1)} collective-permute-done((bf16[768]{0:T(1024)(128)(2,1)}, bf16[768]{0:T(1024)(128)(2,1)S(1)}, u32[]{:S(2)}, u32[]{:S(2)}) %collective-permute-start.6) | collective-permute-done | bytes 1568 | tf_op jit(solution)/shard_map/ppermute | solution.py:229
  9.9 1.5 %collective-permute-start = (bf16[784,128]{1,0:T(8,128)(2,1)}, bf16[784,128]{1,0:T(8,128)(2,1)S(1)}, u32[]{:S(2)}, u32[]{:S(2)}) collective-permute-start(bf16[784,128]{1,0:T(8,128)(2,1)} %shard_map.68.rest_0_.own_ref), channel_id=1, source_target_pairs={{0,2},{1,3},{2,0},{3,1},{4,6},{5,7},{6,4},{7,5},{8,10},{9,11},{10,... | collective-permute-start | bytes 602120 | tf_op jit(solution)/shard_map/ppermute | solution.py:229
  11.4 1.3 %copy-done.1 = bf16[768,768]{1,0:T(8,128)(2,1)S(1)} copy-done((bf16[768,768]{1,0:T(8,128)(2,1)S(1)}, bf16[768,768]{1,0:T(8,128)(2,1)}, u32[]{:S(2)}) %copy-start.1) | copy-done | bytes 1179672
  12.7 0.9 %copy-done.2 = bf16[768,128]{1,0:T(8,128)(2,1)S(1)} copy-done((bf16[768,128]{1,0:T(8,128)(2,1)S(1)}, bf16[768,128]{1,0:T(8,128)(2,1)}, u32[]{:S(2)}) %copy-start.2) | copy-done | bytes 196632
  14.3 0.8 %shard_map.69 = (bf16[912,768]{1,0:T(8,128)(2,1)S(1)}, bf16[912,768]{1,0:T(8,128)(2,1)S(1)}) custom-call(bf16[768,768]{1,0:T(8,128)(2,1)S(1)} %copy-done.1, bf16[768,128]{1,0:T(8,128)(2,1)S(1)} %copy-done.2, bf16[768]{0:T(1024)(128)(2,1)S(1)} %copy-done.3, bf16[768,768]{1,0:T(8,128)(2,1)S(1)} %collective-permute-done.4.refs_3_, ...), custom_call_target="tpu_custom_call" | custom-call | tf_op jit(solution)/shard_map/pallas_call | solution.py:327
  15.1 1.8 %collective-permute-done.2.refs_0_.rest_1_.rest_4_ = bf16[784,128]{1,0:T(8,128)(2,1)S(1)} collective-permute-done((bf16[784,128]{1,0:T(8,128)(2,1)}, bf16[784,128]{1,0:T(8,128)(2,1)S(1)}, u32[]{:S(2)}, u32[]{:S(2)}) %collective-permute-start.2) | collective-permute-done | bytes 200736 | tf_op jit(solution)/shard_map/ppermute | solution.py:229
  17.1 1.6 %collective-permute-start.7 = (bf16[784,128]{1,0:T(8,128)(2,1)S(1)}, bf16[784,128]{1,0:T(8,128)(2,1)S(1)}, u32[]{:S(2)}, u32[]{:S(2)}) collective-permute-start(bf16[784,128]{1,0:T(8,128)(2,1)S(1)} %shard_map.70), channel_id=1, source_target_pairs={{0,4},{1,5},{2,6},{3,7},{4,0},{5,1},{6,2},{7,3},{8,12},{9,13},{10,... | collective-permute-start | bytes 602120 | tf_op jit(solution)/shard_map/ppermute | solution.py:229
  18.7 1.5 %collective-permute-start.9 = (bf16[784,128]{1,0:T(8,128)(2,1)S(1)}, bf16[784,128]{1,0:T(8,128)(2,1)S(1)}, u32[]{:S(2)}, u32[]{:S(2)}) collective-permute-start(bf16[784,128]{1,0:T(8,128)(2,1)S(1)} %shard_map.70), channel_id=1, source_target_pairs={{0,2},{1,3},{2,0},{3,1},{4,6},{5,7},{6,4},{7,5},{8,10},{9,11},{10,... | collective-permute-start | bytes 602120 | tf_op jit(solution)/shard_map/ppermute | solution.py:229
  20.8 3.3 %collective-permute-done.7.rest_1_.rest_6_ = bf16[784,128]{1,0:T(8,128)(2,1)S(1)} collective-permute-done((bf16[784,128]{1,0:T(8,128)(2,1)S(1)}, bf16[784,128]{1,0:T(8,128)(2,1)S(1)}, u32[]{:S(2)}, u32[]{:S(2)}) %collective-permute-start.7) | collective-permute-done | bytes 200736 | tf_op jit(solution)/shard_map/ppermute | solution.py:229
  24.2 2.1 %collective-permute-start.8 = (bf16[784,128]{1,0:T(8,128)(2,1)S(1)}, bf16[784,128]{1,0:T(8,128)(2,1)S(1)}, u32[]{:S(2)}, u32[]{:S(2)}) collective-permute-start(bf16[784,128]{1,0:T(8,128)(2,1)S(1)} %collective-permute-done.7.rest_1_.rest_6_), channel_id=1, source_target_pairs={{0,2},{1,3},{2,0},{3,1},{4,6},{5,7},{6,4},{7,5},{8,10},{9,11},{10,... | collective-permute-start | bytes 602120 | tf_op jit(solution)/shard_map/ppermute | solution.py:229
  26.3 1.3 %shard_map.71.rest_4_ = f32[72,128]{1,0:T(8,128)S(1)} custom-call(bf16[784,128]{1,0:T(8,128)(2,1)S(1)} %copy-done, bf16[784,128]{1,0:T(8,128)(2,1)S(1)} %collective-permute-done.rest_1_, bf16[912,768]{1,0:T(8,128)(2,1)S(1)} %get-tuple-element.6.refs_2_.rest_2_, bf16[912,768]{1,0:T(8,128)(2,1)S(1)} %get-tuple-element.7.rest_3_), custom_call_target="tpu_custom_call" | custom-call | flops 805306368 | tf_op jit(solution)/shard_map/pallas_call | solution.py:299
  27.7 1.4 %shard_map.72.rest_4_ = f32[72,128]{1,0:T(8,128)S(1)} custom-call(bf16[784,128]{1,0:T(8,128)(2,1)S(1)} %collective-permute-done.3.refs_1_.rest_0_.rest_2_, bf16[784,128]{1,0:T(8,128)(2,1)S(1)} %collective-permute-done.2.refs_0_.rest_1_.rest_4_, bf16[912,768]{1,0:T(8,128)(2,1)S(1)} %get-tuple-element.6.refs_2_.rest_2_, ...), custom_call_target="tpu_custom_call" | custom-call | flops 805306368 | tf_op jit(solution)/shard_map/pallas_call | solution.py:299
  29.0 1.4 %shard_map.73.rest_4_ = f32[72,128]{1,0:T(8,128)S(1)} custom-call(bf16[784,128]{1,0:T(8,128)(2,1)S(1)} %collective-permute-done.9.rest_0_.rest_5_, bf16[784,128]{1,0:T(8,128)(2,1)S(1)} %collective-permute-done.7.rest_1_.rest_6_, bf16[912,768]{1,0:T(8,128)(2,1)S(1)} %get-tuple-element.6.refs_2_.rest_2_, bf16[912,768]{1,0:T(8,128)(2,1)S(1)} %get-tuple-element.7.rest_3_, ...), custom_call_target="tpu_custom_call" | custom-call | flops 805306368 | tf_op jit(solution)/shard_map/pallas_call | solution.py:299
  30.4 1.4 %shard_map.74 = f32[72,128]{1,0:T(8,128)S(1)} custom-call(bf16[784,128]{1,0:T(8,128)(2,1)S(1)} %collective-permute-done.1.rest_0_.rest_3_, bf16[784,128]{1,0:T(8,128)(2,1)S(1)} %collective-permute-done.8.rest_1_.rest_7_, bf16[912,768]{1,0:T(8,128)(2,1)S(1)} %get-tuple-element.6.refs_2_.rest_2_, bf16[912,768]{1,0:T(8,128)(2,1)S(1)} %get-tuple-element.7.rest_3_, ...), custom_call_target="tpu_custom_call" | custom-call | flops 805306368 | tf_op jit(solution)/shard_map/pallas_call | solution.py:299
  31.8 1.7 %collective-permute-start.10 = (f32[72,128]{1,0:T(8,128)S(1)}, f32[72,128]{1,0:T(8,128)S(1)}, u32[]{:S(2)}, u32[]{:S(2)}) collective-permute-start(f32[72,128]{1,0:T(8,128)S(1)} %shard_map.74), channel_id=1, source_target_pairs={{0,2},{1,3},{2,0},{3,1},{4,6},{5,7},{6,4},{7,5},{8,10},{9,11},{10,... | collective-permute-start | bytes 110600 | tf_op jit(solution)/shard_map/ppermute | solution.py:229
  33.4 2.3 %collective-permute-done.10 = f32[72,128]{1,0:T(8,128)S(1)} collective-permute-done((f32[72,128]{1,0:T(8,128)S(1)}, f32[72,128]{1,0:T(8,128)S(1)}, u32[]{:S(2)}, u32[]{:S(2)}) %collective-permute-start.10) | collective-permute-done | bytes 36896 | tf_op jit(solution)/shard_map/ppermute | solution.py:229
  35.8 1.9 %collective-permute-start.11 = (f32[72,128]{1,0:T(8,128)S(1)}, f32[72,128]{1,0:T(8,128)S(1)}, u32[]{:S(2)}, u32[]{:S(2)}) collective-permute-start(f32[72,128]{1,0:T(8,128)S(1)} %add.6), channel_id=1, source_target_pairs={{0,4},{1,5},{2,6},{3,7},{4,0},{5,1},{6,2},{7,3},{8,12},{9,13},{10,... | collective-permute-start | bytes 110600 | tf_op jit(solution)/shard_map/ppermute | solution.py:229
  37.7 2.1 %collective-permute-done.11 = f32[72,128]{1,0:T(8,128)S(1)} collective-permute-done((f32[72,128]{1,0:T(8,128)S(1)}, f32[72,128]{1,0:T(8,128)S(1)}, u32[]{:S(2)}, u32[]{:S(2)}) %collective-permute-start.11) | collective-permute-done | bytes 36896 | tf_op jit(solution)/shard_map/ppermute | solution.py:229
  39.8 2.2 %collective-permute-start.12 = (f32[72,128]{1,0:T(8,128)S(1)}, f32[72,128]{1,0:T(8,128)S(1)}, u32[]{:S(2)}, u32[]{:S(2)}) collective-permute-start(f32[72,128]{1,0:T(8,128)S(1)} %add.7.q_ref), channel_id=1, source_target_pairs={{0,8},{1,9},{2,10},{3,11},{4,12},{5,13},{6,14},{7,15},{8,0},{9,1},... | collective-permute-start | bytes 110600 | tf_op jit(solution)/shard_map/ppermute | solution.py:229
  42.0 1.8 %shard_map.75.prior_ref = f32[16,128]{1,0:T(8,128)S(1)} custom-call(bf16[784,128]{1,0:T(8,128)(2,1)S(1)} %copy-done, bf16[784,128]{1,0:T(8,128)(2,1)S(1)} %collective-permute-done.13.sib_ref, bf16[784,128]{1,0:T(8,128)(2,1)S(1)} %copy-done, bf16[784,128]{1,0:T(8,128)(2,1)S(1)} %collective-permute-done.rest_1_, ...), custom_call_target="tpu_custom_call" | custom-call | flops 536870912 | tf_op jit(solution)/shard_map/pallas_call | solution.py:311
  44.7 1.2 %collective-permute-done.14.other_ref = f32[80,128]{1,0:T(8,128)S(1)} collective-permute-done((f32[80,128]{1,0:T(8,128)S(1)}, f32[80,128]{1,0:T(8,128)S(1)}, u32[]{:S(2)}, u32[]{:S(2)}) %collective-permute-start.14) | collective-permute-done | bytes 40992 | tf_op jit(solution)/shard_map/ppermute | solution.py:229
  (26 shorter events, 4.3 us)
Async XLA Ops:
  0.6 10.8 %collective-permute-start.4 = (bf16[768,768]{1,0:T(8,128)(2,1)}, bf16[768,768]{1,0:T(8,128)(2,1)S(1)}, u32[]{:S(2)}, u32[]{:S(2)}) collective-permute-start(bf16[768,768]{1,0:T(8,128)(2,1)} %refs_0_.1), channel_id=1, source_target_pairs={{0,1},{1,0},{2,3},{3,2},{4,5},{5,4},{6,7},{7,6},{8,9},{9,8},{10,11... | collective-permute-start | bytes 3538952 | tf_op jit(solution)/shard_map/ppermute | solution.py:229
  3.0 13.9 %collective-permute-start.2 = (bf16[784,128]{1,0:T(8,128)(2,1)}, bf16[784,128]{1,0:T(8,128)(2,1)S(1)}, u32[]{:S(2)}, u32[]{:S(2)}) collective-permute-start(bf16[784,128]{1,0:T(8,128)(2,1)} %shard_map.68.rest_0_.own_ref), channel_id=1, source_target_pairs={{0,8},{1,9},{2,10},{3,11},{4,12},{5,13},{6,14},{7,15},{8,0},{9,1},... | collective-permute-start | bytes 602120 | tf_op jit(solution)/shard_map/ppermute | solution.py:229
  6.7 10.5 %collective-permute-start.3 = (bf16[784,128]{1,0:T(8,128)(2,1)}, bf16[784,128]{1,0:T(8,128)(2,1)S(1)}, u32[]{:S(2)}, u32[]{:S(2)}) collective-permute-start(bf16[784,128]{1,0:T(8,128)(2,1)} %shard_map.68.rest_0_.own_ref), channel_id=1, source_target_pairs={{0,4},{1,5},{2,6},{3,7},{4,0},{5,1},{6,2},{7,3},{8,12},{9,13},{10,... | collective-permute-start | bytes 602120 | tf_op jit(solution)/shard_map/ppermute | solution.py:229
  8.2 3.1 %collective-permute-start.5 = (bf16[768,128]{1,0:T(8,128)(2,1)}, bf16[768,128]{1,0:T(8,128)(2,1)S(1)}, u32[]{:S(2)}, u32[]{:S(2)}) collective-permute-start(bf16[768,128]{1,0:T(8,128)(2,1)} %refs_1_.1), channel_id=1, source_target_pairs={{0,1},{1,0},{2,3},{3,2},{4,5},{5,4},{6,7},{7,6},{8,9},{9,8},{10,11... | collective-permute-start | bytes 589832 | tf_op jit(solution)/shard_map/ppermute | solution.py:229
  8.2 1.6 %collective-permute-start.6 = (bf16[768]{0:T(1024)(128)(2,1)}, bf16[768]{0:T(1024)(128)(2,1)S(1)}, u32[]{:S(2)}, u32[]{:S(2)}) collective-permute-start(bf16[768]{0:T(1024)(128)(2,1)} %refs_2_.1), channel_id=1, source_target_pairs={{0,1},{1,0},{2,3},{3,2},{4,5},{5,4},{6,7},{7,6},{8,9},{9,8},{10,11... | collective-permute-start | bytes 4616 | tf_op jit(solution)/shard_map/ppermute | solution.py:229
  9.9 10.3 %collective-permute-start = (bf16[784,128]{1,0:T(8,128)(2,1)}, bf16[784,128]{1,0:T(8,128)(2,1)S(1)}, u32[]{:S(2)}, u32[]{:S(2)}) collective-permute-start(bf16[784,128]{1,0:T(8,128)(2,1)} %shard_map.68.rest_0_.own_ref), channel_id=1, source_target_pairs={{0,2},{1,3},{2,0},{3,1},{4,6},{5,7},{6,4},{7,5},{8,10},{9,11},{10,... | collective-permute-start | bytes 602120 | tf_op jit(solution)/shard_map/ppermute | solution.py:229
  11.4 1.3 %copy-start.1 = (bf16[768,768]{1,0:T(8,128)(2,1)S(1)}, bf16[768,768]{1,0:T(8,128)(2,1)}, u32[]{:S(2)}) copy-start(bf16[768,768]{1,0:T(8,128)(2,1)} %refs_0_.1) | copy-start | bytes 3538948
  12.7 0.9 %copy-start.2 = (bf16[768,128]{1,0:T(8,128)(2,1)S(1)}, bf16[768,128]{1,0:T(8,128)(2,1)}, u32[]{:S(2)}) copy-start(bf16[768,128]{1,0:T(8,128)(2,1)} %refs_1_.1) | copy-start | bytes 589828
  13.6 0.7 %copy-start.3 = (bf16[768]{0:T(1024)(128)(2,1)S(1)}, bf16[768]{0:T(1024)(128)(2,1)}, u32[]{:S(2)}) copy-start(bf16[768]{0:T(1024)(128)(2,1)} %refs_2_.1) | copy-start | bytes 4612
  15.1 5.1 %copy-start = (bf16[784,128]{1,0:T(8,128)(2,1)S(1)}, bf16[784,128]{1,0:T(8,128)(2,1)}, u32[]{:S(2)}) copy-start(bf16[784,128]{1,0:T(8,128)(2,1)} %shard_map.68.rest_0_.own_ref) | copy-start | bytes 602116
  17.1 7.0 %collective-permute-start.7 = (bf16[784,128]{1,0:T(8,128)(2,1)S(1)}, bf16[784,128]{1,0:T(8,128)(2,1)S(1)}, u32[]{:S(2)}, u32[]{:S(2)}) collective-permute-start(bf16[784,128]{1,0:T(8,128)(2,1)S(1)} %shard_map.70), channel_id=1, source_target_pairs={{0,4},{1,5},{2,6},{3,7},{4,0},{5,1},{6,2},{7,3},{8,12},{9,13},{10,... | collective-permute-start | bytes 602120 | tf_op jit(solution)/shard_map/ppermute | solution.py:229
  18.7 10.3 %collective-permute-start.9 = (bf16[784,128]{1,0:T(8,128)(2,1)S(1)}, bf16[784,128]{1,0:T(8,128)(2,1)S(1)}, u32[]{:S(2)}, u32[]{:S(2)}) collective-permute-start(bf16[784,128]{1,0:T(8,128)(2,1)S(1)} %shard_map.70), channel_id=1, source_target_pairs={{0,2},{1,3},{2,0},{3,1},{4,6},{5,7},{6,4},{7,5},{8,10},{9,11},{10,... | collective-permute-start | bytes 602120 | tf_op jit(solution)/shard_map/ppermute | solution.py:229
  20.2 21.9 %collective-permute-start.13 = (bf16[784,128]{1,0:T(8,128)(2,1)S(1)}, bf16[784,128]{1,0:T(8,128)(2,1)S(1)}, u32[]{:S(2)}, u32[]{:S(2)}) collective-permute-start(bf16[784,128]{1,0:T(8,128)(2,1)S(1)} %copy-done), channel_id=1, source_target_pairs={{0,1},{1,0},{2,3},{3,2},{4,5},{5,4},{6,7},{7,6},{8,9},{9,8},{10,11... | collective-permute-start | bytes 602120 | tf_op jit(solution)/shard_map/ppermute | solution.py:229
  20.2 10.2 %collective-permute-start.1 = (bf16[784,128]{1,0:T(8,128)(2,1)S(1)}, bf16[784,128]{1,0:T(8,128)(2,1)S(1)}, u32[]{:S(2)}, u32[]{:S(2)}) collective-permute-start(bf16[784,128]{1,0:T(8,128)(2,1)S(1)} %collective-permute-done.rest_1_), channel_id=1, source_target_pairs={{0,4},{1,5},{2,6},{3,7},{4,0},{5,1},{6,2},{7,3},{8,12},{9,13},{10,... | collective-permute-start | bytes 602120 | tf_op jit(solution)/shard_map/ppermute | solution.py:229
  24.2 6.2 %collective-permute-start.8 = (bf16[784,128]{1,0:T(8,128)(2,1)S(1)}, bf16[784,128]{1,0:T(8,128)(2,1)S(1)}, u32[]{:S(2)}, u32[]{:S(2)}) collective-permute-start(bf16[784,128]{1,0:T(8,128)(2,1)S(1)} %collective-permute-done.7.rest_1_.rest_6_), channel_id=1, source_target_pairs={{0,2},{1,3},{2,0},{3,1},{4,6},{5,7},{6,4},{7,5},{8,10},{9,11},{10,... | collective-permute-start | bytes 602120 | tf_op jit(solution)/shard_map/ppermute | solution.py:229
  31.8 4.0 %collective-permute-start.10 = (f32[72,128]{1,0:T(8,128)S(1)}, f32[72,128]{1,0:T(8,128)S(1)}, u32[]{:S(2)}, u32[]{:S(2)}) collective-permute-start(f32[72,128]{1,0:T(8,128)S(1)} %shard_map.74), channel_id=1, source_target_pairs={{0,2},{1,3},{2,0},{3,1},{4,6},{5,7},{6,4},{7,5},{8,10},{9,11},{10,... | collective-permute-start | bytes 110600 | tf_op jit(solution)/shard_map/ppermute | solution.py:229
  35.8 4.0 %collective-permute-start.11 = (f32[72,128]{1,0:T(8,128)S(1)}, f32[72,128]{1,0:T(8,128)S(1)}, u32[]{:S(2)}, u32[]{:S(2)}) collective-permute-start(f32[72,128]{1,0:T(8,128)S(1)} %add.6), channel_id=1, source_target_pairs={{0,4},{1,5},{2,6},{3,7},{4,0},{5,1},{6,2},{7,3},{8,12},{9,13},{10,... | collective-permute-start | bytes 110600 | tf_op jit(solution)/shard_map/ppermute | solution.py:229
  39.8 4.9 %collective-permute-start.12 = (f32[72,128]{1,0:T(8,128)S(1)}, f32[72,128]{1,0:T(8,128)S(1)}, u32[]{:S(2)}, u32[]{:S(2)}) collective-permute-start(f32[72,128]{1,0:T(8,128)S(1)} %add.7.q_ref), channel_id=1, source_target_pairs={{0,8},{1,9},{2,10},{3,11},{4,12},{5,13},{6,14},{7,15},{8,0},{9,1},... | collective-permute-start | bytes 110600 | tf_op jit(solution)/shard_map/ppermute | solution.py:229
  44.7 1.2 %collective-permute-start.14 = (f32[80,128]{1,0:T(8,128)S(1)}, f32[80,128]{1,0:T(8,128)S(1)}, u32[]{:S(2)}, u32[]{:S(2)}) collective-permute-start(f32[80,128]{1,0:T(8,128)S(1)} %shard_map.76.q_ref), channel_id=1, source_target_pairs={{0,1},{1,0},{2,3},{3,2},{4,5},{5,4},{6,7},{7,6},{8,9},{9,8},{10,11... | collective-permute-start | bytes 122888 | tf_op jit(solution)/shard_map/ppermute | solution.py:229

commit v5 on v4

--- a/solution.py
+++ b/solution.py
@@ -48,6 +48,14 @@
         copy.wait()
     out_ref[:width, :] = unit_rows(raw[...]).T
     within = (ids[...] - ids[0, 0]).astype(jnp.float32)
+    out_ref[width:, :] = jnp.broadcast_to(within, (TAIL, rows)).astype(jnp.bfloat16)
+
+
+def pack_here(cand_ref, ids_ref, *rest):
+    out_ref = rest[-1]
+    rows, width = cand_ref.shape
+    out_ref[:width, :] = unit_rows(cand_ref[...]).T
+    within = (ids_ref[...] - ids_ref[0, 0]).astype(jnp.float32)
     out_ref[width:, :] = jnp.broadcast_to(within, (TAIL, rows)).astype(jnp.bfloat16)
 
 
@@ -263,6 +271,15 @@
             compiler_params=pltpu.CompilerParams(vmem_limit_bytes=24 * 2**20),
         )(*others, value)
 
+    def pack_received(mask, *others):
+        return pl.pallas_call(
+            pack_here,
+            out_shape=block_shape,
+            in_specs=[VMEM, VMEM] + [pl.BlockSpec(memory_space=pl.ANY)] * len(others),
+            out_specs=VMEM,
+            compiler_params=pltpu.CompilerParams(vmem_limit_bytes=24 * 2**20),
+        )(swap(cand_desc, mask), swap(struct_id.reshape(1, rows), mask), *others)
+
     def again_pieces(value, pieces, *others):
         shapes = [
             jax.ShapeDtypeStruct((piece, value.shape[1]), value.dtype) for piece in pieces
@@ -317,7 +334,7 @@
 
     blocks = {0: own}
     if size == 16:
-        for mask in (2, 4, 1):
+        for mask in (2, 1):
             blocks[mask] = swap(own, 2 * mask)
     else:
         for mask in range(1, chips):
@@ -328,9 +345,11 @@
         *train, *[swap(value, 1) for value in train]
     )
     if size == 16:
-        far = again_first(blocks[4], blocks[2], train_own)
+        far = pack_received(8, train_own)
+        blocks[4] = far
+        late = again_first(far, blocks[2])
         blocks[6] = swap(far, 4)
-        blocks[5] = swap(far, 2)
+        blocks[5] = swap(late, 2)
         blocks[3] = swap(blocks[1], 4)
         blocks[7] = swap(blocks[6], 2)
         groups = ((0, 1), (2, 4), (5, 6), (3, 7))

time: 47 us -> 45.4 us (0.966)
  starting transfers between devices: 19.4 us -> 15.7 us
  waiting for transfers between devices: 13 us -> 14.8 us
    ppermute x15 -> x16, starting transfers between devices: 19.4 us -> 15.7 us  [swap(): return lax.ppermute(value, 'train', [(i, i ^ mask) for i in range(size)])]
    ppermute x15 -> x16, waiting for transfers between devices: 13 us -> 14.8 us  [swap(): return lax.ppermute(value, 'train', [(i, i ^ mask) for i in range(size)])]
  transfers between devices with their start and end apart: 15 -> 16, of which waited for: 8 -> 8; matrix products, arithmetic and copies ran while one was open for 0% -> 0% of each run, Pallas kernels for 21% -> 23%
where the time goes in v5:
time: 45.4 us; the launch traced here: 45.2 us
  starting transfers between devices  15.7 us (35%)
  waiting for transfers between devices  14.8 us (33%)
  Pallas kernels  11 us (24%)
  local copies, waits for them, and re-layouts  2.88 us (6%)
  between operations  0.75 us (2%)
    ppermute x16, starting transfers between devices, swap(): return lax.ppermute(value, 'train', [(i, i ^ mask) for i in range(size)])  15.7 us
    ppermute x16, waiting for transfers between devices, swap(): return lax.ppermute(value, 'train', [(i, i ^ mask) for i in range(size)])  14.8 us
    pallas_call x4, Pallas kernels, add_projection(): call(kernel, q_shape, 2 + len(pair) + len(state), flops=2 * 2 * rows * 2...  5.4 us
    unnamed x8, local copies, waits for them, and re-layouts  2.88 us
    pallas_call x1, Pallas kernels, body(): pl.pallas_call(pack_cand, out_shape=block_shape, in_specs=[HBM, HBM], out...  1.86 us
    pallas_call x1, Pallas kernels, add_prior(): call(kernel, prior_shape, 2 + len(refs) + len(state), flops=2 * 2 * rows...  1.84 us
  transfers between devices with their start and end apart: 16, of which 8 were waited for; matrix products, arithmetic and copies ran while one was open for 0% of the time, Pallas kernels for 23%

profile of v5, /device:TPU:0, one launch (start us, length us, event | category | flops | bytes accessed | tf_op | source)
XLA Modules:
  0.0 45.2 jit_solution(18356730148202557665)
XLA Ops:
  1.2 4.0 %collective-permute-start.2 = (bf16[128,768]{1,0:T(8,128)(2,1)}, bf16[128,768]{1,0:T(8,128)(2,1)S(1)}, u32[]{:S(2)}, u32[]{:S(2)}) collective-permute-start(bf16[128,768]{1,0:T(8,128)(2,1)} %cand_ref.1), channel_id=1, source_target_pairs={{0,8},{1,9},{2,10},{3,11},{4,12},{5,13},{6,14},{7,15},{8,0},{9,1},... | collective-permute-start | bytes 589832 | tf_op jit(solution)/shard_map/ppermute | solution.py:237
  5.2 1.9 %shard_map.68.rest_0_.own_ref = bf16[784,128]{1,0:T(8,128)(2,1)} custom-call(bf16[128,768]{1,0:T(8,128)(2,1)} %cand_ref.1, s32[1,128]{1,0:T(1,128)} %bitcast.2), custom_call_target="tpu_custom_call" | custom-call | tf_op jit(solution)/shard_map/pallas_call | solution.py:240
  7.1 1.6 %collective-permute-start.9 = (bf16[784,128]{1,0:T(8,128)(2,1)}, bf16[784,128]{1,0:T(8,128)(2,1)S(1)}, u32[]{:S(2)}, u32[]{:S(2)}) collective-permute-start(bf16[784,128]{1,0:T(8,128)(2,1)} %shard_map.68.rest_0_.own_ref), channel_id=1, source_target_pairs={{0,4},{1,5},{2,6},{3,7},{4,0},{5,1},{6,2},{7,3},{8,12},{9,13},{10,... | collective-permute-start | bytes 602120 | tf_op jit(solution)/shard_map/ppermute | solution.py:237
  8.8 1.4 %collective-permute-done.6.refs_5_ = bf16[768]{0:T(1024)(128)(2,1)S(1)} collective-permute-done((bf16[768]{0:T(1024)(128)(2,1)}, bf16[768]{0:T(1024)(128)(2,1)S(1)}, u32[]{:S(2)}, u32[]{:S(2)}) %collective-permute-start.6) | collective-permute-done | bytes 1568 | tf_op jit(solution)/shard_map/ppermute | solution.py:237
  10.5 1.5 %collective-permute-start = (bf16[784,128]{1,0:T(8,128)(2,1)}, bf16[784,128]{1,0:T(8,128)(2,1)S(1)}, u32[]{:S(2)}, u32[]{:S(2)}) collective-permute-start(bf16[784,128]{1,0:T(8,128)(2,1)} %shard_map.68.rest_0_.own_ref), channel_id=1, source_target_pairs={{0,2},{1,3},{2,0},{3,1},{4,6},{5,7},{6,4},{7,5},{8,10},{9,11},{10,... | collective-permute-start | bytes 602120 | tf_op jit(solution)/shard_map/ppermute | solution.py:237
  12.0 1.3 %copy-done.1 = bf16[768,768]{1,0:T(8,128)(2,1)S(1)} copy-done((bf16[768,768]{1,0:T(8,128)(2,1)S(1)}, bf16[768,768]{1,0:T(8,128)(2,1)}, u32[]{:S(2)}) %copy-start.1) | copy-done | bytes 1179672
  13.2 0.9 %copy-done.2 = bf16[768,128]{1,0:T(8,128)(2,1)S(1)} copy-done((bf16[768,128]{1,0:T(8,128)(2,1)S(1)}, bf16[768,128]{1,0:T(8,128)(2,1)}, u32[]{:S(2)}) %copy-start.2) | copy-done | bytes 196632
  14.2 0.7 %copy-done.3 = bf16[768]{0:T(1024)(128)(2,1)S(1)} copy-done((bf16[768]{0:T(1024)(128)(2,1)S(1)}, bf16[768]{0:T(1024)(128)(2,1)}, u32[]{:S(2)}) %copy-start.3) | copy-done | bytes 1560
  14.8 0.8 %shard_map.69 = (bf16[912,768]{1,0:T(8,128)(2,1)S(1)}, bf16[912,768]{1,0:T(8,128)(2,1)S(1)}) custom-call(bf16[768,768]{1,0:T(8,128)(2,1)S(1)} %copy-done.1, bf16[768,128]{1,0:T(8,128)(2,1)S(1)} %copy-done.2, bf16[768]{0:T(1024)(128)(2,1)S(1)} %copy-done.3, bf16[768,768]{1,0:T(8,128)(2,1)S(1)} %collective-permute-done.4.refs_3_, ...), custom_call_target="tpu_custom_call" | custom-call | tf_op jit(solution)/shard_map/pallas_call | solution.py:344
  15.9 0.9 %collective-permute-start.7 = (bf16[784,128]{1,0:T(8,128)(2,1)S(1)}, bf16[784,128]{1,0:T(8,128)(2,1)S(1)}, u32[]{:S(2)}, u32[]{:S(2)}) collective-permute-start(bf16[784,128]{1,0:T(8,128)(2,1)S(1)} %shard_map.70.refs_0_.rest_1_.rest_4_), channel_id=1, source_target_pairs={{0,4},{1,5},{2,6},{3,7},{4,0},{5,1},{6,2},{7,3},{8,12},{9,13},{10,... | collective-permute-start | bytes 602120 | tf_op jit(solution)/shard_map/ppermute | solution.py:237
  17.2 1.6 %collective-permute-start.10 = (bf16[784,128]{1,0:T(8,128)(2,1)S(1)}, bf16[784,128]{1,0:T(8,128)(2,1)S(1)}, u32[]{:S(2)}, u32[]{:S(2)}) collective-permute-start(bf16[784,128]{1,0:T(8,128)(2,1)S(1)} %shard_map.71), channel_id=1, source_target_pairs={{0,2},{1,3},{2,0},{3,1},{4,6},{5,7},{6,4},{7,5},{8,10},{9,11},{10,... | collective-permute-start | bytes 602120 | tf_op jit(solution)/shard_map/ppermute | solution.py:237
  19.0 4.1 %collective-permute-done.7.rest_1_.rest_6_ = bf16[784,128]{1,0:T(8,128)(2,1)S(1)} collective-permute-done((bf16[784,128]{1,0:T(8,128)(2,1)S(1)}, bf16[784,128]{1,0:T(8,128)(2,1)S(1)}, u32[]{:S(2)}, u32[]{:S(2)}) %collective-permute-start.7) | collective-permute-done | bytes 200736 | tf_op jit(solution)/shard_map/ppermute | solution.py:237
  23.7 1.3 %shard_map.72.rest_4_ = f32[72,128]{1,0:T(8,128)S(1)} custom-call(bf16[784,128]{1,0:T(8,128)(2,1)S(1)} %copy-done, bf16[784,128]{1,0:T(8,128)(2,1)S(1)} %collective-permute-done.rest_1_, bf16[912,768]{1,0:T(8,128)(2,1)S(1)} %get-tuple-element.6.rest_0_.rest_2_, bf16[912,768]{1,0:T(8,128)(2,1)S(1)} %get-tuple-element.7.rest_3_), custom_call_target="tpu_custom_call" | custom-call | flops 805306368 | tf_op jit(solution)/shard_map/pallas_call | solution.py:316
  25.0 1.4 %shard_map.73.rest_4_ = f32[72,128]{1,0:T(8,128)S(1)} custom-call(bf16[784,128]{1,0:T(8,128)(2,1)S(1)} %collective-permute-done.9.refs_1_.rest_0_.rest_2_, bf16[784,128]{1,0:T(8,128)(2,1)S(1)} %shard_map.70.refs_0_.rest_1_.rest_4_, bf16[912,768]{1,0:T(8,128)(2,1)S(1)} %get-tuple-element.6.rest_0_.rest_2_, bf16[912,768]{1,0:T(8,128)(2,1)S(1)} %get-tuple-element.7.rest_3_, ...), custom_call_target="tpu_custom_call" | custom-call | flops 805306368 | tf_op jit(solution)/shard_map/pallas_call | solution.py:316
  26.4 1.4 %shard_map.74.rest_4_ = f32[72,128]{1,0:T(8,128)S(1)} custom-call(bf16[784,128]{1,0:T(8,128)(2,1)S(1)} %collective-permute-done.10.rest_0_.rest_5_, bf16[784,128]{1,0:T(8,128)(2,1)S(1)} %collective-permute-done.7.rest_1_.rest_6_, bf16[912,768]{1,0:T(8,128)(2,1)S(1)} %get-tuple-element.6.rest_0_.rest_2_, bf16[912,768]{1,0:T(8,128)(2,1)S(1)} %get-tuple-element.7.rest_3_, ...), custom_call_target="tpu_custom_call" | custom-call | flops 805306368 | tf_op jit(solution)/shard_map/pallas_call | solution.py:316
  27.8 1.0 %collective-permute-done.8.rest_1_.rest_7_ = bf16[784,128]{1,0:T(8,128)(2,1)S(1)} collective-permute-done((bf16[784,128]{1,0:T(8,128)(2,1)S(1)}, bf16[784,128]{1,0:T(8,128)(2,1)S(1)}, u32[]{:S(2)}, u32[]{:S(2)}) %collective-permute-start.8) | collective-permute-done | bytes 200736 | tf_op jit(solution)/shard_map/ppermute | solution.py:237
  28.8 1.4 %shard_map.75 = f32[72,128]{1,0:T(8,128)S(1)} custom-call(bf16[784,128]{1,0:T(8,128)(2,1)S(1)} %collective-permute-done.1.rest_0_.rest_3_, bf16[784,128]{1,0:T(8,128)(2,1)S(1)} %collective-permute-done.8.rest_1_.rest_7_, bf16[912,768]{1,0:T(8,128)(2,1)S(1)} %get-tuple-element.6.rest_0_.rest_2_, bf16[912,768]{1,0:T(8,128)(2,1)S(1)} %get-tuple-element.7.rest_3_, ...), custom_call_target="tpu_custom_call" | custom-call | flops 805306368 | tf_op jit(solution)/shard_map/pallas_call | solution.py:316
  30.1 0.7 %collective-permute-start.11 = (f32[72,128]{1,0:T(8,128)S(1)}, f32[72,128]{1,0:T(8,128)S(1)}, u32[]{:S(2)}, u32[]{:S(2)}) collective-permute-start(f32[72,128]{1,0:T(8,128)S(1)} %shard_map.75), channel_id=1, source_target_pairs={{0,2},{1,3},{2,0},{3,1},{4,6},{5,7},{6,4},{7,5},{8,10},{9,11},{10,... | collective-permute-start | bytes 110600 | tf_op jit(solution)/shard_map/ppermute | solution.py:237
  30.8 3.4 %collective-permute-done.11 = f32[72,128]{1,0:T(8,128)S(1)} collective-permute-done((f32[72,128]{1,0:T(8,128)S(1)}, f32[72,128]{1,0:T(8,128)S(1)}, u32[]{:S(2)}, u32[]{:S(2)}) %collective-permute-start.11) | collective-permute-done | bytes 36896 | tf_op jit(solution)/shard_map/ppermute | solution.py:237
  34.8 3.3 %collective-permute-done.12 = f32[72,128]{1,0:T(8,128)S(1)} collective-permute-done((f32[72,128]{1,0:T(8,128)S(1)}, f32[72,128]{1,0:T(8,128)S(1)}, u32[]{:S(2)}, u32[]{:S(2)}) %collective-permute-start.12) | collective-permute-done | bytes 36896 | tf_op jit(solution)/shard_map/ppermute | solution.py:237
  38.1 3.0 %collective-permute-start.13 = (f32[72,128]{1,0:T(8,128)S(1)}, f32[72,128]{1,0:T(8,128)S(1)}, u32[]{:S(2)}, u32[]{:S(2)}) collective-permute-start(f32[72,128]{1,0:T(8,128)S(1)} %add.7.q_ref), channel_id=1, source_target_pairs={{0,8},{1,9},{2,10},{3,11},{4,12},{5,13},{6,14},{7,15},{8,0},{9,1},... | collective-permute-start | bytes 110600 | tf_op jit(solution)/shard_map/ppermute | solution.py:237
  41.1 1.8 %shard_map.76.prior_ref = f32[16,128]{1,0:T(8,128)S(1)} custom-call(bf16[784,128]{1,0:T(8,128)(2,1)S(1)} %copy-done, bf16[784,128]{1,0:T(8,128)(2,1)S(1)} %collective-permute-done.14.sib_ref, bf16[784,128]{1,0:T(8,128)(2,1)S(1)} %copy-done, bf16[784,128]{1,0:T(8,128)(2,1)S(1)} %collective-permute-done.rest_1_, ...), custom_call_target="tpu_custom_call" | custom-call | flops 536870912 | tf_op jit(solution)/shard_map/pallas_call | solution.py:328
  43.1 1.2 %collective-permute-done.15.other_ref = f32[80,128]{1,0:T(8,128)S(1)} collective-permute-done((f32[80,128]{1,0:T(8,128)S(1)}, f32[80,128]{1,0:T(8,128)S(1)}, u32[]{:S(2)}, u32[]{:S(2)}) %collective-permute-start.15) | collective-permute-done | bytes 40992 | tf_op jit(solution)/shard_map/ppermute | solution.py:237
  44.3 0.8 %shard_map.78 = (f32[8]{0:T(128)}, f32[8,128]{1,0:T(8,128)}) custom-call(f32[80,128]{1,0:T(8,128)S(1)} %shard_map.77.q_ref, f32[80,128]{1,0:T(8,128)S(1)} %collective-permute-done.15.other_ref, f32[16,128]{1,0:T(8,128)S(1)} %shard_map.76.prior_ref), custom_call_target="tpu_custom_call" | custom-call | tf_op jit(solution)/shard_map/pallas_call | solution.py:373
  (29 shorter events, 3.1 us)
Async XLA Ops:
  0.6 11.3 %collective-permute-start.4 = (bf16[768,768]{1,0:T(8,128)(2,1)}, bf16[768,768]{1,0:T(8,128)(2,1)S(1)}, u32[]{:S(2)}, u32[]{:S(2)}) collective-permute-start(bf16[768,768]{1,0:T(8,128)(2,1)} %refs_0_.1), channel_id=1, source_target_pairs={{0,1},{1,0},{2,3},{3,2},{4,5},{5,4},{6,7},{7,6},{8,9},{9,8},{10,11... | collective-permute-start | bytes 3538952 | tf_op jit(solution)/shard_map/ppermute | solution.py:237
  1.1 9.3 %collective-permute-start.5 = (bf16[768,128]{1,0:T(8,128)(2,1)}, bf16[768,128]{1,0:T(8,128)(2,1)S(1)}, u32[]{:S(2)}, u32[]{:S(2)}) collective-permute-start(bf16[768,128]{1,0:T(8,128)(2,1)} %refs_1_.1), channel_id=1, source_target_pairs={{0,1},{1,0},{2,3},{3,2},{4,5},{5,4},{6,7},{7,6},{8,9},{9,8},{10,11... | collective-permute-start | bytes 589832 | tf_op jit(solution)/shard_map/ppermute | solution.py:237
  1.2 14.5 %collective-permute-start.2 = (bf16[128,768]{1,0:T(8,128)(2,1)}, bf16[128,768]{1,0:T(8,128)(2,1)S(1)}, u32[]{:S(2)}, u32[]{:S(2)}) collective-permute-start(bf16[128,768]{1,0:T(8,128)(2,1)} %cand_ref.1), channel_id=1, source_target_pairs={{0,8},{1,9},{2,10},{3,11},{4,12},{5,13},{6,14},{7,15},{8,0},{9,1},... | collective-permute-start | bytes 589832 | tf_op jit(solution)/shard_map/ppermute | solution.py:237
  7.1 10.0 %collective-permute-start.9 = (bf16[784,128]{1,0:T(8,128)(2,1)}, bf16[784,128]{1,0:T(8,128)(2,1)S(1)}, u32[]{:S(2)}, u32[]{:S(2)}) collective-permute-start(bf16[784,128]{1,0:T(8,128)(2,1)} %shard_map.68.rest_0_.own_ref), channel_id=1, source_target_pairs={{0,4},{1,5},{2,6},{3,7},{4,0},{5,1},{6,2},{7,3},{8,12},{9,13},{10,... | collective-permute-start | bytes 602120 | tf_op jit(solution)/shard_map/ppermute | solution.py:237
  8.8 1.4 %collective-permute-start.6 = (bf16[768]{0:T(1024)(128)(2,1)}, bf16[768]{0:T(1024)(128)(2,1)S(1)}, u32[]{:S(2)}, u32[]{:S(2)}) collective-permute-start(bf16[768]{0:T(1024)(128)(2,1)} %refs_2_.1), channel_id=1, source_target_pairs={{0,1},{1,0},{2,3},{3,2},{4,5},{5,4},{6,7},{7,6},{8,9},{9,8},{10,11... | collective-permute-start | bytes 4616 | tf_op jit(solution)/shard_map/ppermute | solution.py:237
  10.1 5.6 %collective-permute-start.3 = (s32[1,128]{1,0:T(1,128)}, s32[1,128]{1,0:T(1,128)S(1)}, u32[]{:S(2)}, u32[]{:S(2)}) collective-permute-start(s32[1,128]{1,0:T(1,128)} %bitcast.3), channel_id=1, source_target_pairs={{0,8},{1,9},{2,10},{3,11},{4,12},{5,13},{6,14},{7,15},{8,0},{9,1},... | collective-permute-start | bytes 1544 | tf_op jit(solution)/shard_map/ppermute | solution.py:237
  10.5 8.3 %collective-permute-start = (bf16[784,128]{1,0:T(8,128)(2,1)}, bf16[784,128]{1,0:T(8,128)(2,1)S(1)}, u32[]{:S(2)}, u32[]{:S(2)}) collective-permute-start(bf16[784,128]{1,0:T(8,128)(2,1)} %shard_map.68.rest_0_.own_ref), channel_id=1, source_target_pairs={{0,2},{1,3},{2,0},{3,1},{4,6},{5,7},{6,4},{7,5},{8,10},{9,11},{10,... | collective-permute-start | bytes 602120 | tf_op jit(solution)/shard_map/ppermute | solution.py:237
  12.0 1.3 %copy-start.1 = (bf16[768,768]{1,0:T(8,128)(2,1)S(1)}, bf16[768,768]{1,0:T(8,128)(2,1)}, u32[]{:S(2)}) copy-start(bf16[768,768]{1,0:T(8,128)(2,1)} %refs_0_.1) | copy-start | bytes 3538948
  13.2 0.9 %copy-start.2 = (bf16[768,128]{1,0:T(8,128)(2,1)S(1)}, bf16[768,128]{1,0:T(8,128)(2,1)}, u32[]{:S(2)}) copy-start(bf16[768,128]{1,0:T(8,128)(2,1)} %refs_1_.1) | copy-start | bytes 589828
  14.2 0.7 %copy-start.3 = (bf16[768]{0:T(1024)(128)(2,1)S(1)}, bf16[768]{0:T(1024)(128)(2,1)}, u32[]{:S(2)}) copy-start(bf16[768]{0:T(1024)(128)(2,1)} %refs_2_.1) | copy-start | bytes 4612
  15.7 3.1 %copy-start = (bf16[784,128]{1,0:T(8,128)(2,1)S(1)}, bf16[784,128]{1,0:T(8,128)(2,1)}, u32[]{:S(2)}) copy-start(bf16[784,128]{1,0:T(8,128)(2,1)} %shard_map.68.rest_0_.own_ref) | copy-start | bytes 602116
  15.9 7.1 %collective-permute-start.7 = (bf16[784,128]{1,0:T(8,128)(2,1)S(1)}, bf16[784,128]{1,0:T(8,128)(2,1)S(1)}, u32[]{:S(2)}, u32[]{:S(2)}) collective-permute-start(bf16[784,128]{1,0:T(8,128)(2,1)S(1)} %shard_map.70.refs_0_.rest_1_.rest_4_), channel_id=1, source_target_pairs={{0,4},{1,5},{2,6},{3,7},{4,0},{5,1},{6,2},{7,3},{8,12},{9,13},{10,... | collective-permute-start | bytes 602120 | tf_op jit(solution)/shard_map/ppermute | solution.py:237
  17.2 9.2 %collective-permute-start.10 = (bf16[784,128]{1,0:T(8,128)(2,1)S(1)}, bf16[784,128]{1,0:T(8,128)(2,1)S(1)}, u32[]{:S(2)}, u32[]{:S(2)}) collective-permute-start(bf16[784,128]{1,0:T(8,128)(2,1)S(1)} %shard_map.71), channel_id=1, source_target_pairs={{0,2},{1,3},{2,0},{3,1},{4,6},{5,7},{6,4},{7,5},{8,10},{9,11},{10,... | collective-permute-start | bytes 602120 | tf_op jit(solution)/shard_map/ppermute | solution.py:237
  18.8 22.4 %collective-permute-start.14 = (bf16[784,128]{1,0:T(8,128)(2,1)S(1)}, bf16[784,128]{1,0:T(8,128)(2,1)S(1)}, u32[]{:S(2)}, u32[]{:S(2)}) collective-permute-start(bf16[784,128]{1,0:T(8,128)(2,1)S(1)} %copy-done), channel_id=1, source_target_pairs={{0,1},{1,0},{2,3},{3,2},{4,5},{5,4},{6,7},{7,6},{8,9},{9,8},{10,11... | collective-permute-start | bytes 602120 | tf_op jit(solution)/shard_map/ppermute | solution.py:237
  18.8 9.0 %collective-permute-start.1 = (bf16[784,128]{1,0:T(8,128)(2,1)S(1)}, bf16[784,128]{1,0:T(8,128)(2,1)S(1)}, u32[]{:S(2)}, u32[]{:S(2)}) collective-permute-start(bf16[784,128]{1,0:T(8,128)(2,1)S(1)} %collective-permute-done.rest_1_), channel_id=1, source_target_pairs={{0,4},{1,5},{2,6},{3,7},{4,0},{5,1},{6,2},{7,3},{8,12},{9,13},{10,... | collective-permute-start | bytes 602120 | tf_op jit(solution)/shard_map/ppermute | solution.py:237
  23.1 5.7 %collective-permute-start.8 = (bf16[784,128]{1,0:T(8,128)(2,1)S(1)}, bf16[784,128]{1,0:T(8,128)(2,1)S(1)}, u32[]{:S(2)}, u32[]{:S(2)}) collective-permute-start(bf16[784,128]{1,0:T(8,128)(2,1)S(1)} %collective-permute-done.7.rest_1_.rest_6_), channel_id=1, source_target_pairs={{0,2},{1,3},{2,0},{3,1},{4,6},{5,7},{6,4},{7,5},{8,10},{9,11},{10,... | collective-permute-start | bytes 602120 | tf_op jit(solution)/shard_map/ppermute | solution.py:237
  30.1 4.0 %collective-permute-start.11 = (f32[72,128]{1,0:T(8,128)S(1)}, f32[72,128]{1,0:T(8,128)S(1)}, u32[]{:S(2)}, u32[]{:S(2)}) collective-permute-start(f32[72,128]{1,0:T(8,128)S(1)} %shard_map.75), channel_id=1, source_target_pairs={{0,2},{1,3},{2,0},{3,1},{4,6},{5,7},{6,4},{7,5},{8,10},{9,11},{10,... | collective-permute-start | bytes 110600 | tf_op jit(solution)/shard_map/ppermute | solution.py:237
  34.2 4.0 %collective-permute-start.12 = (f32[72,128]{1,0:T(8,128)S(1)}, f32[72,128]{1,0:T(8,128)S(1)}, u32[]{:S(2)}, u32[]{:S(2)}) collective-permute-start(f32[72,128]{1,0:T(8,128)S(1)} %add.6), channel_id=1, source_target_pairs={{0,4},{1,5},{2,6},{3,7},{4,0},{5,1},{6,2},{7,3},{8,12},{9,13},{10,... | collective-permute-start | bytes 110600 | tf_op jit(solution)/shard_map/ppermute | solution.py:237
  38.1 4.9 %collective-permute-start.13 = (f32[72,128]{1,0:T(8,128)S(1)}, f32[72,128]{1,0:T(8,128)S(1)}, u32[]{:S(2)}, u32[]{:S(2)}) collective-permute-start(f32[72,128]{1,0:T(8,128)S(1)} %add.7.q_ref), channel_id=1, source_target_pairs={{0,8},{1,9},{2,10},{3,11},{4,12},{5,13},{6,14},{7,15},{8,0},{9,1},... | collective-permute-start | bytes 110600 | tf_op jit(solution)/shard_map/ppermute | solution.py:237
  43.1 1.3 %collective-permute-start.15 = (f32[80,128]{1,0:T(8,128)S(1)}, f32[80,128]{1,0:T(8,128)S(1)}, u32[]{:S(2)}, u32[]{:S(2)}) collective-permute-start(f32[80,128]{1,0:T(8,128)S(1)} %shard_map.77.q_ref), channel_id=1, source_target_pairs={{0,1},{1,0},{2,3},{3,2},{4,5},{5,4},{6,7},{7,6},{8,9},{9,8},{10,11... | collective-permute-start | bytes 122888 | tf_op jit(solution)/shard_map/ppermute | solution.py:237

commit v6 on v5

--- a/solution.py
+++ b/solution.py
@@ -36,11 +36,15 @@
     return parts
 
 
-def pack_cand(cand_ref, ids_ref, out_ref, raw, ids, sems):
+def pack_own(cand_ref, ids_ref, lanczos_ref, weight_ref, out_ref, tail_ref,
+             raw, ids, factor, weights, sems):
     rows, width = raw.shape
+    rank = factor.shape[1]
     copies = [
-        pltpu.make_async_copy(cand_ref, raw, sems.at[0]),
-        pltpu.make_async_copy(ids_ref, ids, sems.at[1]),
+        pltpu.make_async_copy(source, target, sems.at[i])
+        for i, (source, target) in enumerate(
+            ((cand_ref, raw), (ids_ref, ids), (lanczos_ref, factor), (weight_ref, weights))
+        )
     ]
     for copy in copies:
         copy.start()
@@ -49,6 +53,10 @@
     out_ref[:width, :] = unit_rows(raw[...]).T
     within = (ids[...] - ids[0, 0]).astype(jnp.float32)
     out_ref[width:, :] = jnp.broadcast_to(within, (TAIL, rows)).astype(jnp.bfloat16)
+    tail_ref[:rank, :] = factor[...].T
+    tail_ref[rank:, :] = jnp.broadcast_to(
+        weights[...].astype(jnp.float32).reshape(1, -1), (TAIL, factor.shape[0])
+    ).astype(jnp.bfloat16)
 
 
 def pack_here(cand_ref, ids_ref, *rest):
@@ -59,27 +67,16 @@
     out_ref[width:, :] = jnp.broadcast_to(within, (TAIL, rows)).astype(jnp.bfloat16)
 
 
-def pack_train(*refs):
-    for train_ref, lanczos_ref, weight_ref, out_ref in (
-        refs[:3] + refs[6:7],
-        refs[3:6] + refs[7:],
-    ):
-        count, rank = lanczos_ref.shape
-        step = count // 6
+def unit_train(own_ref, sib_ref, own_out, sib_out):
+    step = own_ref.shape[0] // 6
+    for raw, out in ((own_ref, own_out), (sib_ref, sib_out)):
         for i in range(6):
             part = slice(i * step, (i + 1) * step)
-            out_ref[part, :] = unit_rows(train_ref[part, :])
-        out_ref[count : count + rank, :] = lanczos_ref[...].T
-        out_ref[count + rank :, :] = jnp.broadcast_to(
-            weight_ref[...].astype(jnp.float32).reshape(1, count), (TAIL, count)
-        ).astype(jnp.bfloat16)
-
-
-def copy_after(value_ref, _, *out_refs):
-    start = 0
-    for ref in out_refs:
-        ref[...] = value_ref[start : start + ref.shape[0], :]
-        start += ref.shape[0]
+            out[part, :] = unit_rows(raw[part, :])
+
+
+def copy_after(value_ref, *rest):
+    rest[-1][...] = value_ref[...]
 
 
 def quartic(products, width):
@@ -95,7 +92,8 @@
 
 
 def project(masks, chips, width, rank, first, cut, parts, *rest):
-    refs, (town_ref, tsib_ref, *rest) = rest[:parts], rest[parts:]
+    refs, (*train_refs, ) = rest[:parts], rest[parts : parts + 4]
+    rest = rest[parts + 4 :]
     chip = lax.axis_index("train") // 2
     one, two = (
         jnp.concatenate([ref[...] for ref in piece], axis=0)
@@ -111,10 +109,9 @@
         axis=1,
     )
     proj = None
-    for ref in (town_ref, tsib_ref):
-        count = ref.shape[0] - rank - TAIL
-        kernel_rows = quartic(product(ref[:count, :], pair), width).astype(jnp.bfloat16)
-        term = product(ref[count:, :], kernel_rows)
+    for ref, tail in (train_refs[:2], train_refs[2:]):
+        kernel_rows = quartic(product(ref[...], pair), width).astype(jnp.bfloat16)
+        term = product(tail[...], kernel_rows)
         proj = term if proj is None else proj + term
     sums = sum(product(member, part, ((1,), (1,))) for part in thirds(proj))
     size = jnp.sum(member.astype(jnp.float32), axis=1, keepdims=True)
@@ -237,39 +234,23 @@
         return lax.ppermute(value, "train", [(i, i ^ mask) for i in range(size)])
 
     block_shape = jax.ShapeDtypeStruct((width + TAIL, rows), jnp.bfloat16)
-    own = pl.pallas_call(
-        pack_cand,
-        out_shape=block_shape,
-        in_specs=[HBM, HBM],
-        out_specs=VMEM,
+    own, tail_own = pl.pallas_call(
+        pack_own,
+        out_shape=[
+            block_shape,
+            jax.ShapeDtypeStruct((rank + TAIL, count), jnp.bfloat16),
+        ],
+        in_specs=[HBM] * 4,
+        out_specs=[VMEM] * 2,
         scratch_shapes=[
             pltpu.VMEM((rows, width), jnp.bfloat16),
             pltpu.VMEM((1, rows), jnp.int32),
-            pltpu.SemaphoreType.DMA((2,)),
+            pltpu.VMEM((count, rank), jnp.bfloat16),
+            pltpu.VMEM((count,), jnp.bfloat16),
+            pltpu.SemaphoreType.DMA((4,)),
         ],
         compiler_params=pltpu.CompilerParams(vmem_limit_bytes=58 * 2**20),
-    )(cand_desc, struct_id.reshape(1, rows))
-
-    def again(value, other, pieces):
-        shapes = [
-            jax.ShapeDtypeStruct((piece, value.shape[1]), value.dtype) for piece in pieces
-        ]
-        return pl.pallas_call(
-            copy_after,
-            out_shape=shapes,
-            in_specs=[VMEM, pl.BlockSpec(memory_space=pl.ANY)],
-            out_specs=[VMEM] * len(shapes),
-            compiler_params=pltpu.CompilerParams(vmem_limit_bytes=24 * 2**20),
-        )(value, other)
-
-    def again_last(value, *others):
-        return pl.pallas_call(
-            lambda *refs: copy_after(refs[-2], None, refs[-1]),
-            out_shape=block_shape,
-            in_specs=[pl.BlockSpec(memory_space=pl.ANY)] * len(others) + [VMEM],
-            out_specs=VMEM,
-            compiler_params=pltpu.CompilerParams(vmem_limit_bytes=24 * 2**20),
-        )(*others, value)
+    )(cand_desc, struct_id.reshape(1, rows), lanczos, mean_weight)
 
     def pack_received(mask, *others):
         return pl.pallas_call(
@@ -280,24 +261,9 @@
             compiler_params=pltpu.CompilerParams(vmem_limit_bytes=24 * 2**20),
         )(swap(cand_desc, mask), swap(struct_id.reshape(1, rows), mask), *others)
 
-    def again_pieces(value, pieces, *others):
-        shapes = [
-            jax.ShapeDtypeStruct((piece, value.shape[1]), value.dtype) for piece in pieces
-        ]
-        def kernel(*refs):
-            refs[1 + len(others)][...] = refs[0][...]
-            copy_after(refs[0], None, *refs[2 + len(others) :])
+    def again(value, *others):
         return pl.pallas_call(
-            kernel,
-            out_shape=[block_shape, *shapes],
-            in_specs=[VMEM] + [pl.BlockSpec(memory_space=pl.ANY)] * len(others),
-            out_specs=[VMEM] * (1 + len(shapes)),
-            compiler_params=pltpu.CompilerParams(vmem_limit_bytes=24 * 2**20),
-        )(value, *others)
-
-    def again_first(value, *others):
-        return pl.pallas_call(
-            lambda *refs: copy_after(refs[0], None, refs[-1]),
+            copy_after,
             out_shape=block_shape,
             in_specs=[VMEM] + [pl.BlockSpec(memory_space=pl.ANY)] * len(others),
             out_specs=VMEM,
@@ -316,9 +282,9 @@
         return call(
             kernel,
             q_shape,
-            2 + len(pair) + len(state),
+            4 + len(pair) + len(state),
             flops=2 * 2 * rows * 2 * count * (width + 2 * rank),
-        )(*pair, train_own, train_sib, *state)
+        )(*pair, train_own, tail_own, train_sib, tail_sib, *state)
 
     def add_prior(masks, state, *refs):
         state = () if state is None else (state,)
@@ -339,18 +305,17 @@
     else:
         for mask in range(1, chips):
             blocks[mask] = swap(own, 2 * mask)
-    train = (train_desc, lanczos, mean_weight)
-    train_shape = jax.ShapeDtypeStruct((count + rank + TAIL, width), jnp.bfloat16)
-    train_own, train_sib = call(pack_train, (train_shape, train_shape), 6)(
-        *train, *[swap(value, 1) for value in train]
-    )
+    train_shape = jax.ShapeDtypeStruct(train_desc.shape, jnp.bfloat16)
+    train_own, train_sib = call(unit_train, (train_shape, train_shape), 2)(
+        train_desc, swap(train_desc, 1)
+    )
+    tail_sib = swap(tail_own, 1)
     if size == 16:
         far = pack_received(8, train_own)
         blocks[4] = far
-        late = again_first(far, blocks[2])
         blocks[6] = swap(far, 4)
-        blocks[5] = swap(late, 2)
-        blocks[3] = swap(blocks[1], 4)
+        blocks[5] = swap(again(far, blocks[2]), 2)
+        blocks[3] = swap(again(blocks[1], far), 4)
         blocks[7] = swap(blocks[6], 2)
         groups = ((0, 1), (2, 4), (5, 6), (3, 7))
     else:

time: 45.4 us -> 44.8 us (0.987)
  starting transfers between devices: 15.7 us -> 20.1 us
  waiting for transfers between devices: 14.8 us -> 11.4 us
  local copies, waits for them, and re-layouts: 2.88 us -> 1.28 us
    ppermute x16 -> x15, starting transfers between devices: 15.7 us -> 20.1 us  [swap(): return lax.ppermute(value, 'train', [(i, i ^ mask) for i in range(size)])]
    ppermute x16 -> x15, waiting for transfers between devices: 14.8 us -> 11.4 us  [swap(): return lax.ppermute(value, 'train', [(i, i ^ mask) for i in range(size)])]
    unnamed x8 -> x6, local copies, waits for them, and re-layouts: 2.88 us -> 1.28 us
    pallas_call x7 -> x8, Pallas kernels: 8.12 us -> 8.2 us  [the longest x4 5.38 us: add_projection(): call(kernel, q_shape, 4 + len(pair) + len(state), flops=2 * 2 * rows * 2...]
  transfers between devices with their start and end apart: 16 -> 15, of which waited for: 8 -> 7; matrix products, arithmetic and copies ran while one was open for 0% -> 0% of each run, Pallas kernels for 23% -> 23%
where the time goes in v6:
time: 44.8 us; the launch traced here: 44.7 us
  starting transfers between devices  20.1 us (45%)
  waiting for transfers between devices  11.4 us (25%)
  Pallas kernels  11.1 us (25%)
  local copies, waits for them, and re-layouts  1.28 us (3%)
  between operations  0.75 us (2%)
    ppermute x15, starting transfers between devices, swap(): return lax.ppermute(value, 'train', [(i, i ^ mask) for i in range(size)])  20.1 us
    ppermute x15, waiting for transfers between devices, swap(): return lax.ppermute(value, 'train', [(i, i ^ mask) for i in range(size)])  11.4 us
    pallas_call x4, Pallas kernels, add_projection(): call(kernel, q_shape, 4 + len(pair) + len(state), flops=2 * 2 * rows * 2...  5.38 us
    pallas_call x1, Pallas kernels, body(): pl.pallas_call(pack_own, out_shape=[block_shape, jax.ShapeDtypeStruct((ra...  2.04 us
    pallas_call x1, Pallas kernels, add_prior(): call(kernel, prior_shape, 2 + len(refs) + len(state), flops=2 * 2 * rows...  1.84 us
    unnamed x6, local copies, waits for them, and re-layouts  1.28 us
  transfers between devices with their start and end apart: 15, of which 7 were waited for; matrix products, arithmetic and copies ran while one was open for 0% of the time, Pallas kernels for 23%

profile of v6, /device:TPU:0, one launch (start us, length us, event | category | flops | bytes accessed | tf_op | source)
XLA Modules:
  0.0 44.7 jit_solution(5502934950083777259)
XLA Ops:
  0.6 0.5 %collective-permute-start.3 = (bf16[768,768]{1,0:T(8,128)(2,1)}, bf16[768,768]{1,0:T(8,128)(2,1)S(1)}, u32[]{:S(2)}, u32[]{:S(2)}) collective-permute-start(bf16[768,768]{1,0:T(8,128)(2,1)} %own_ref.1), channel_id=1, source_target_pairs={{0,1},{1,0},{2,3},{3,2},{4,5},{5,4},{6,7},{7,6},{8,9},{9,8},{10,11... | collective-permute-start | bytes 3538952 | tf_op jit(solution)/shard_map/ppermute | solution.py:234
  1.1 3.7 %collective-permute-start.1 = (bf16[128,768]{1,0:T(8,128)(2,1)}, bf16[128,768]{1,0:T(8,128)(2,1)S(1)}, u32[]{:S(2)}, u32[]{:S(2)}) collective-permute-start(bf16[128,768]{1,0:T(8,128)(2,1)} %cand_ref.1), channel_id=1, source_target_pairs={{0,8},{1,9},{2,10},{3,11},{4,12},{5,13},{6,14},{7,15},{8,0},{9,1},... | collective-permute-start | bytes 589832 | tf_op jit(solution)/shard_map/ppermute | solution.py:234
  4.8 2.0 %shard_map.68 = (bf16[784,128]{1,0:T(8,128)(2,1)}, bf16[144,768]{1,0:T(8,128)(2,1)}) custom-call(bf16[128,768]{1,0:T(8,128)(2,1)} %cand_ref.1, s32[1,128]{1,0:T(1,128)} %bitcast.2, bf16[768,128]{1,0:T(8,128)(2,1)} %lanczos_ref.1, bf16[768]{0:T(1024)(128)(2,1)} %weight_ref.1), custom_call_target="tpu_custom_call" | custom-call | tf_op jit(solution)/shard_map/pallas_call | solution.py:237
  6.9 1.6 %collective-permute-start.8 = (bf16[784,128]{1,0:T(8,128)(2,1)}, bf16[784,128]{1,0:T(8,128)(2,1)S(1)}, u32[]{:S(2)}, u32[]{:S(2)}) collective-permute-start(bf16[784,128]{1,0:T(8,128)(2,1)} %get-tuple-element.8.rest_0_.own_ref), channel_id=1, source_target_pairs={{0,4},{1,5},{2,6},{3,7},{4,0},{5,1},{6,2},{7,3},{8,12},{9,13},{10,... | collective-permute-start | bytes 602120 | tf_op jit(solution)/shard_map/ppermute | solution.py:234
  8.8 1.5 %collective-permute-start = (bf16[784,128]{1,0:T(8,128)(2,1)}, bf16[784,128]{1,0:T(8,128)(2,1)S(1)}, u32[]{:S(2)}, u32[]{:S(2)}) collective-permute-start(bf16[784,128]{1,0:T(8,128)(2,1)} %get-tuple-element.8.rest_0_.own_ref), channel_id=1, source_target_pairs={{0,2},{1,3},{2,0},{3,1},{4,6},{5,7},{6,4},{7,5},{8,10},{9,11},{10,... | collective-permute-start | bytes 602120 | tf_op jit(solution)/shard_map/ppermute | solution.py:234
  10.3 1.3 %copy-done.2 = bf16[768,768]{1,0:T(8,128)(2,1)S(1)} copy-done((bf16[768,768]{1,0:T(8,128)(2,1)S(1)}, bf16[768,768]{1,0:T(8,128)(2,1)}, u32[]{:S(2)}) %copy-start.2) | copy-done | bytes 1179672
  11.6 0.7 %shard_map.69 = (bf16[768,768]{1,0:T(8,128)(2,1)S(1)}, bf16[768,768]{1,0:T(8,128)(2,1)S(1)}) custom-call(bf16[768,768]{1,0:T(8,128)(2,1)S(1)} %copy-done.2, bf16[768,768]{1,0:T(8,128)(2,1)S(1)} %collective-permute-done.3.sib_ref), custom_call_target="tpu_custom_call" | custom-call | tf_op jit(solution)/shard_map/pallas_call | solution.py:309
  12.4 2.5 %collective-permute-done.2.ids_ref = s32[1,128]{1,0:T(1,128)S(1)} collective-permute-done((s32[1,128]{1,0:T(1,128)}, s32[1,128]{1,0:T(1,128)S(1)}, u32[]{:S(2)}, u32[]{:S(2)}) %collective-permute-start.2) | collective-permute-done | bytes 544 | tf_op jit(solution)/shard_map/ppermute | solution.py:234
  15.1 1.7 %collective-permute-start.5 = (bf16[784,128]{1,0:T(8,128)(2,1)S(1)}, bf16[784,128]{1,0:T(8,128)(2,1)S(1)}, u32[]{:S(2)}, u32[]{:S(2)}) collective-permute-start(bf16[784,128]{1,0:T(8,128)(2,1)S(1)} %shard_map.70.rest_0_.value_ref.rest_1_.rest_4_), channel_id=1, source_target_pairs={{0,4},{1,5},{2,6},{3,7},{4,0},{5,1},{6,2},{7,3},{8,12},{9,13},{10,... | collective-permute-start | bytes 602120 | tf_op jit(solution)/shard_map/ppermute | solution.py:234
  17.3 1.6 %collective-permute-start.9 = (bf16[784,128]{1,0:T(8,128)(2,1)S(1)}, bf16[784,128]{1,0:T(8,128)(2,1)S(1)}, u32[]{:S(2)}, u32[]{:S(2)}) collective-permute-start(bf16[784,128]{1,0:T(8,128)(2,1)S(1)} %shard_map.72), channel_id=1, source_target_pairs={{0,2},{1,3},{2,0},{3,1},{4,6},{5,7},{6,4},{7,5},{8,10},{9,11},{10,... | collective-permute-start | bytes 602120 | tf_op jit(solution)/shard_map/ppermute | solution.py:234
  19.0 2.8 %collective-permute-done.5.rest_1_.rest_6_ = bf16[784,128]{1,0:T(8,128)(2,1)S(1)} collective-permute-done((bf16[784,128]{1,0:T(8,128)(2,1)S(1)}, bf16[784,128]{1,0:T(8,128)(2,1)S(1)}, u32[]{:S(2)}, u32[]{:S(2)}) %collective-permute-start.5) | collective-permute-done | bytes 200736 | tf_op jit(solution)/shard_map/ppermute | solution.py:234
  21.8 1.9 %collective-permute-start.6 = (bf16[784,128]{1,0:T(8,128)(2,1)S(1)}, bf16[784,128]{1,0:T(8,128)(2,1)S(1)}, u32[]{:S(2)}, u32[]{:S(2)}) collective-permute-start(bf16[784,128]{1,0:T(8,128)(2,1)S(1)} %collective-permute-done.5.rest_1_.rest_6_), channel_id=1, source_target_pairs={{0,2},{1,3},{2,0},{3,1},{4,6},{5,7},{6,4},{7,5},{8,10},{9,11},{10,... | collective-permute-start | bytes 602120 | tf_op jit(solution)/shard_map/ppermute | solution.py:234
  23.8 1.3 %shard_map.73.rest_6_ = f32[72,128]{1,0:T(8,128)S(1)} custom-call(bf16[784,128]{1,0:T(8,128)(2,1)S(1)} %copy-done.1, bf16[784,128]{1,0:T(8,128)(2,1)S(1)} %collective-permute-done.value_ref.rest_1_, bf16[768,768]{1,0:T(8,128)(2,1)S(1)} %get-tuple-element.9.rest_0_.rest_2_, bf16[144,768]{1,0:T(8,128)(2,1)S(1)} %copy-done, ...), custom_call_target="tpu_custom_call" | custom-call | flops 805306368 | tf_op jit(solution)/shard_map/pallas_call | solution.py:282
  25.1 1.3 %shard_map.74.rest_6_ = f32[72,128]{1,0:T(8,128)S(1)} custom-call(bf16[784,128]{1,0:T(8,128)(2,1)S(1)} %collective-permute-done.8.rest_0_.rest_2_, bf16[784,128]{1,0:T(8,128)(2,1)S(1)} %shard_map.70.rest_0_.value_ref.rest_1_.rest_4_, bf16[768,768]{1,0:T(8,128)(2,1)S(1)} %get-tuple-element.9.rest_0_.rest_2_, bf16[144,768]{1,0:T(8,128)(2,1)S(1)} %copy-done, ...), custom_call_target="tpu_custom_call" | custom-call | flops 805306368 | tf_op jit(solution)/shard_map/pallas_call | solution.py:282
  26.5 1.3 %shard_map.75.rest_6_ = f32[72,128]{1,0:T(8,128)S(1)} custom-call(bf16[784,128]{1,0:T(8,128)(2,1)S(1)} %collective-permute-done.9.rest_0_.rest_5_, bf16[784,128]{1,0:T(8,128)(2,1)S(1)} %collective-permute-done.5.rest_1_.rest_6_, bf16[768,768]{1,0:T(8,128)(2,1)S(1)} %get-tuple-element.9.rest_0_.rest_2_, bf16[144,768]{1,0:T(8,128)(2,1)S(1)} %copy-done, ...), custom_call_target="tpu_custom_call" | custom-call | flops 805306368 | tf_op jit(solution)/shard_map/pallas_call | solution.py:282
  27.9 1.3 %shard_map.76 = f32[72,128]{1,0:T(8,128)S(1)} custom-call(bf16[784,128]{1,0:T(8,128)(2,1)S(1)} %collective-permute-done.4.rest_0_.rest_3_, bf16[784,128]{1,0:T(8,128)(2,1)S(1)} %collective-permute-done.6.rest_1_.rest_7_, bf16[768,768]{1,0:T(8,128)(2,1)S(1)} %get-tuple-element.9.rest_0_.rest_2_, bf16[144,768]{1,0:T(8,128)(2,1)S(1)} %copy-done, ...), custom_call_target="tpu_custom_call" | custom-call | flops 805306368 | tf_op jit(solution)/shard_map/pallas_call | solution.py:282
  29.2 1.7 %collective-permute-start.10 = (f32[72,128]{1,0:T(8,128)S(1)}, f32[72,128]{1,0:T(8,128)S(1)}, u32[]{:S(2)}, u32[]{:S(2)}) collective-permute-start(f32[72,128]{1,0:T(8,128)S(1)} %shard_map.76), channel_id=1, source_target_pairs={{0,2},{1,3},{2,0},{3,1},{4,6},{5,7},{6,4},{7,5},{8,10},{9,11},{10,... | collective-permute-start | bytes 110600 | tf_op jit(solution)/shard_map/ppermute | solution.py:234
  30.9 2.3 %collective-permute-done.10 = f32[72,128]{1,0:T(8,128)S(1)} collective-permute-done((f32[72,128]{1,0:T(8,128)S(1)}, f32[72,128]{1,0:T(8,128)S(1)}, u32[]{:S(2)}, u32[]{:S(2)}) %collective-permute-start.10) | collective-permute-done | bytes 36896 | tf_op jit(solution)/shard_map/ppermute | solution.py:234
  33.2 2.4 %collective-permute-start.11 = (f32[72,128]{1,0:T(8,128)S(1)}, f32[72,128]{1,0:T(8,128)S(1)}, u32[]{:S(2)}, u32[]{:S(2)}) collective-permute-start(f32[72,128]{1,0:T(8,128)S(1)} %add.6), channel_id=1, source_target_pairs={{0,4},{1,5},{2,6},{3,7},{4,0},{5,1},{6,2},{7,3},{8,12},{9,13},{10,... | collective-permute-start | bytes 110600 | tf_op jit(solution)/shard_map/ppermute | solution.py:234
  35.7 2.0 %collective-permute-done.11 = f32[72,128]{1,0:T(8,128)S(1)} collective-permute-done((f32[72,128]{1,0:T(8,128)S(1)}, f32[72,128]{1,0:T(8,128)S(1)}, u32[]{:S(2)}, u32[]{:S(2)}) %collective-permute-start.11) | collective-permute-done | bytes 36896 | tf_op jit(solution)/shard_map/ppermute | solution.py:234
  37.6 3.0 %collective-permute-start.12 = (f32[72,128]{1,0:T(8,128)S(1)}, f32[72,128]{1,0:T(8,128)S(1)}, u32[]{:S(2)}, u32[]{:S(2)}) collective-permute-start(f32[72,128]{1,0:T(8,128)S(1)} %add.7.q_ref), channel_id=1, source_target_pairs={{0,8},{1,9},{2,10},{3,11},{4,12},{5,13},{6,14},{7,15},{8,0},{9,1},... | collective-permute-start | bytes 110600 | tf_op jit(solution)/shard_map/ppermute | solution.py:234
  40.6 1.8 %shard_map.77.prior_ref = f32[16,128]{1,0:T(8,128)S(1)} custom-call(bf16[784,128]{1,0:T(8,128)(2,1)S(1)} %copy-done.1, bf16[784,128]{1,0:T(8,128)(2,1)S(1)} %collective-permute-done.13.sib_ref, bf16[784,128]{1,0:T(8,128)(2,1)S(1)} %copy-done.1, bf16[784,128]{1,0:T(8,128)(2,1)S(1)} %collective-permute-done.value_ref.rest_1_, ...), custom_call_target="tpu_custom_call" | custom-call | flops 536870912 | tf_op jit(solution)/shard_map/pallas_call | solution.py:294
  42.6 1.2 %collective-permute-done.14.other_ref = f32[80,128]{1,0:T(8,128)S(1)} collective-permute-done((f32[80,128]{1,0:T(8,128)S(1)}, f32[80,128]{1,0:T(8,128)S(1)}, u32[]{:S(2)}, u32[]{:S(2)}) %collective-permute-start.14) | collective-permute-done | bytes 40992 | tf_op jit(solution)/shard_map/ppermute | solution.py:234
  43.8 0.8 %shard_map.79 = (f32[8]{0:T(128)}, f32[8,128]{1,0:T(8,128)}) custom-call(f32[80,128]{1,0:T(8,128)S(1)} %shard_map.78.q_ref, f32[80,128]{1,0:T(8,128)S(1)} %collective-permute-done.14.other_ref, f32[16,128]{1,0:T(8,128)S(1)} %shard_map.77.prior_ref), custom_call_target="tpu_custom_call" | custom-call | tf_op jit(solution)/shard_map/pallas_call | solution.py:338
  (26 shorter events, 1.3 us)
Async XLA Ops:
  0.6 8.2 %collective-permute-start.3 = (bf16[768,768]{1,0:T(8,128)(2,1)}, bf16[768,768]{1,0:T(8,128)(2,1)S(1)}, u32[]{:S(2)}, u32[]{:S(2)}) collective-permute-start(bf16[768,768]{1,0:T(8,128)(2,1)} %own_ref.1), channel_id=1, source_target_pairs={{0,1},{1,0},{2,3},{3,2},{4,5},{5,4},{6,7},{7,6},{8,9},{9,8},{10,11... | collective-permute-start | bytes 3538952 | tf_op jit(solution)/shard_map/ppermute | solution.py:234
  1.1 13.8 %collective-permute-start.1 = (bf16[128,768]{1,0:T(8,128)(2,1)}, bf16[128,768]{1,0:T(8,128)(2,1)S(1)}, u32[]{:S(2)}, u32[]{:S(2)}) collective-permute-start(bf16[128,768]{1,0:T(8,128)(2,1)} %cand_ref.1), channel_id=1, source_target_pairs={{0,8},{1,9},{2,10},{3,11},{4,12},{5,13},{6,14},{7,15},{8,0},{9,1},... | collective-permute-start | bytes 589832 | tf_op jit(solution)/shard_map/ppermute | solution.py:234
  6.9 10.4 %collective-permute-start.8 = (bf16[784,128]{1,0:T(8,128)(2,1)}, bf16[784,128]{1,0:T(8,128)(2,1)S(1)}, u32[]{:S(2)}, u32[]{:S(2)}) collective-permute-start(bf16[784,128]{1,0:T(8,128)(2,1)} %get-tuple-element.8.rest_0_.own_ref), channel_id=1, source_target_pairs={{0,4},{1,5},{2,6},{3,7},{4,0},{5,1},{6,2},{7,3},{8,12},{9,13},{10,... | collective-permute-start | bytes 602120 | tf_op jit(solution)/shard_map/ppermute | solution.py:234
  8.5 15.3 %collective-permute-start.7 = (bf16[144,768]{1,0:T(8,128)(2,1)}, bf16[144,768]{1,0:T(8,128)(2,1)S(1)}, u32[]{:S(2)}, u32[]{:S(2)}) collective-permute-start(bf16[144,768]{1,0:T(8,128)(2,1)} %get-tuple-element.10.rest_3_), channel_id=1, source_target_pairs={{0,1},{1,0},{2,3},{3,2},{4,5},{5,4},{6,7},{7,6},{8,9},{9,8},{10,11... | collective-permute-start | bytes 663560 | tf_op jit(solution)/shard_map/ppermute | solution.py:234
  8.5 6.4 %collective-permute-start.2 = (s32[1,128]{1,0:T(1,128)}, s32[1,128]{1,0:T(1,128)S(1)}, u32[]{:S(2)}, u32[]{:S(2)}) collective-permute-start(s32[1,128]{1,0:T(1,128)} %bitcast.3), channel_id=1, source_target_pairs={{0,8},{1,9},{2,10},{3,11},{4,12},{5,13},{6,14},{7,15},{8,0},{9,1},... | collective-permute-start | bytes 1544 | tf_op jit(solution)/shard_map/ppermute | solution.py:234
  8.8 10.0 %collective-permute-start = (bf16[784,128]{1,0:T(8,128)(2,1)}, bf16[784,128]{1,0:T(8,128)(2,1)S(1)}, u32[]{:S(2)}, u32[]{:S(2)}) collective-permute-start(bf16[784,128]{1,0:T(8,128)(2,1)} %get-tuple-element.8.rest_0_.own_ref), channel_id=1, source_target_pairs={{0,2},{1,3},{2,0},{3,1},{4,6},{5,7},{6,4},{7,5},{8,10},{9,11},{10,... | collective-permute-start | bytes 602120 | tf_op jit(solution)/shard_map/ppermute | solution.py:234
  10.3 1.3 %copy-start.2 = (bf16[768,768]{1,0:T(8,128)(2,1)S(1)}, bf16[768,768]{1,0:T(8,128)(2,1)}, u32[]{:S(2)}) copy-start(bf16[768,768]{1,0:T(8,128)(2,1)} %own_ref.1) | copy-start | bytes 3538948
  12.4 6.5 %copy-start.1 = (bf16[784,128]{1,0:T(8,128)(2,1)S(1)}, bf16[784,128]{1,0:T(8,128)(2,1)}, u32[]{:S(2)}) copy-start(bf16[784,128]{1,0:T(8,128)(2,1)} %get-tuple-element.8.rest_0_.own_ref) | copy-start | bytes 602116
  14.9 8.9 %copy-start = (bf16[144,768]{1,0:T(8,128)(2,1)S(1)}, bf16[144,768]{1,0:T(8,128)(2,1)}, u32[]{:S(2)}) copy-start(bf16[144,768]{1,0:T(8,128)(2,1)} %get-tuple-element.10.rest_3_) | copy-start | bytes 663556
  15.1 6.7 %collective-permute-start.5 = (bf16[784,128]{1,0:T(8,128)(2,1)S(1)}, bf16[784,128]{1,0:T(8,128)(2,1)S(1)}, u32[]{:S(2)}, u32[]{:S(2)}) collective-permute-start(bf16[784,128]{1,0:T(8,128)(2,1)S(1)} %shard_map.70.rest_0_.value_ref.rest_1_.rest_4_), channel_id=1, source_target_pairs={{0,4},{1,5},{2,6},{3,7},{4,0},{5,1},{6,2},{7,3},{8,12},{9,13},{10,... | collective-permute-start | bytes 602120 | tf_op jit(solution)/shard_map/ppermute | solution.py:234
  17.3 9.2 %collective-permute-start.9 = (bf16[784,128]{1,0:T(8,128)(2,1)S(1)}, bf16[784,128]{1,0:T(8,128)(2,1)S(1)}, u32[]{:S(2)}, u32[]{:S(2)}) collective-permute-start(bf16[784,128]{1,0:T(8,128)(2,1)S(1)} %shard_map.72), channel_id=1, source_target_pairs={{0,2},{1,3},{2,0},{3,1},{4,6},{5,7},{6,4},{7,5},{8,10},{9,11},{10,... | collective-permute-start | bytes 602120 | tf_op jit(solution)/shard_map/ppermute | solution.py:234
  18.9 21.8 %collective-permute-start.13 = (bf16[784,128]{1,0:T(8,128)(2,1)S(1)}, bf16[784,128]{1,0:T(8,128)(2,1)S(1)}, u32[]{:S(2)}, u32[]{:S(2)}) collective-permute-start(bf16[784,128]{1,0:T(8,128)(2,1)S(1)} %copy-done.1), channel_id=1, source_target_pairs={{0,1},{1,0},{2,3},{3,2},{4,5},{5,4},{6,7},{7,6},{8,9},{9,8},{10,11... | collective-permute-start | bytes 602120 | tf_op jit(solution)/shard_map/ppermute | solution.py:234
  18.9 8.9 %collective-permute-start.4 = (bf16[784,128]{1,0:T(8,128)(2,1)S(1)}, bf16[784,128]{1,0:T(8,128)(2,1)S(1)}, u32[]{:S(2)}, u32[]{:S(2)}) collective-permute-start(bf16[784,128]{1,0:T(8,128)(2,1)S(1)} %shard_map.71), channel_id=1, source_target_pairs={{0,4},{1,5},{2,6},{3,7},{4,0},{5,1},{6,2},{7,3},{8,12},{9,13},{10,... | collective-permute-start | bytes 602120 | tf_op jit(solution)/shard_map/ppermute | solution.py:234
  21.8 6.0 %collective-permute-start.6 = (bf16[784,128]{1,0:T(8,128)(2,1)S(1)}, bf16[784,128]{1,0:T(8,128)(2,1)S(1)}, u32[]{:S(2)}, u32[]{:S(2)}) collective-permute-start(bf16[784,128]{1,0:T(8,128)(2,1)S(1)} %collective-permute-done.5.rest_1_.rest_6_), channel_id=1, source_target_pairs={{0,2},{1,3},{2,0},{3,1},{4,6},{5,7},{6,4},{7,5},{8,10},{9,11},{10,... | collective-permute-start | bytes 602120 | tf_op jit(solution)/shard_map/ppermute | solution.py:234
  29.2 4.0 %collective-permute-start.10 = (f32[72,128]{1,0:T(8,128)S(1)}, f32[72,128]{1,0:T(8,128)S(1)}, u32[]{:S(2)}, u32[]{:S(2)}) collective-permute-start(f32[72,128]{1,0:T(8,128)S(1)} %shard_map.76), channel_id=1, source_target_pairs={{0,2},{1,3},{2,0},{3,1},{4,6},{5,7},{6,4},{7,5},{8,10},{9,11},{10,... | collective-permute-start | bytes 110600 | tf_op jit(solution)/shard_map/ppermute | solution.py:234
  33.2 4.4 %collective-permute-start.11 = (f32[72,128]{1,0:T(8,128)S(1)}, f32[72,128]{1,0:T(8,128)S(1)}, u32[]{:S(2)}, u32[]{:S(2)}) collective-permute-start(f32[72,128]{1,0:T(8,128)S(1)} %add.6), channel_id=1, source_target_pairs={{0,4},{1,5},{2,6},{3,7},{4,0},{5,1},{6,2},{7,3},{8,12},{9,13},{10,... | collective-permute-start | bytes 110600 | tf_op jit(solution)/shard_map/ppermute | solution.py:234
  37.6 4.9 %collective-permute-start.12 = (f32[72,128]{1,0:T(8,128)S(1)}, f32[72,128]{1,0:T(8,128)S(1)}, u32[]{:S(2)}, u32[]{:S(2)}) collective-permute-start(f32[72,128]{1,0:T(8,128)S(1)} %add.7.q_ref), channel_id=1, source_target_pairs={{0,8},{1,9},{2,10},{3,11},{4,12},{5,13},{6,14},{7,15},{8,0},{9,1},... | collective-permute-start | bytes 110600 | tf_op jit(solution)/shard_map/ppermute | solution.py:234
  42.6 1.3 %collective-permute-start.14 = (f32[80,128]{1,0:T(8,128)S(1)}, f32[80,128]{1,0:T(8,128)S(1)}, u32[]{:S(2)}, u32[]{:S(2)}) collective-permute-start(f32[80,128]{1,0:T(8,128)S(1)} %shard_map.78.q_ref), channel_id=1, source_target_pairs={{0,1},{1,0},{2,3},{3,2},{4,5},{5,4},{6,7},{7,6},{8,9},{9,8},{10,11... | collective-permute-start | bytes 122888 | tf_op jit(solution)/shard_map/ppermute | solution.py:234

commit v7 on v6

--- a/solution.py
+++ b/solution.py
@@ -75,8 +75,11 @@
             out[part, :] = unit_rows(raw[part, :])
 
 
-def copy_after(value_ref, *rest):
-    rest[-1][...] = value_ref[...]
+def copy_after(value_ref, _, *out_refs):
+    start = 0
+    for ref in out_refs:
+        ref[...] = value_ref[start : start + ref.shape[0], :]
+        start += ref.shape[0]
 
 
 def quartic(products, width):
@@ -252,6 +255,27 @@
         compiler_params=pltpu.CompilerParams(vmem_limit_bytes=58 * 2**20),
     )(cand_desc, struct_id.reshape(1, rows), lanczos, mean_weight)
 
+    def again(value, other, pieces):
+        shapes = [
+            jax.ShapeDtypeStruct((piece, value.shape[1]), value.dtype) for piece in pieces
+        ]
+        return pl.pallas_call(
+            copy_after,
+            out_shape=shapes,
+            in_specs=[VMEM, pl.BlockSpec(memory_space=pl.ANY)],
+            out_specs=[VMEM] * len(shapes),
+            compiler_params=pltpu.CompilerParams(vmem_limit_bytes=24 * 2**20),
+        )(value, other)
+
+    def again_last(value, *others):
+        return pl.pallas_call(
+            lambda *refs: copy_after(refs[-2], None, refs[-1]),
+            out_shape=block_shape,
+            in_specs=[pl.BlockSpec(memory_space=pl.ANY)] * len(others) + [VMEM],
+            out_specs=VMEM,
+            compiler_params=pltpu.CompilerParams(vmem_limit_bytes=24 * 2**20),
+        )(*others, value)
+
     def pack_received(mask, *others):
         return pl.pallas_call(
             pack_here,
@@ -261,9 +285,24 @@
             compiler_params=pltpu.CompilerParams(vmem_limit_bytes=24 * 2**20),
         )(swap(cand_desc, mask), swap(struct_id.reshape(1, rows), mask), *others)
 
-    def again(value, *others):
+    def again_pieces(value, pieces, *others):
+        shapes = [
+            jax.ShapeDtypeStruct((piece, value.shape[1]), value.dtype) for piece in pieces
+        ]
+        def kernel(*refs):
+            refs[1 + len(others)][...] = refs[0][...]
+            copy_after(refs[0], None, *refs[2 + len(others) :])
         return pl.pallas_call(
-            copy_after,
+            kernel,
+            out_shape=[block_shape, *shapes],
+            in_specs=[VMEM] + [pl.BlockSpec(memory_space=pl.ANY)] * len(others),
+            out_specs=[VMEM] * (1 + len(shapes)),
+            compiler_params=pltpu.CompilerParams(vmem_limit_bytes=24 * 2**20),
+        )(value, *others)
+
+    def again_first(value, *others):
+        return pl.pallas_call(
+            lambda *refs: copy_after(refs[0], None, refs[-1]),
             out_shape=block_shape,
             in_specs=[VMEM] + [pl.BlockSpec(memory_space=pl.ANY)] * len(others),
             out_specs=VMEM,
@@ -314,16 +353,18 @@
         far = pack_received(8, train_own)
         blocks[4] = far
         blocks[6] = swap(far, 4)
-        blocks[5] = swap(again(far, blocks[2]), 2)
-        blocks[3] = swap(again(blocks[1], far), 4)
-        blocks[7] = swap(blocks[6], 2)
-        groups = ((0, 1), (2, 4), (5, 6), (3, 7))
+        blocks[5] = swap(again_first(far, blocks[2]), 2)
+        groups = ((0, 1), (2, 5), (4, 6), (3, 7))
     else:
         groups = [(m, m + 1) for m in range(0, chips, 2)]
     blocks = {m: b if isinstance(b, (tuple, list)) else (b,) for m, b in blocks.items()}
     q = None
     for one, two in groups:
         q = add_projection((one, two), q, blocks[one], blocks[two])
+        if size == 16 and (one, two) == groups[0]:
+            blocks[3] = (swap(again_first(blocks[1][0], q), 4),)
+        if size == 16 and (one, two) == groups[0]:
+            blocks[7] = (swap(again_first(blocks[6][0], q), 2),)
     sib = swap(own, 1)
     prior = add_prior(tuple(range(chips)), None, *[blocks[m] for m in range(chips)])
 

time: 44.8 us -> 44.7 us (level)
  transfers between devices with their start and end apart: 15 -> 15, of which waited for: 7 -> 8; matrix products, arithmetic and copies ran while one was open for 0% -> 0% of each run, Pallas kernels for 23% -> 23%
where the time goes in v7:
time: 44.7 us; the launch traced here: 44.6 us
  starting transfers between devices  20.3 us (45%)
  Pallas kernels  11.1 us (25%)
  waiting for transfers between devices  11.1 us (25%)
  local copies, waits for them, and re-layouts  1.28 us (3%)
  between operations  0.76 us (2%)
    ppermute x15, starting transfers between devices, swap(): return lax.ppermute(value, 'train', [(i, i ^ mask) for i in range(size)])  20.3 us
    ppermute x15, waiting for transfers between devices, swap(): return lax.ppermute(value, 'train', [(i, i ^ mask) for i in range(size)])  11.1 us
    pallas_call x4, Pallas kernels, add_projection(): call(kernel, q_shape, 4 + len(pair) + len(state), flops=2 * 2 * rows * 2...  5.37 us
    pallas_call x1, Pallas kernels, body(): pl.pallas_call(pack_own, out_shape=[block_shape, jax.ShapeDtypeStruct((ra...  2.04 us
    pallas_call x1, Pallas kernels, add_prior(): call(kernel, prior_shape, 2 + len(refs) + len(state), flops=2 * 2 * rows...  1.84 us
    unnamed x6, local copies, waits for them, and re-layouts  1.28 us
  transfers between devices with their start and end apart: 15, of which 8 were waited for; matrix products, arithmetic and copies ran while one was open for 0% of the time, Pallas kernels for 23%

profile of v7, /device:TPU:0, one launch (start us, length us, event | category | flops | bytes accessed | tf_op | source)
XLA Modules:
  0.0 44.6 jit_solution(16352004418904306)
XLA Ops:
  1.1 3.7 %collective-permute-start.4 = (bf16[128,768]{1,0:T(8,128)(2,1)}, bf16[128,768]{1,0:T(8,128)(2,1)S(1)}, u32[]{:S(2)}, u32[]{:S(2)}) collective-permute-start(bf16[128,768]{1,0:T(8,128)(2,1)} %cand_ref.1), channel_id=1, source_target_pairs={{0,8},{1,9},{2,10},{3,11},{4,12},{5,13},{6,14},{7,15},{8,0},{9,1},... | collective-permute-start | bytes 589832 | tf_op jit(solution)/shard_map/ppermute | solution.py:237
  4.8 2.0 %shard_map.68 = (bf16[784,128]{1,0:T(8,128)(2,1)}, bf16[144,768]{1,0:T(8,128)(2,1)}) custom-call(bf16[128,768]{1,0:T(8,128)(2,1)} %cand_ref.1, s32[1,128]{1,0:T(1,128)} %bitcast.2, bf16[768,128]{1,0:T(8,128)(2,1)} %lanczos_ref.1, bf16[768]{0:T(1024)(128)(2,1)} %weight_ref.1), custom_call_target="tpu_custom_call" | custom-call | tf_op jit(solution)/shard_map/pallas_call | solution.py:240
  6.9 1.6 %collective-permute-start.8 = (bf16[784,128]{1,0:T(8,128)(2,1)}, bf16[784,128]{1,0:T(8,128)(2,1)S(1)}, u32[]{:S(2)}, u32[]{:S(2)}) collective-permute-start(bf16[784,128]{1,0:T(8,128)(2,1)} %get-tuple-element.8.rest_0_.own_ref), channel_id=1, source_target_pairs={{0,4},{1,5},{2,6},{3,7},{4,0},{5,1},{6,2},{7,3},{8,12},{9,13},{10,... | collective-permute-start | bytes 602120 | tf_op jit(solution)/shard_map/ppermute | solution.py:237
  8.5 1.5 %collective-permute-start = (bf16[784,128]{1,0:T(8,128)(2,1)}, bf16[784,128]{1,0:T(8,128)(2,1)S(1)}, u32[]{:S(2)}, u32[]{:S(2)}) collective-permute-start(bf16[784,128]{1,0:T(8,128)(2,1)} %get-tuple-element.8.rest_0_.own_ref), channel_id=1, source_target_pairs={{0,2},{1,3},{2,0},{3,1},{4,6},{5,7},{6,4},{7,5},{8,10},{9,11},{10,... | collective-permute-start | bytes 602120 | tf_op jit(solution)/shard_map/ppermute | solution.py:237
  10.3 1.3 %copy-done.2 = bf16[768,768]{1,0:T(8,128)(2,1)S(1)} copy-done((bf16[768,768]{1,0:T(8,128)(2,1)S(1)}, bf16[768,768]{1,0:T(8,128)(2,1)}, u32[]{:S(2)}) %copy-start.2) | copy-done | bytes 1179672
  11.6 0.7 %shard_map.69 = (bf16[768,768]{1,0:T(8,128)(2,1)S(1)}, bf16[768,768]{1,0:T(8,128)(2,1)S(1)}) custom-call(bf16[768,768]{1,0:T(8,128)(2,1)S(1)} %copy-done.2, bf16[768,768]{1,0:T(8,128)(2,1)S(1)} %collective-permute-done.1.sib_ref), custom_call_target="tpu_custom_call" | custom-call | tf_op jit(solution)/shard_map/pallas_call | solution.py:348
  12.4 2.5 %collective-permute-done.5.ids_ref = s32[1,128]{1,0:T(1,128)S(1)} collective-permute-done((s32[1,128]{1,0:T(1,128)}, s32[1,128]{1,0:T(1,128)S(1)}, u32[]{:S(2)}, u32[]{:S(2)}) %collective-permute-start.5) | collective-permute-done | bytes 544 | tf_op jit(solution)/shard_map/ppermute | solution.py:237
  15.1 1.7 %collective-permute-start.6 = (bf16[784,128]{1,0:T(8,128)(2,1)S(1)}, bf16[784,128]{1,0:T(8,128)(2,1)S(1)}, u32[]{:S(2)}, u32[]{:S(2)}) collective-permute-start(bf16[784,128]{1,0:T(8,128)(2,1)S(1)} %shard_map.72.refs_0_.rest_0_.rest_4_), channel_id=1, source_target_pairs={{0,4},{1,5},{2,6},{3,7},{4,0},{5,1},{6,2},{7,3},{8,12},{9,13},{10,... | collective-permute-start | bytes 602120 | tf_op jit(solution)/shard_map/ppermute | solution.py:237
  17.3 1.6 %collective-permute-start.9 = (bf16[784,128]{1,0:T(8,128)(2,1)S(1)}, bf16[784,128]{1,0:T(8,128)(2,1)S(1)}, u32[]{:S(2)}, u32[]{:S(2)}) collective-permute-start(bf16[784,128]{1,0:T(8,128)(2,1)S(1)} %shard_map.74), channel_id=1, source_target_pairs={{0,2},{1,3},{2,0},{3,1},{4,6},{5,7},{6,4},{7,5},{8,10},{9,11},{10,... | collective-permute-start | bytes 602120 | tf_op jit(solution)/shard_map/ppermute | solution.py:237
  18.9 1.3 %shard_map.70.refs_1_.rest_6_ = f32[72,128]{1,0:T(8,128)S(1)} custom-call(bf16[784,128]{1,0:T(8,128)(2,1)S(1)} %copy-done.1, bf16[784,128]{1,0:T(8,128)(2,1)S(1)} %collective-permute-done.rest_1_.refs_0_, bf16[768,768]{1,0:T(8,128)(2,1)S(1)} %get-tuple-element.9.rest_2_.rest_0_, bf16[144,768]{1,0:T(8,128)(2,1)S(1)} %copy-done, ...), custom_call_target="tpu_custom_call" | custom-call | flops 805306368 | tf_op jit(solution)/shard_map/pallas_call | solution.py:321
  20.4 1.5 %collective-permute-done.6.refs_0_.rest_1_.rest_6_ = bf16[784,128]{1,0:T(8,128)(2,1)S(1)} collective-permute-done((bf16[784,128]{1,0:T(8,128)(2,1)S(1)}, bf16[784,128]{1,0:T(8,128)(2,1)S(1)}, u32[]{:S(2)}, u32[]{:S(2)}) %collective-permute-start.6) | collective-permute-done | bytes 200736 | tf_op jit(solution)/shard_map/ppermute | solution.py:237
  21.8 2.1 %collective-permute-start.7 = (bf16[784,128]{1,0:T(8,128)(2,1)S(1)}, bf16[784,128]{1,0:T(8,128)(2,1)S(1)}, u32[]{:S(2)}, u32[]{:S(2)}) collective-permute-start(bf16[784,128]{1,0:T(8,128)(2,1)S(1)} %shard_map.73), channel_id=1, source_target_pairs={{0,2},{1,3},{2,0},{3,1},{4,6},{5,7},{6,4},{7,5},{8,10},{9,11},{10,... | collective-permute-start | bytes 602120 | tf_op jit(solution)/shard_map/ppermute | solution.py:237
  23.9 1.3 %shard_map.75.rest_6_ = f32[72,128]{1,0:T(8,128)S(1)} custom-call(bf16[784,128]{1,0:T(8,128)(2,1)S(1)} %collective-permute-done.8.refs_1_.rest_0_.rest_2_, bf16[784,128]{1,0:T(8,128)(2,1)S(1)} %collective-permute-done.9.rest_1_.rest_5_, bf16[768,768]{1,0:T(8,128)(2,1)S(1)} %get-tuple-element.9.rest_2_.rest_0_, bf16[144,768]{1,0:T(8,128)(2,1)S(1)} %copy-done, ...), custom_call_target="tpu_custom_call" | custom-call | flops 805306368 | tf_op jit(solution)/shard_map/pallas_call | solution.py:321
  25.3 1.3 %shard_map.76.rest_6_ = f32[72,128]{1,0:T(8,128)S(1)} custom-call(bf16[784,128]{1,0:T(8,128)(2,1)S(1)} %shard_map.72.refs_0_.rest_0_.rest_4_, bf16[784,128]{1,0:T(8,128)(2,1)S(1)} %collective-permute-done.6.refs_0_.rest_1_.rest_6_, bf16[768,768]{1,0:T(8,128)(2,1)S(1)} %get-tuple-element.9.rest_2_.rest_0_, bf16[144,768]{1,0:T(8,128)(2,1)S(1)} %copy-done, ...), custom_call_target="tpu_custom_call" | custom-call | flops 805306368 | tf_op jit(solution)/shard_map/pallas_call | solution.py:321
  26.6 1.2 %collective-permute-done.7.rest_1_.rest_7_ = bf16[784,128]{1,0:T(8,128)(2,1)S(1)} collective-permute-done((bf16[784,128]{1,0:T(8,128)(2,1)S(1)}, bf16[784,128]{1,0:T(8,128)(2,1)S(1)}, u32[]{:S(2)}, u32[]{:S(2)}) %collective-permute-start.7) | collective-permute-done | bytes 200736 | tf_op jit(solution)/shard_map/ppermute | solution.py:237
  27.9 1.3 %shard_map.77 = f32[72,128]{1,0:T(8,128)S(1)} custom-call(bf16[784,128]{1,0:T(8,128)(2,1)S(1)} %collective-permute-done.3.rest_0_.rest_3_, bf16[784,128]{1,0:T(8,128)(2,1)S(1)} %collective-permute-done.7.rest_1_.rest_7_, bf16[768,768]{1,0:T(8,128)(2,1)S(1)} %get-tuple-element.9.rest_2_.rest_0_, bf16[144,768]{1,0:T(8,128)(2,1)S(1)} %copy-done, ...), custom_call_target="tpu_custom_call" | custom-call | flops 805306368 | tf_op jit(solution)/shard_map/pallas_call | solution.py:321
  29.2 1.8 %collective-permute-start.10 = (f32[72,128]{1,0:T(8,128)S(1)}, f32[72,128]{1,0:T(8,128)S(1)}, u32[]{:S(2)}, u32[]{:S(2)}) collective-permute-start(f32[72,128]{1,0:T(8,128)S(1)} %shard_map.77), channel_id=1, source_target_pairs={{0,2},{1,3},{2,0},{3,1},{4,6},{5,7},{6,4},{7,5},{8,10},{9,11},{10,... | collective-permute-start | bytes 110600 | tf_op jit(solution)/shard_map/ppermute | solution.py:237
  31.0 2.2 %collective-permute-done.10 = f32[72,128]{1,0:T(8,128)S(1)} collective-permute-done((f32[72,128]{1,0:T(8,128)S(1)}, f32[72,128]{1,0:T(8,128)S(1)}, u32[]{:S(2)}, u32[]{:S(2)}) %collective-permute-start.10) | collective-permute-done | bytes 36896 | tf_op jit(solution)/shard_map/ppermute | solution.py:237
  33.2 2.1 %collective-permute-start.11 = (f32[72,128]{1,0:T(8,128)S(1)}, f32[72,128]{1,0:T(8,128)S(1)}, u32[]{:S(2)}, u32[]{:S(2)}) collective-permute-start(f32[72,128]{1,0:T(8,128)S(1)} %add.6), channel_id=1, source_target_pairs={{0,4},{1,5},{2,6},{3,7},{4,0},{5,1},{6,2},{7,3},{8,12},{9,13},{10,... | collective-permute-start | bytes 110600 | tf_op jit(solution)/shard_map/ppermute | solution.py:237
  35.4 1.9 %collective-permute-done.11 = f32[72,128]{1,0:T(8,128)S(1)} collective-permute-done((f32[72,128]{1,0:T(8,128)S(1)}, f32[72,128]{1,0:T(8,128)S(1)}, u32[]{:S(2)}, u32[]{:S(2)}) %collective-permute-start.11) | collective-permute-done | bytes 36896 | tf_op jit(solution)/shard_map/ppermute | solution.py:237
  37.3 3.2 %collective-permute-start.12 = (f32[72,128]{1,0:T(8,128)S(1)}, f32[72,128]{1,0:T(8,128)S(1)}, u32[]{:S(2)}, u32[]{:S(2)}) collective-permute-start(f32[72,128]{1,0:T(8,128)S(1)} %add.7.q_ref), channel_id=1, source_target_pairs={{0,8},{1,9},{2,10},{3,11},{4,12},{5,13},{6,14},{7,15},{8,0},{9,1},... | collective-permute-start | bytes 110600 | tf_op jit(solution)/shard_map/ppermute | solution.py:237
  40.5 1.8 %shard_map.78.prior_ref = f32[16,128]{1,0:T(8,128)S(1)} custom-call(bf16[784,128]{1,0:T(8,128)(2,1)S(1)} %copy-done.1, bf16[784,128]{1,0:T(8,128)(2,1)S(1)} %collective-permute-done.13.sib_ref, bf16[784,128]{1,0:T(8,128)(2,1)S(1)} %copy-done.1, bf16[784,128]{1,0:T(8,128)(2,1)S(1)} %collective-permute-done.rest_1_.refs_0_, ...), custom_call_target="tpu_custom_call" | custom-call | flops 536870912 | tf_op jit(solution)/shard_map/pallas_call | solution.py:333
  42.5 1.2 %collective-permute-done.14.other_ref = f32[80,128]{1,0:T(8,128)S(1)} collective-permute-done((f32[80,128]{1,0:T(8,128)S(1)}, f32[80,128]{1,0:T(8,128)S(1)}, u32[]{:S(2)}, u32[]{:S(2)}) %collective-permute-start.14) | collective-permute-done | bytes 40992 | tf_op jit(solution)/shard_map/ppermute | solution.py:237
  43.7 0.8 %shard_map.80 = (f32[8]{0:T(128)}, f32[8,128]{1,0:T(8,128)}) custom-call(f32[80,128]{1,0:T(8,128)S(1)} %shard_map.79.q_ref, f32[80,128]{1,0:T(8,128)S(1)} %collective-permute-done.14.other_ref, f32[16,128]{1,0:T(8,128)S(1)} %shard_map.78.prior_ref), custom_call_target="tpu_custom_call" | custom-call | tf_op jit(solution)/shard_map/pallas_call | solution.py:379
  (27 shorter events, 1.8 us)
Async XLA Ops:
  0.6 9.4 %collective-permute-start.1 = (bf16[768,768]{1,0:T(8,128)(2,1)}, bf16[768,768]{1,0:T(8,128)(2,1)S(1)}, u32[]{:S(2)}, u32[]{:S(2)}) collective-permute-start(bf16[768,768]{1,0:T(8,128)(2,1)} %own_ref.1), channel_id=1, source_target_pairs={{0,1},{1,0},{2,3},{3,2},{4,5},{5,4},{6,7},{7,6},{8,9},{9,8},{10,11... | collective-permute-start | bytes 3538952 | tf_op jit(solution)/shard_map/ppermute | solution.py:237
  1.1 13.8 %collective-permute-start.4 = (bf16[128,768]{1,0:T(8,128)(2,1)}, bf16[128,768]{1,0:T(8,128)(2,1)S(1)}, u32[]{:S(2)}, u32[]{:S(2)}) collective-permute-start(bf16[128,768]{1,0:T(8,128)(2,1)} %cand_ref.1), channel_id=1, source_target_pairs={{0,8},{1,9},{2,10},{3,11},{4,12},{5,13},{6,14},{7,15},{8,0},{9,1},... | collective-permute-start | bytes 589832 | tf_op jit(solution)/shard_map/ppermute | solution.py:237
  6.9 10.4 %collective-permute-start.8 = (bf16[784,128]{1,0:T(8,128)(2,1)}, bf16[784,128]{1,0:T(8,128)(2,1)S(1)}, u32[]{:S(2)}, u32[]{:S(2)}) collective-permute-start(bf16[784,128]{1,0:T(8,128)(2,1)} %get-tuple-element.8.rest_0_.own_ref), channel_id=1, source_target_pairs={{0,4},{1,5},{2,6},{3,7},{4,0},{5,1},{6,2},{7,3},{8,12},{9,13},{10,... | collective-permute-start | bytes 602120 | tf_op jit(solution)/shard_map/ppermute | solution.py:237
  8.5 10.4 %collective-permute-start.2 = (bf16[144,768]{1,0:T(8,128)(2,1)}, bf16[144,768]{1,0:T(8,128)(2,1)S(1)}, u32[]{:S(2)}, u32[]{:S(2)}) collective-permute-start(bf16[144,768]{1,0:T(8,128)(2,1)} %get-tuple-element.10.rest_3_), channel_id=1, source_target_pairs={{0,1},{1,0},{2,3},{3,2},{4,5},{5,4},{6,7},{7,6},{8,9},{9,8},{10,11... | collective-permute-start | bytes 663560 | tf_op jit(solution)/shard_map/ppermute | solution.py:237
  8.5 10.4 %collective-permute-start = (bf16[784,128]{1,0:T(8,128)(2,1)}, bf16[784,128]{1,0:T(8,128)(2,1)S(1)}, u32[]{:S(2)}, u32[]{:S(2)}) collective-permute-start(bf16[784,128]{1,0:T(8,128)(2,1)} %get-tuple-element.8.rest_0_.own_ref), channel_id=1, source_target_pairs={{0,2},{1,3},{2,0},{3,1},{4,6},{5,7},{6,4},{7,5},{8,10},{9,11},{10,... | collective-permute-start | bytes 602120 | tf_op jit(solution)/shard_map/ppermute | solution.py:237
  10.0 4.9 %collective-permute-start.5 = (s32[1,128]{1,0:T(1,128)}, s32[1,128]{1,0:T(1,128)S(1)}, u32[]{:S(2)}, u32[]{:S(2)}) collective-permute-start(s32[1,128]{1,0:T(1,128)} %bitcast.3), channel_id=1, source_target_pairs={{0,8},{1,9},{2,10},{3,11},{4,12},{5,13},{6,14},{7,15},{8,0},{9,1},... | collective-permute-start | bytes 1544 | tf_op jit(solution)/shard_map/ppermute | solution.py:237
  10.3 1.3 %copy-start.2 = (bf16[768,768]{1,0:T(8,128)(2,1)S(1)}, bf16[768,768]{1,0:T(8,128)(2,1)}, u32[]{:S(2)}) copy-start(bf16[768,768]{1,0:T(8,128)(2,1)} %own_ref.1) | copy-start | bytes 3538948
  12.4 6.5 %copy-start = (bf16[144,768]{1,0:T(8,128)(2,1)S(1)}, bf16[144,768]{1,0:T(8,128)(2,1)}, u32[]{:S(2)}) copy-start(bf16[144,768]{1,0:T(8,128)(2,1)} %get-tuple-element.10.rest_3_) | copy-start | bytes 663556
  12.4 6.5 %copy-start.1 = (bf16[784,128]{1,0:T(8,128)(2,1)S(1)}, bf16[784,128]{1,0:T(8,128)(2,1)}, u32[]{:S(2)}) copy-start(bf16[784,128]{1,0:T(8,128)(2,1)} %get-tuple-element.8.rest_0_.own_ref) | copy-start | bytes 602116
  15.1 6.7 %collective-permute-start.6 = (bf16[784,128]{1,0:T(8,128)(2,1)S(1)}, bf16[784,128]{1,0:T(8,128)(2,1)S(1)}, u32[]{:S(2)}, u32[]{:S(2)}) collective-permute-start(bf16[784,128]{1,0:T(8,128)(2,1)S(1)} %shard_map.72.refs_0_.rest_0_.rest_4_), channel_id=1, source_target_pairs={{0,4},{1,5},{2,6},{3,7},{4,0},{5,1},{6,2},{7,3},{8,12},{9,13},{10,... | collective-permute-start | bytes 602120 | tf_op jit(solution)/shard_map/ppermute | solution.py:237
  17.3 6.7 %collective-permute-start.9 = (bf16[784,128]{1,0:T(8,128)(2,1)S(1)}, bf16[784,128]{1,0:T(8,128)(2,1)S(1)}, u32[]{:S(2)}, u32[]{:S(2)}) collective-permute-start(bf16[784,128]{1,0:T(8,128)(2,1)S(1)} %shard_map.74), channel_id=1, source_target_pairs={{0,2},{1,3},{2,0},{3,1},{4,6},{5,7},{6,4},{7,5},{8,10},{9,11},{10,... | collective-permute-start | bytes 602120 | tf_op jit(solution)/shard_map/ppermute | solution.py:237
  20.3 6.4 %collective-permute-start.3 = (bf16[784,128]{1,0:T(8,128)(2,1)S(1)}, bf16[784,128]{1,0:T(8,128)(2,1)S(1)}, u32[]{:S(2)}, u32[]{:S(2)}) collective-permute-start(bf16[784,128]{1,0:T(8,128)(2,1)S(1)} %shard_map.71), channel_id=1, source_target_pairs={{0,4},{1,5},{2,6},{3,7},{4,0},{5,1},{6,2},{7,3},{8,12},{9,13},{10,... | collective-permute-start | bytes 602120 | tf_op jit(solution)/shard_map/ppermute | solution.py:237
  21.8 6.0 %collective-permute-start.7 = (bf16[784,128]{1,0:T(8,128)(2,1)S(1)}, bf16[784,128]{1,0:T(8,128)(2,1)S(1)}, u32[]{:S(2)}, u32[]{:S(2)}) collective-permute-start(bf16[784,128]{1,0:T(8,128)(2,1)S(1)} %shard_map.73), channel_id=1, source_target_pairs={{0,2},{1,3},{2,0},{3,1},{4,6},{5,7},{6,4},{7,5},{8,10},{9,11},{10,... | collective-permute-start | bytes 602120 | tf_op jit(solution)/shard_map/ppermute | solution.py:237
  23.9 16.6 %collective-permute-start.13 = (bf16[784,128]{1,0:T(8,128)(2,1)S(1)}, bf16[784,128]{1,0:T(8,128)(2,1)S(1)}, u32[]{:S(2)}, u32[]{:S(2)}) collective-permute-start(bf16[784,128]{1,0:T(8,128)(2,1)S(1)} %copy-done.1), channel_id=1, source_target_pairs={{0,1},{1,0},{2,3},{3,2},{4,5},{5,4},{6,7},{7,6},{8,9},{9,8},{10,11... | collective-permute-start | bytes 602120 | tf_op jit(solution)/shard_map/ppermute | solution.py:237
  29.2 4.0 %collective-permute-start.10 = (f32[72,128]{1,0:T(8,128)S(1)}, f32[72,128]{1,0:T(8,128)S(1)}, u32[]{:S(2)}, u32[]{:S(2)}) collective-permute-start(f32[72,128]{1,0:T(8,128)S(1)} %shard_map.77), channel_id=1, source_target_pairs={{0,2},{1,3},{2,0},{3,1},{4,6},{5,7},{6,4},{7,5},{8,10},{9,11},{10,... | collective-permute-start | bytes 110600 | tf_op jit(solution)/shard_map/ppermute | solution.py:237
  33.2 4.1 %collective-permute-start.11 = (f32[72,128]{1,0:T(8,128)S(1)}, f32[72,128]{1,0:T(8,128)S(1)}, u32[]{:S(2)}, u32[]{:S(2)}) collective-permute-start(f32[72,128]{1,0:T(8,128)S(1)} %add.6), channel_id=1, source_target_pairs={{0,4},{1,5},{2,6},{3,7},{4,0},{5,1},{6,2},{7,3},{8,12},{9,13},{10,... | collective-permute-start | bytes 110600 | tf_op jit(solution)/shard_map/ppermute | solution.py:237
  37.3 5.2 %collective-permute-start.12 = (f32[72,128]{1,0:T(8,128)S(1)}, f32[72,128]{1,0:T(8,128)S(1)}, u32[]{:S(2)}, u32[]{:S(2)}) collective-permute-start(f32[72,128]{1,0:T(8,128)S(1)} %add.7.q_ref), channel_id=1, source_target_pairs={{0,8},{1,9},{2,10},{3,11},{4,12},{5,13},{6,14},{7,15},{8,0},{9,1},... | collective-permute-start | bytes 110600 | tf_op jit(solution)/shard_map/ppermute | solution.py:237
  42.5 1.3 %collective-permute-start.14 = (f32[80,128]{1,0:T(8,128)S(1)}, f32[80,128]{1,0:T(8,128)S(1)}, u32[]{:S(2)}, u32[]{:S(2)}) collective-permute-start(f32[80,128]{1,0:T(8,128)S(1)} %shard_map.79.q_ref), channel_id=1, source_target_pairs={{0,1},{1,0},{2,3},{3,2},{4,5},{5,4},{6,7},{7,6},{8,9},{9,8},{10,11... | collective-permute-start | bytes 122888 | tf_op jit(solution)/shard_map/ppermute | solution.py:237
